TPU v7x, 32 devices: a whole 2x2x4 slice. The times are simulated.
32 devices in a mesh: groups: 2 (over x), shard: 8 (over z, y), sub: 2 (over core).
Axes of the slice: x: 2, y: 2, z: 4, core: 2. Of those that a mesh axis runs over, the one named last changes fastest.
Arguments:
- queries: bfloat16 [256, 32, 128], P(('groups', 'shard'), 'sub'), parts along dimension 0, may hold values from -6 to 6
- candidates: int32 [256, 16], P(('groups', 'shard')), parts along dimension 0, may hold values from 0 to 1023, as said below
- residuals: int32 [1024, 128, 16], P(('shard', 'sub')), may hold values from 0 to 65535, as said below
- centroid_ids: int32 [1024, 128], P(('shard', 'sub')), may hold values from 0 to 4095
- block_scales: bfloat16 [1024, 128], P(('shard', 'sub')), may hold values from 0.25 to 1
- lengths: int32 [1024], P(('shard', 'sub')), may hold values from 17 to 128
- centroids: bfloat16 [4096, 128], replicated, may hold values from -0.5 to 0.5
- bucket_weights: bfloat16 [4], replicated, may hold values from -0.25 to 0.25
Outputs:
- scores: float32 [256, 16], P(('groups', 'shard')), parts along dimension 0
There are 2 independent parts, one for each index of `groups`. A program takes and returns all parts, laid end to end along the dimension named above; an argument that names none is the same for every part. Nothing has to cross between parts.
Inputs may be any that keep to these rules, and one draw needn't show every extreme that they name: `candidates`: each id names a passage; passage p lies on device p // 64 of shard+sub. Among the 256 pairs of one block of 16 queries (one index of shard), at most 32 name passages of any one device; in every draw one device receives exactly 32 pairs from every block. `residuals`: each word packs 8 independent 2-bit codes, code e % 8 in bits 2 * (e % 8) and 2 * (e % 8) + 1; higher bits are zero.
All inputs are finite; a program needn't handle non-finite values.
Results may differ from a plain program's by a relative error of at most 0.0003.
Values may be sent and summed in bfloat16 or wider, within the bound.
No kernel may reach another device: no remote copies, remote signals or barrier semaphores. Data moves between devices by JAX's collectives and lax.ppermute only.
A program may use at most 64 MiB of HBM per device.

v0:
```python
import math

import jax
import jax.numpy as jnp
from jax import lax
from jax.sharding import PartitionSpec as P

masked_floor = -1000000000.0


def decode_tokens(packed, ids_here, scales_here, centroids, buckets):
    shifts = 2 * jnp.arange(8, dtype=jnp.int32)
    codes = jnp.bitwise_and(jnp.right_shift(packed[..., None], shifts), 3)
    codes = codes.reshape(packed.shape[:-1] + (packed.shape[-1] * 8,))
    levels = jnp.arange(4, dtype=jnp.int32)
    values = jnp.sum(
        jnp.where(codes[..., None] == levels, buckets.astype(jnp.float32), jnp.float32(0.0)),
        axis=-1,
    )
    centre = jnp.take(centroids, ids_here, axis=0).astype(jnp.float32)
    summed = centre + scales_here.astype(jnp.float32)[..., None] * values
    inverse = lax.rsqrt(jnp.sum(summed * summed, axis=-1, keepdims=True) + 1e-06)
    return (summed * inverse).astype(jnp.bfloat16)


def score_slots(stored, ids_here, scales_here, counts_here, query_rows, centroids, buckets):
    slot_count = stored.shape[0]
    token_slots = stored.shape[1]
    group_size = math.gcd(slot_count, max(1, 4096 // token_slots))

    def score_group(operands):
        stored_g, ids_g, scales_g, counts_g, query_g = operands
        embedded = decode_tokens(stored_g, ids_g, scales_g, centroids, buckets)
        similar = jnp.einsum("gpd,gtd->gtp", embedded, query_g, preferred_element_type=jnp.float32)
        positions = lax.broadcasted_iota(jnp.int32, similar.shape, 2)
        living = positions < counts_g[:, None, None]
        best_match = jnp.max(jnp.where(living, similar, masked_floor), axis=2)
        return jnp.sum(best_match, axis=1)

    def blocked(tensor):
        return tensor.reshape((slot_count // group_size, group_size) + tensor.shape[1:])

    partial_value = lax.map(
        score_group,
        (
            blocked(stored),
            blocked(ids_here),
            blocked(scales_here),
            blocked(counts_here),
            blocked(query_rows),
        ),
    )
    return partial_value.reshape(slot_count)


def body(
    queries, candidates, residuals, centroid_ids, block_scales, lengths, centroids, bucket_weights
):
    shards = lax.axis_size("shard")
    halves = lax.axis_size("sub")
    my_half = lax.axis_index("sub")
    query_count, per_query = candidates.shape
    passages, token_slots, word_count = residuals.shape
    feature_width = queries.shape[2]
    pair_count = query_count * per_query
    capacity = max(2, 2 * pair_count // (shards * halves))
    slot_total = shards * capacity
    full_tokens = queries.shape[1] * halves
    pair_ids = candidates.reshape(pair_count)
    owner_dev = pair_ids // passages
    local_index = pair_ids % passages
    devices = lax.broadcasted_iota(jnp.int32, (pair_count, shards * halves), 1)
    onehot = (owner_dev[:, None] == devices).astype(jnp.int32)
    before = jnp.sum((jnp.cumsum(onehot, axis=0) - onehot) * onehot, axis=1)
    owner_shard = owner_dev // halves
    owner_half = owner_dev % halves
    is_mine = owner_half == my_half
    own_slot = jnp.where(is_mine, owner_shard * capacity + before, slot_total)
    pair_index = jnp.arange(pair_count, dtype=jnp.int32)
    wanted = (
        jnp.zeros((slot_total,), jnp.int32)
        .at[own_slot]
        .set(local_index, mode="drop")
        .reshape(shards, capacity)
    )
    pair_of_slot = (
        jnp.full((slot_total,), pair_count, jnp.int32).at[own_slot].set(pair_index, mode="drop")
    )
    query_of_slot = jnp.minimum(pair_of_slot, pair_count - 1) // per_query
    empty_total = jnp.zeros((pair_count,), jnp.float32)
    whole = lax.all_gather(queries, "sub", axis=1, tiled=True)
    outgoing_rows = jnp.take(whole, query_of_slot, axis=0).reshape(
        shards, capacity, full_tokens, feature_width
    )
    asked, query_in = (
        lax.all_to_all(wanted, "shard", split_axis=0, concat_axis=0, tiled=True),
        lax.all_to_all(outgoing_rows, "shard", split_axis=0, concat_axis=0, tiled=True),
    )
    asked = asked.reshape(slot_total)
    partial_value = score_slots(
        jnp.take(residuals, asked, axis=0),
        jnp.take(centroid_ids, asked, axis=0),
        jnp.take(block_scales, asked, axis=0),
        jnp.take(lengths, asked, axis=0),
        query_in.reshape(slot_total, full_tokens, feature_width),
        centroids,
        bucket_weights,
    )
    returned = lax.all_to_all(
        partial_value.reshape(shards, capacity), "shard", split_axis=0, concat_axis=0, tiled=True
    ).reshape(slot_total)
    pair_total = empty_total.at[pair_of_slot].set(returned, mode="drop")
    summed_all = lax.psum(pair_total, "sub")
    return (summed_all / full_tokens).reshape(query_count, per_query)


def solution(mesh):
    return jax.shard_map(
        body,
        mesh=mesh,
        in_specs=(
            P(("groups", "shard"), "sub", None),
            P(("groups", "shard"), None),
            P(("shard", "sub"), None, None),
            P(("shard", "sub"), None),
            P(("shard", "sub"), None),
            P(("shard", "sub")),
            P(),
            P(),
        ),
        out_specs=P(("groups", "shard"), None),
        check_vma=False,
    )
```

profile of v0, /device:TPU:0, one launch (start us, length us, event | category | flops | bytes accessed | tf_op | source)
XLA Modules:
  0.0 332.8 jit_solution(7493319141832677866)
XLA Ops:
  5.5 7.3 %all-to-all-start = ((s32[8,1,32]{2,1,0:T(1,128)}), s32[8,1,32]{2,1,0:T(1,128)S(1)}, u32[]{:S(2)}, u32[]{:S(2)}) async-start(s32[8,1,32]{2,1,0:T(1,128)} %all_to_all.15), calls=%async_computation | async-start | bytes 8192 | tf_op jit(solution)/shard_map/all_to_all | solution.py:96
  19.1 6.1 %all-to-all-start.1 = ((bf16[8,32,32,128]{3,2,1,0:T(8,128)(2,1)}), bf16[8,32,32,128]{3,2,1,0:T(8,128)(2,1)}, u32[]{:S(2)}, u32[]{:S(2)}) async-start(bf16[8,32,32,128]{3,2,1,0:T(8,128)(2,1)} %broadcast_select_fusion.2), calls=%async_computation.1 | async-start | bytes 4194304 | tf_op jit(solution)/shard_map/all_to_all | solution.py:97
  32.7 3.3 broadcast_select_fusion.3
  36.0 37.9 %all-to-all-done.1 = bf16[8,32,32,128]{3,2,1,0:T(8,128)(2,1)} async-done(((bf16[8,32,32,128]{3,2,1,0:T(8,128)(2,1)}), bf16[8,32,32,128]{3,2,1,0:T(8,128)(2,1)}, u32[]{:S(2)}, u32[]{:S(2)}) %all-to-all-start.1) | async-done | bytes 2097184 | tf_op jit(solution)/shard_map/all_to_all | solution.py:97
  73.9 243.0 %while.10 = (s32[]{:T(128)}, f32[8,32]{1,0:T(8,128)}, s32[8,32]{1,0:T(8,128)S(1)}, bf16[8,32,32,128]{3,2,1,0:T(8,128)(2,1)}, s32[8,32,128]{2,1,0:T(8,128)S(1)}, ...) while((s32[]{:T(128)}, f32[8,32]{1,0:T(8,128)}, ...), condition=%wide.region_10.11_spmd, body=%wide.region_5.10_spmd.sunk | while | flops 47099884 | bytes 28523552 | solution.py:43
  76.7 2.9 copy.18
  79.6 4.1 %select_reduce_fusion.2 = f32[32,128,128]{2,1,0:T(8,128)} fusion(f32[4]{0:T(128)S(1)} %convert_element_type.46, s32[32,128,128]{2,1,0:T(8,128)} %copy.18), kind=kLoop, calls=%fused_computation.9.clone.1 | loop fusion | flops 5767168 | bytes 4194320 | tf_op jit(solution)/shard_map/while/body/eval_jaxpr/reduce_sum | solution.py:16
  83.7 12.1 %gather_fusion = bf16[4096,128]{1,0:T(8,128)(2,1)S(1)} fusion(bf16[4096,128]{1,0:T(8,128)(2,1)S(1)} %get-tuple-element.161, s32[4096]{0:T(1024)S(1)} %fusion.29), kind=kCustom, calls=%fused_computation.clone.1 | custom fusion | bytes 2113536 | tf_op jit(solution)/shard_map/while/body/eval_jaxpr/jit(_take)/gather | solution.py:20
  95.9 3.8 %multiply_reduce_fusion.2 = f32[32,128]{1,0:T(8,128)S(1)} fusion(f32[32,128,128]{2,1,0:T(8,128)} %select_reduce_fusion.2, f32[32,128]{1,0:T(8,128)S(1)} %bitcast_convert_fusion.2, bf16[32,128,128]{2,1,0:T(8,128)(2,1)S(1)} %bitcast.75, pred[32,128]{1,0:T(8,128)(4,1)S(1)} %compare_and_fusion.5), kind=kLoop, calls=%fused_computation.14.clone.1 | loop fusion | flops 3141632 | bytes 3182592 | tf_op jit(solution)/shard_map/while/body/eval_jaxpr/reduce_sum | solution.py:22
  99.8 3.1 fusion.31
  107.1 2.9 copy.18
  110.0 4.1 %select_reduce_fusion.2 = f32[32,128,128]{2,1,0:T(8,128)} fusion(f32[4]{0:T(128)S(1)} %convert_element_type.46, s32[32,128,128]{2,1,0:T(8,128)} %copy.18), kind=kLoop, calls=%fused_computation.9.clone.1 | loop fusion | flops 5767168 | bytes 4194320 | tf_op jit(solution)/shard_map/while/body/eval_jaxpr/reduce_sum | solution.py:16
  114.1 12.1 %gather_fusion = bf16[4096,128]{1,0:T(8,128)(2,1)S(1)} fusion(bf16[4096,128]{1,0:T(8,128)(2,1)S(1)} %get-tuple-element.161, s32[4096]{0:T(1024)S(1)} %fusion.29), kind=kCustom, calls=%fused_computation.clone.1 | custom fusion | bytes 2113536 | tf_op jit(solution)/shard_map/while/body/eval_jaxpr/jit(_take)/gather | solution.py:20
  126.3 3.8 %multiply_reduce_fusion.2 = f32[32,128]{1,0:T(8,128)S(1)} fusion(f32[32,128,128]{2,1,0:T(8,128)} %select_reduce_fusion.2, f32[32,128]{1,0:T(8,128)S(1)} %bitcast_convert_fusion.2, bf16[32,128,128]{2,1,0:T(8,128)(2,1)S(1)} %bitcast.75, pred[32,128]{1,0:T(8,128)(4,1)S(1)} %compare_and_fusion.5), kind=kLoop, calls=%fused_computation.14.clone.1 | loop fusion | flops 3141632 | bytes 3182592 | tf_op jit(solution)/shard_map/while/body/eval_jaxpr/reduce_sum | solution.py:22
  130.1 3.1 fusion.31
  137.4 2.9 copy.18
  140.4 4.1 %select_reduce_fusion.2 = f32[32,128,128]{2,1,0:T(8,128)} fusion(f32[4]{0:T(128)S(1)} %convert_element_type.46, s32[32,128,128]{2,1,0:T(8,128)} %copy.18), kind=kLoop, calls=%fused_computation.9.clone.1 | loop fusion | flops 5767168 | bytes 4194320 | tf_op jit(solution)/shard_map/while/body/eval_jaxpr/reduce_sum | solution.py:16
  144.5 12.1 %gather_fusion = bf16[4096,128]{1,0:T(8,128)(2,1)S(1)} fusion(bf16[4096,128]{1,0:T(8,128)(2,1)S(1)} %get-tuple-element.161, s32[4096]{0:T(1024)S(1)} %fusion.29), kind=kCustom, calls=%fused_computation.clone.1 | custom fusion | bytes 2113536 | tf_op jit(solution)/shard_map/while/body/eval_jaxpr/jit(_take)/gather | solution.py:20
  156.7 3.8 %multiply_reduce_fusion.2 = f32[32,128]{1,0:T(8,128)S(1)} fusion(f32[32,128,128]{2,1,0:T(8,128)} %select_reduce_fusion.2, f32[32,128]{1,0:T(8,128)S(1)} %bitcast_convert_fusion.2, bf16[32,128,128]{2,1,0:T(8,128)(2,1)S(1)} %bitcast.75, pred[32,128]{1,0:T(8,128)(4,1)S(1)} %compare_and_fusion.5), kind=kLoop, calls=%fused_computation.14.clone.1 | loop fusion | flops 3141632 | bytes 3182592 | tf_op jit(solution)/shard_map/while/body/eval_jaxpr/reduce_sum | solution.py:22
  160.5 3.1 fusion.31
  167.8 2.9 copy.18
  170.7 4.1 %select_reduce_fusion.2 = f32[32,128,128]{2,1,0:T(8,128)} fusion(f32[4]{0:T(128)S(1)} %convert_element_type.46, s32[32,128,128]{2,1,0:T(8,128)} %copy.18), kind=kLoop, calls=%fused_computation.9.clone.1 | loop fusion | flops 5767168 | bytes 4194320 | tf_op jit(solution)/shard_map/while/body/eval_jaxpr/reduce_sum | solution.py:16
  174.8 12.1 %gather_fusion = bf16[4096,128]{1,0:T(8,128)(2,1)S(1)} fusion(bf16[4096,128]{1,0:T(8,128)(2,1)S(1)} %get-tuple-element.161, s32[4096]{0:T(1024)S(1)} %fusion.29), kind=kCustom, calls=%fused_computation.clone.1 | custom fusion | bytes 2113536 | tf_op jit(solution)/shard_map/while/body/eval_jaxpr/jit(_take)/gather | solution.py:20
  187.0 3.8 %multiply_reduce_fusion.2 = f32[32,128]{1,0:T(8,128)S(1)} fusion(f32[32,128,128]{2,1,0:T(8,128)} %select_reduce_fusion.2, f32[32,128]{1,0:T(8,128)S(1)} %bitcast_convert_fusion.2, bf16[32,128,128]{2,1,0:T(8,128)(2,1)S(1)} %bitcast.75, pred[32,128]{1,0:T(8,128)(4,1)S(1)} %compare_and_fusion.5), kind=kLoop, calls=%fused_computation.14.clone.1 | loop fusion | flops 3141632 | bytes 3182592 | tf_op jit(solution)/shard_map/while/body/eval_jaxpr/reduce_sum | solution.py:22
  190.9 3.1 fusion.31
  198.2 2.9 copy.18
  201.1 4.1 %select_reduce_fusion.2 = f32[32,128,128]{2,1,0:T(8,128)} fusion(f32[4]{0:T(128)S(1)} %convert_element_type.46, s32[32,128,128]{2,1,0:T(8,128)} %copy.18), kind=kLoop, calls=%fused_computation.9.clone.1 | loop fusion | flops 5767168 | bytes 4194320 | tf_op jit(solution)/shard_map/while/body/eval_jaxpr/reduce_sum | solution.py:16
  205.2 12.1 %gather_fusion = bf16[4096,128]{1,0:T(8,128)(2,1)S(1)} fusion(bf16[4096,128]{1,0:T(8,128)(2,1)S(1)} %get-tuple-element.161, s32[4096]{0:T(1024)S(1)} %fusion.29), kind=kCustom, calls=%fused_computation.clone.1 | custom fusion | bytes 2113536 | tf_op jit(solution)/shard_map/while/body/eval_jaxpr/jit(_take)/gather | solution.py:20
  217.4 3.8 %multiply_reduce_fusion.2 = f32[32,128]{1,0:T(8,128)S(1)} fusion(f32[32,128,128]{2,1,0:T(8,128)} %select_reduce_fusion.2, f32[32,128]{1,0:T(8,128)S(1)} %bitcast_convert_fusion.2, bf16[32,128,128]{2,1,0:T(8,128)(2,1)S(1)} %bitcast.75, pred[32,128]{1,0:T(8,128)(4,1)S(1)} %compare_and_fusion.5), kind=kLoop, calls=%fused_computation.14.clone.1 | loop fusion | flops 3141632 | bytes 3182592 | tf_op jit(solution)/shard_map/while/body/eval_jaxpr/reduce_sum | solution.py:22
  221.3 3.1 fusion.31
  228.6 2.9 copy.18
  231.5 4.1 %select_reduce_fusion.2 = f32[32,128,128]{2,1,0:T(8,128)} fusion(f32[4]{0:T(128)S(1)} %convert_element_type.46, s32[32,128,128]{2,1,0:T(8,128)} %copy.18), kind=kLoop, calls=%fused_computation.9.clone.1 | loop fusion | flops 5767168 | bytes 4194320 | tf_op jit(solution)/shard_map/while/body/eval_jaxpr/reduce_sum | solution.py:16
  235.6 12.1 %gather_fusion = bf16[4096,128]{1,0:T(8,128)(2,1)S(1)} fusion(bf16[4096,128]{1,0:T(8,128)(2,1)S(1)} %get-tuple-element.161, s32[4096]{0:T(1024)S(1)} %fusion.29), kind=kCustom, calls=%fused_computation.clone.1 | custom fusion | bytes 2113536 | tf_op jit(solution)/shard_map/while/body/eval_jaxpr/jit(_take)/gather | solution.py:20
  247.8 3.8 %multiply_reduce_fusion.2 = f32[32,128]{1,0:T(8,128)S(1)} fusion(f32[32,128,128]{2,1,0:T(8,128)} %select_reduce_fusion.2, f32[32,128]{1,0:T(8,128)S(1)} %bitcast_convert_fusion.2, bf16[32,128,128]{2,1,0:T(8,128)(2,1)S(1)} %bitcast.75, pred[32,128]{1,0:T(8,128)(4,1)S(1)} %compare_and_fusion.5), kind=kLoop, calls=%fused_computation.14.clone.1 | loop fusion | flops 3141632 | bytes 3182592 | tf_op jit(solution)/shard_map/while/body/eval_jaxpr/reduce_sum | solution.py:22
  251.6 3.1 fusion.31
  258.9 2.9 copy.18
  261.9 4.1 %select_reduce_fusion.2 = f32[32,128,128]{2,1,0:T(8,128)} fusion(f32[4]{0:T(128)S(1)} %convert_element_type.46, s32[32,128,128]{2,1,0:T(8,128)} %copy.18), kind=kLoop, calls=%fused_computation.9.clone.1 | loop fusion | flops 5767168 | bytes 4194320 | tf_op jit(solution)/shard_map/while/body/eval_jaxpr/reduce_sum | solution.py:16
  266.0 12.1 %gather_fusion = bf16[4096,128]{1,0:T(8,128)(2,1)S(1)} fusion(bf16[4096,128]{1,0:T(8,128)(2,1)S(1)} %get-tuple-element.161, s32[4096]{0:T(1024)S(1)} %fusion.29), kind=kCustom, calls=%fused_computation.clone.1 | custom fusion | bytes 2113536 | tf_op jit(solution)/shard_map/while/body/eval_jaxpr/jit(_take)/gather | solution.py:20
  278.1 3.8 %multiply_reduce_fusion.2 = f32[32,128]{1,0:T(8,128)S(1)} fusion(f32[32,128,128]{2,1,0:T(8,128)} %select_reduce_fusion.2, f32[32,128]{1,0:T(8,128)S(1)} %bitcast_convert_fusion.2, bf16[32,128,128]{2,1,0:T(8,128)(2,1)S(1)} %bitcast.75, pred[32,128]{1,0:T(8,128)(4,1)S(1)} %compare_and_fusion.5), kind=kLoop, calls=%fused_computation.14.clone.1 | loop fusion | flops 3141632 | bytes 3182592 | tf_op jit(solution)/shard_map/while/body/eval_jaxpr/reduce_sum | solution.py:22
  282.0 3.1 fusion.31
  289.3 2.9 copy.18
  292.2 4.1 %select_reduce_fusion.2 = f32[32,128,128]{2,1,0:T(8,128)} fusion(f32[4]{0:T(128)S(1)} %convert_element_type.46, s32[32,128,128]{2,1,0:T(8,128)} %copy.18), kind=kLoop, calls=%fused_computation.9.clone.1 | loop fusion | flops 5767168 | bytes 4194320 | tf_op jit(solution)/shard_map/while/body/eval_jaxpr/reduce_sum | solution.py:16
  296.3 12.1 %gather_fusion = bf16[4096,128]{1,0:T(8,128)(2,1)S(1)} fusion(bf16[4096,128]{1,0:T(8,128)(2,1)S(1)} %get-tuple-element.161, s32[4096]{0:T(1024)S(1)} %fusion.29), kind=kCustom, calls=%fused_computation.clone.1 | custom fusion | bytes 2113536 | tf_op jit(solution)/shard_map/while/body/eval_jaxpr/jit(_take)/gather | solution.py:20
  308.5 3.8 %multiply_reduce_fusion.2 = f32[32,128]{1,0:T(8,128)S(1)} fusion(f32[32,128,128]{2,1,0:T(8,128)} %select_reduce_fusion.2, f32[32,128]{1,0:T(8,128)S(1)} %bitcast_convert_fusion.2, bf16[32,128,128]{2,1,0:T(8,128)(2,1)S(1)} %bitcast.75, pred[32,128]{1,0:T(8,128)(4,1)S(1)} %compare_and_fusion.5), kind=kLoop, calls=%fused_computation.14.clone.1 | loop fusion | flops 3141632 | bytes 3182592 | tf_op jit(solution)/shard_map/while/body/eval_jaxpr/reduce_sum | solution.py:22
  312.4 3.1 fusion.31
  316.9 3.7 %all-to-all-start.2 = ((f32[8,1,32]{2,1,0:T(1,128)}), f32[8,1,32]{2,1,0:T(1,128)S(1)}, u32[]{:S(2)}, u32[]{:S(2)}) async-start(f32[8,1,32]{2,1,0:T(1,128)} %bitcast.19), calls=%async_computation.2 | async-start | bytes 8192 | tf_op jit(solution)/shard_map/all_to_all | solution.py:109
  320.6 6.4 %all-to-all-done.2 = f32[8,1,32]{2,1,0:T(1,128)S(1)} async-done(((f32[8,1,32]{2,1,0:T(1,128)}), f32[8,1,32]{2,1,0:T(1,128)S(1)}, u32[]{:S(2)}, u32[]{:S(2)}) %all-to-all-start.2) | async-done | bytes 1056 | tf_op jit(solution)/shard_map/all_to_all | solution.py:109
  329.6 2.5 psum.7
  (176 shorter events, 56.2 us)
Async XLA Ops:
  0.0 30.1 %copy-start = (s32[64,128,16]{1,2,0:T(8,128)S(1)}, s32[64,128,16]{1,2,0:T(8,128)}, u32[]{:S(2)}) copy-start(s32[64,128,16]{1,2,0:T(8,128)} %param.12) | copy-start | bytes 1572868
  5.5 13.7 %all-to-all-start = ((s32[8,1,32]{2,1,0:T(1,128)}), s32[8,1,32]{2,1,0:T(1,128)S(1)}, u32[]{:S(2)}, u32[]{:S(2)}) async-start(s32[8,1,32]{2,1,0:T(1,128)} %all_to_all.15), calls=%async_computation | async-start | bytes 8192 | tf_op jit(solution)/shard_map/all_to_all | solution.py:96
  19.1 7.4 %copy-start.1 = (s32[64]{0:T(128)S(1)}, s32[64]{0:T(128)}, u32[]{:S(2)}) copy-start(s32[64]{0:T(128)} %param.15) | copy-start | bytes 772
  19.1 9.4 %copy-start.4 = (s32[64,128]{1,0:T(8,128)S(1)}, s32[64,128]{1,0:T(8,128)}, u32[]{:S(2)}) copy-start(s32[64,128]{1,0:T(8,128)} %param.13) | copy-start | bytes 98308
  19.1 54.8 %all-to-all-start.1 = ((bf16[8,32,32,128]{3,2,1,0:T(8,128)(2,1)}), bf16[8,32,32,128]{3,2,1,0:T(8,128)(2,1)}, u32[]{:S(2)}, u32[]{:S(2)}) async-start(bf16[8,32,32,128]{3,2,1,0:T(8,128)(2,1)} %broadcast_select_fusion.2), calls=%async_computation.1 | async-start | bytes 4194304 | tf_op jit(solution)/shard_map/all_to_all | solution.py:97
  25.3 4.0 %copy-start.5 = (bf16[64,128]{1,0:T(8,128)(2,1)S(1)}, bf16[64,128]{1,0:T(8,128)(2,1)}, u32[]{:S(2)}) copy-start(bf16[64,128]{1,0:T(8,128)(2,1)} %param.14) | copy-start | bytes 49156
  32.7 41.3 %copy-start.2 = (bf16[4096,128]{1,0:T(8,128)(2,1)S(1)}, bf16[4096,128]{1,0:T(8,128)(2,1)}, u32[]{:S(2)}) copy-start(bf16[4096,128]{1,0:T(8,128)(2,1)} %param.16) | copy-start | bytes 3145732
  32.7 41.3 %copy-start.6 = (bf16[4]{0:T(256)(128)(2,1)S(1)}, bf16[4]{0:T(256)(128)(2,1)}, u32[]{:S(2)}) copy-start(bf16[4]{0:T(256)(128)(2,1)} %param.17) | copy-start | bytes 28
  95.9 3.9 %copy-start.3 = (f32[32,128,128]{2,1,0:T(8,128)S(1)}, f32[32,128,128]{2,1,0:T(8,128)}, u32[]{:S(2)}) copy-start(f32[32,128,128]{2,1,0:T(8,128)} %select_reduce_fusion.2) | copy-start | bytes 6291460 | tf_op jit(solution)/shard_map/while
  126.2 3.9 %copy-start.3 = (f32[32,128,128]{2,1,0:T(8,128)S(1)}, f32[32,128,128]{2,1,0:T(8,128)}, u32[]{:S(2)}) copy-start(f32[32,128,128]{2,1,0:T(8,128)} %select_reduce_fusion.2) | copy-start | bytes 6291460 | tf_op jit(solution)/shard_map/while
  156.6 3.9 %copy-start.3 = (f32[32,128,128]{2,1,0:T(8,128)S(1)}, f32[32,128,128]{2,1,0:T(8,128)}, u32[]{:S(2)}) copy-start(f32[32,128,128]{2,1,0:T(8,128)} %select_reduce_fusion.2) | copy-start | bytes 6291460 | tf_op jit(solution)/shard_map/while
  187.0 3.9 %copy-start.3 = (f32[32,128,128]{2,1,0:T(8,128)S(1)}, f32[32,128,128]{2,1,0:T(8,128)}, u32[]{:S(2)}) copy-start(f32[32,128,128]{2,1,0:T(8,128)} %select_reduce_fusion.2) | copy-start | bytes 6291460 | tf_op jit(solution)/shard_map/while
  217.4 3.9 %copy-start.3 = (f32[32,128,128]{2,1,0:T(8,128)S(1)}, f32[32,128,128]{2,1,0:T(8,128)}, u32[]{:S(2)}) copy-start(f32[32,128,128]{2,1,0:T(8,128)} %select_reduce_fusion.2) | copy-start | bytes 6291460 | tf_op jit(solution)/shard_map/while
  247.7 3.9 %copy-start.3 = (f32[32,128,128]{2,1,0:T(8,128)S(1)}, f32[32,128,128]{2,1,0:T(8,128)}, u32[]{:S(2)}) copy-start(f32[32,128,128]{2,1,0:T(8,128)} %select_reduce_fusion.2) | copy-start | bytes 6291460 | tf_op jit(solution)/shard_map/while
  278.1 3.9 %copy-start.3 = (f32[32,128,128]{2,1,0:T(8,128)S(1)}, f32[32,128,128]{2,1,0:T(8,128)}, u32[]{:S(2)}) copy-start(f32[32,128,128]{2,1,0:T(8,128)} %select_reduce_fusion.2) | copy-start | bytes 6291460 | tf_op jit(solution)/shard_map/while
  308.5 3.9 %copy-start.3 = (f32[32,128,128]{2,1,0:T(8,128)S(1)}, f32[32,128,128]{2,1,0:T(8,128)}, u32[]{:S(2)}) copy-start(f32[32,128,128]{2,1,0:T(8,128)} %select_reduce_fusion.2) | copy-start | bytes 6291460 | tf_op jit(solution)/shard_map/while
  316.9 10.1 %all-to-all-start.2 = ((f32[8,1,32]{2,1,0:T(1,128)}), f32[8,1,32]{2,1,0:T(1,128)S(1)}, u32[]{:S(2)}, u32[]{:S(2)}) async-start(f32[8,1,32]{2,1,0:T(1,128)} %bitcast.19), calls=%async_computation.2 | async-start | bytes 8192 | tf_op jit(solution)/shard_map/all_to_all | solution.py:109
where the time goes:
time: 335 us; the launch traced here: 333 us
  local copies, waits for them, and re-layouts  156 us (47%)
  other arithmetic  85 us (25%)
  waiting for transfers between devices  44.3 us (13%)
  matrix products  25 us (7%)
  starting transfers between devices  17.1 us (5%)
  blocking collectives  4.74 us (1%)
    gather x8, local copies, waits for them, and re-layouts, decode_tokens(): centre = jnp.take(centroids, ids_here, axis=0).astype(jnp.float32)  97.1 us
    all_to_all x1, waiting for transfers between devices, body(): lax.all_to_all(outgoing_rows, 'shard', split_axis=0, concat_axis=0, tiled...  37.9 us
    reduce_sum x8, other arithmetic, decode_tokens(): jnp.sum(jnp.where(codes[..., None] == levels, buckets.astype(jnp.float32)...  32.7 us
    reduce_sum x8, other arithmetic, decode_tokens(): jnp.sum(summed * summed, axis=-1, keepdims=True) + 1e-06  30.4 us
    dot_general x8, matrix products, score_group(): jnp.einsum('gpd,gtd->gtp', embedded, query_g, preferred_element_type=jnp....  25 us
    and x8, local copies, waits for them, and re-layouts, decode_tokens(): codes = jnp.bitwise_and(jnp.right_shift(packed[..., None], shifts), 3)  23.4 us
    and x8, other arithmetic, decode_tokens(): codes = jnp.bitwise_and(jnp.right_shift(packed[..., None], shifts), 3)  13.4 us
    dynamic_update_slice x8, local copies, waits for them, and re-layouts, score_slots(): lax.map(score_group, (blocked(stored), blocked(ids_here), blocked(scales_...  10.4 us
  transfers between devices with their start and end apart: 3, of which 2 were waited for; matrix products, arithmetic and copies ran while one was open for 4% of the time, Pallas kernels for 0%

commit v1 on v0

v1 whole, which is shorter than its diff:
```python
import functools

import jax
import jax.numpy as jnp
from jax import lax
from jax.experimental import pallas as pl
from jax.experimental.pallas import tpu as pltpu
from jax.sharding import PartitionSpec as P

masked_floor = -1000000000.0
VMEM = pltpu.VMEM
SMEM = pltpu.SMEM
LIMIT = pltpu.CompilerParams(vmem_limit_bytes=40 * 2**20)


def iota(shape, dim):
    return lax.broadcasted_iota(jnp.int32, shape, dim)


def ones_where(mask):
    return jnp.where(mask, 1.0, 0.0).astype(jnp.bfloat16)


def dot(a, b, contract=((1,), (0,))):
    return lax.dot_general(a, b, (contract, ((), ())), preferred_element_type=jnp.float32)


def spread(feature, words, per):
    return per * (feature % words) + feature // words


def pack_kernel(words, passages, query_ref, cand_ref, out_ref):
    count, tokens, width = query_ref.shape
    per = width // words
    order = ones_where(iota((width, width), 0) == spread(iota((width, width), 1), words, per))
    flat = query_ref[...].reshape(count * tokens, width)
    rows = count * tokens
    out_ref[0:rows, :] = dot(flat, order).astype(jnp.bfloat16)
    picks = cand_ref.shape[1]
    repeat = ones_where(iota((picks, width), 0) == iota((picks, width), 1) % picks)
    ids = cand_ref[...]
    owner = ids // passages
    local = ids - owner * passages
    for i, part in enumerate((owner, local)):
        part = part.astype(jnp.float32).astype(jnp.bfloat16)
        out_ref[rows + i * count : rows + (i + 1) * count, :] = dot(part, repeat).astype(jnp.bfloat16)


def decode_kernel(ids_ref, len_ref, words_ref, scale_ref, table_ref, bucket_ref, out_ref, wide, rows):
    count, slots = ids_ref.shape
    entries, width = table_ref.shape
    words = words_ref.shape[1]
    per = width // words
    chunk = 512

    def widen(i, _):
        r = pl.ds(pl.multiple_of(i * chunk, chunk), chunk)
        wide[r, :] = table_ref[r, :].astype(jnp.float32)
        return 0

    lax.fori_loop(0, entries // chunk, widen, 0)
    order = ones_where(iota((width, width), 1) == spread(iota((width, width), 0), words, per))
    eye = iota((slots, slots), 0) == iota((slots, slots), 1)
    levels = [
        jnp.broadcast_to(bucket_ref[0:1, i : i + 1].astype(jnp.float32), (words, slots))
        for i in range(4)
    ]

    def fetch(p, buf):
        for g in range(slots // 16):
            got = jnp.concatenate(
                [wide[pl.ds(ids_ref[p, g * 16 + i], 1), :] for i in range(16)], axis=0
            )
            rows[buf, g * 16 : (g + 1) * 16, :] = got.astype(jnp.bfloat16)

    def build(p, buf):
        packed = words_ref[p]
        parts = []
        for k in range(per):
            low = (packed & (1 << (2 * k))) != 0
            high = (packed & (2 << (2 * k))) != 0
            parts.append(
                jnp.where(
                    high,
                    jnp.where(low, levels[3], levels[2]),
                    jnp.where(low, levels[1], levels[0]),
                )
            )
        value = jnp.concatenate(parts, axis=0)
        scale = scale_ref[pl.ds(p, 1), :]
        raw = dot(order, rows[buf], ((1,), (1,))) + scale * value
        inverse = lax.rsqrt(jnp.sum(raw * raw, axis=0, keepdims=True) + 1e-06)
        out_ref[p] = (raw * inverse).astype(jnp.bfloat16)

    fetch(0, 0)

    def step(i, _):
        fetch(2 * i + 1, 1)
        build(2 * i, 0)
        fetch(jnp.minimum(2 * i + 2, count - 1), 0)
        build(2 * i + 1, 1)
        return 0

    lax.fori_loop(0, count // 2, step, 0)


def pair_kernel(
    queries, picks, capacity, me_ref, len_ref, mine_ref, other_ref, emb_ref, out_ref, slot_v, slot_s, score, sem
):
    blocks = mine_ref.shape[0]
    width = mine_ref.shape[2]
    tokens = (mine_ref.shape[1] - 2 * queries) // queries
    body_rows = queries * tokens
    groups = width // picks
    rows = blocks * queries
    owner = mine_ref[:, body_rows : body_rows + queries, :].reshape(rows, width).astype(jnp.float32)
    local = (
        mine_ref[:, body_rows + queries : body_rows + 2 * queries, :]
        .reshape(rows, width)
        .astype(jnp.float32)
    )
    here = owner == me_ref[0].astype(jnp.float32)
    here_bf = ones_where(here)
    li = iota((width, width), 0)
    lj = iota((width, width), 1)
    before_lane = ones_where((li < picks) & (li < lj % picks))
    whole_row = ones_where(li < picks)
    ri = iota((rows, rows), 0)
    rj = iota((rows, rows), 1)
    before_row = ones_where((ri // queries == rj // queries) & (rj < ri))
    totals = dot(here_bf, whole_row).astype(jnp.bfloat16)
    rank = dot(here_bf, before_lane) + dot(before_row, totals)
    rank = rank.astype(jnp.int32)
    lane_group = iota((rows, width), 1) // picks
    which = (iota((rows, width), 0) % queries).astype(jnp.float32)
    padded = slot_v.shape[0] // 2
    collect = ones_where(iota((padded, rows), 0) == iota((padded, rows), 1) // queries)
    slot_q = jnp.zeros((padded, width), jnp.float32)
    slot_p = jnp.zeros((padded, width), jnp.float32)
    for i in range(-(-capacity // groups)):
        chosen = here & (rank == i * groups + lane_group)
        to_slot = ones_where(lj == i * groups + li // picks)
        got_q = dot(collect, jnp.where(chosen, which, 0.0).astype(jnp.bfloat16))
        got_p = dot(collect, jnp.where(chosen, local, 0.0).astype(jnp.bfloat16))
        slot_q += dot(got_q.astype(jnp.bfloat16), to_slot)
        slot_p += dot(got_p.astype(jnp.bfloat16), to_slot)
    slot_v[0:padded, :] = slot_q.astype(jnp.int32)
    slot_v[padded : 2 * padded, :] = slot_p.astype(jnp.int32)
    copy = pltpu.make_async_copy(slot_v, slot_s, sem)
    copy.start()
    copy.wait()

    lane = iota((2 * tokens, width), 1)
    full_tokens = 2 * tokens

    def block(b, _):
        best_all = jnp.zeros((full_tokens, width), jnp.float32)
        for s in range(capacity):
            p = slot_s[padded + b, s]
            r = pl.ds(pl.multiple_of(slot_s[b, s] * tokens, tokens), tokens)
            rows_q = jnp.concatenate([mine_ref[b, r, :], other_ref[b, r, :]], axis=0)
            similar = dot(rows_q, emb_ref[p])
            similar = jnp.where(lane < len_ref[p], similar, masked_floor)
            best = jnp.max(similar, axis=1, keepdims=True)
            best_all = jnp.where(lane == s, best, best_all)
        score[pl.ds(b, 1), :] = jnp.sum(best_all, axis=0, keepdims=True) * (1.0 / full_tokens)
        return 0

    lax.fori_loop(0, blocks, block, 0)
    for b in range(blocks):
        r = slice(b * queries, (b + 1) * queries)
        line = jnp.broadcast_to(score[b : b + 1, :], (queries, width))
        line = jnp.take_along_axis(line, rank[r], axis=1)
        out_ref[r, :] = jnp.where(here[r], line, 0.0)


def whole(n, *spaces):
    return [pl.BlockSpec(memory_space=s) for s in spaces] * n


def body(queries, candidates, residuals, centroid_ids, block_scales, lengths, centroids, bucket_weights):
    shards = lax.axis_size("shard")
    halves = lax.axis_size("sub")
    query_count, picks = candidates.shape
    tokens, width = queries.shape[1:]
    passages, slots, words = residuals.shape
    capacity = max(2, 2 * query_count * picks // (shards * halves))
    me = (lax.axis_index("shard") * halves + lax.axis_index("sub")).reshape(1)

    def swap_shard(x, d):
        return lax.ppermute(x, "shard", [(i, i ^ d) for i in range(shards)])

    def swap_sub(x):
        return lax.ppermute(x, "sub", [(i, i ^ 1) for i in range(halves)])

    payload = pl.pallas_call(
        functools.partial(pack_kernel, words, passages),
        out_shape=jax.ShapeDtypeStruct((query_count * (tokens + 2), width), jnp.bfloat16),
        in_specs=whole(2, VMEM),
        out_specs=pl.BlockSpec(memory_space=VMEM),
        compiler_params=LIMIT,
        name="pack",
    )(queries, candidates)

    embedded = pl.pallas_call(
        decode_kernel,
        out_shape=jax.ShapeDtypeStruct((passages, width, slots), jnp.bfloat16),
        in_specs=whole(2, SMEM) + whole(4, VMEM),
        out_specs=pl.BlockSpec(memory_space=VMEM),
        scratch_shapes=[
            VMEM((centroids.shape[0], width), jnp.float32),
            VMEM((2, slots, width), jnp.bfloat16),
        ],
        compiler_params=LIMIT,
        name="decode",
    )(
        centroid_ids,
        lengths,
        jnp.swapaxes(residuals, 1, 2),
        block_scales.astype(jnp.float32),
        centroids,
        bucket_weights.reshape(1, 4),
    )

    def score(mine, other):
        blocks = mine.shape[0]
        padded = -(-blocks // 8) * 8
        return pl.pallas_call(
            functools.partial(pair_kernel, query_count, picks, capacity),
            out_shape=jax.ShapeDtypeStruct((blocks * query_count, width), jnp.float32),
            in_specs=whole(2, SMEM) + whole(3, VMEM),
            out_specs=pl.BlockSpec(memory_space=VMEM),
            scratch_shapes=[
                VMEM((2 * padded, width), jnp.int32),
                SMEM((2 * padded, width), jnp.int32),
                VMEM((padded, width), jnp.float32),
                pltpu.SemaphoreType.DMA,
            ],
            compiler_params=LIMIT,
            name="pairs",
        )(me, lengths, mine, other, embedded)

    held = payload[None]
    steps = []
    d = shards // 2
    while d > 1:
        held = jnp.concatenate([held, swap_shard(held, d)], axis=0)
        steps.append(d)
        d //= 2
    far = swap_shard(held, 1)
    near_scores = score(held, swap_sub(held))
    far_scores = score(far, swap_sub(far))
    total = near_scores[:, :picks] + swap_shard(far_scores[:, :picks], 1)
    for d in reversed(steps):
        half = total.shape[0] // 2
        total = total[:half] + swap_shard(total[half:], d)
    return total + swap_sub(total)


def solution(mesh):
    return jax.shard_map(
        body,
        mesh=mesh,
        in_specs=(
            P(("groups", "shard"), "sub", None),
            P(("groups", "shard"), None),
            P(("shard", "sub"), None, None),
            P(("shard", "sub"), None),
            P(("shard", "sub"), None),
            P(("shard", "sub")),
            P(),
            P(),
        ),
        out_specs=P(("groups", "shard"), None),
        check_vma=False,
    )
```

time: 335 us -> 62.3 us (0.19)
  local copies, waits for them, and re-layouts: 156 us -> 5.88 us
  other arithmetic: 85 us -> 1.38 us
  waiting for transfers between devices: 44.3 us -> 18 us
  matrix products: 25 us -> 0 us
  Pallas kernels: 0 us -> 21.8 us
  blocking collectives: 4.74 us -> 0 us
    gather x14 -> x0, local copies, waits for them, and re-layouts: 104 us -> none  [the longest x8 97.1 us: decode_tokens(): centre = jnp.take(centroids, ids_here, axis=0).astype(jnp.float32)]
    reduce_sum x25 -> x0, other arithmetic: 64.2 us -> none  [the longest x8 32.7 us: decode_tokens(): jnp.sum(jnp.where(codes[..., None] == levels, buckets.astype(jnp.float32)...]
    all_to_all x3 -> x0, waiting for transfers between devices: 44.3 us -> none  [the longest x1 37.9 us: body(): lax.all_to_all(outgoing_rows, 'shard', split_axis=0, concat_axis=0, tiled...]
    dot_general x8 -> x0, matrix products: 25 us -> none  [score_group(): jnp.einsum('gpd,gtd->gtp', embedded, query_g, preferred_element_type=jnp....]
    and x8 -> x0, local copies, waits for them, and re-layouts: 23.4 us -> none  [decode_tokens(): codes = jnp.bitwise_and(jnp.right_shift(packed[..., None], shifts), 3)]
    pallas_call x0 -> x4, Pallas kernels: none -> 21.8 us  [the longest x1 13.6 us: body(): pl.pallas_call(decode_kernel, out_shape=jax.ShapeDtypeStruct((passages, w...]
    ppermute x0 -> x9, waiting for transfers between devices: none -> 18 us  [the longest x6 16.9 us: swap_shard(): return lax.ppermute(x, 'shard', [(i, i ^ d) for i in range(shards)])]
    all_to_all x3 -> x0, starting transfers between devices: 17.1 us -> none  [the longest x1 7.28 us: body(): lax.all_to_all(wanted, 'shard', split_axis=0, concat_axis=0, tiled=True)]
  transfers between devices with their start and end apart: 3 -> 9, of which waited for: 2 -> 6; matrix products, arithmetic and copies ran while one was open for 4% -> 1% of each run, Pallas kernels for 0% -> 35%
where the time goes in v1:
time: 62.3 us; the launch traced here: 61.9 us
  Pallas kernels  21.8 us (35%)
  waiting for transfers between devices  18 us (29%)
  starting transfers between devices  14.8 us (24%)
  local copies, waits for them, and re-layouts  5.88 us (9%)
  other arithmetic  1.38 us (2%)
    ppermute x6, waiting for transfers between devices, swap_shard(): return lax.ppermute(x, 'shard', [(i, i ^ d) for i in range(shards)])  16.9 us
    ppermute x6, starting transfers between devices, swap_shard(): return lax.ppermute(x, 'shard', [(i, i ^ d) for i in range(shards)])  14.2 us
    pallas_call x1, Pallas kernels, body(): pl.pallas_call(decode_kernel, out_shape=jax.ShapeDtypeStruct((passages, w...  13.6 us
    pallas_call x2, Pallas kernels, score(): pl.pallas_call(functools.partial(pair_kernel, query_count, picks, capacit...  8.03 us
    unnamed x14, local copies, waits for them, and re-layouts  5.87 us
  transfers between devices with their start and end apart: 9, of which 6 were waited for; matrix products, arithmetic and copies ran while one was open for 1% of the time, Pallas kernels for 35%

profile of v1, /device:TPU:0, one launch (start us, length us, event | category | flops | bytes accessed | tf_op | source)
XLA Modules:
  0.0 61.9 jit_solution(14311703115399972095)
XLA Ops:
  0.0 0.0 copy-start.2
  0.0 0.8 %copy-done.2 = bf16[16,16,128]{2,1,0:T(8,128)(2,1)S(1)} copy-done((bf16[16,16,128]{2,1,0:T(8,128)(2,1)S(1)}, bf16[16,16,128]{2,1,0:T(8,128)(2,1)}, u32[]{:S(2)}) %copy-start.2) | copy-done | bytes 65560
  0.8 0.0 copy-start.4
  0.8 0.7 %copy-done.4 = s32[16,16]{1,0:T(8,128)S(1)} copy-done((s32[16,16]{1,0:T(8,128)S(1)}, s32[16,16]{1,0:T(8,128)}, u32[]{:S(2)}) %copy-start.4) | copy-done | bytes 1048
  1.5 0.2 pack.1
  1.7 4.1 %collective-permute-start = (bf16[1,288,128]{2,1,0:T(8,128)(2,1)S(1)}, bf16[1,288,128]{2,1,0:T(8,128)(2,1)S(1)}, u32[]{:S(2)}, u32[]{:S(2)}) collective-permute-start(bf16[1,288,128]{2,1,0:T(8,128)(2,1)S(1)} %bitcast.5), channel_id=1, source_target_pairs={{0,8},{2,10},{4,12},{6,14},{8,0},{10,2},{12,4},{14,6},{1,9},{3,11}... | collective-permute-start | bytes 221192 | tf_op jit(solution)/shard_map/ppermute | solution.py:191
  5.8 3.9 %collective-permute-done = bf16[1,288,128]{2,1,0:T(8,128)(2,1)S(1)} collective-permute-done((bf16[1,288,128]{2,1,0:T(8,128)(2,1)S(1)}, bf16[1,288,128]{2,1,0:T(8,128)(2,1)S(1)}, u32[]{:S(2)}, u32[]{:S(2)}) %collective-permute-start) | collective-permute-done | bytes 73760 | tf_op jit(solution)/shard_map/ppermute | solution.py:191
  9.7 0.7 %collective-permute-start.1 = (bf16[2,288,128]{2,1,0:T(8,128)(2,1)S(1)}, bf16[2,288,128]{2,1,0:T(8,128)(2,1)S(1)}, u32[]{:S(2)}, u32[]{:S(2)}) collective-permute-start(bf16[2,288,128]{2,1,0:T(8,128)(2,1)S(1)} %pad_maximum_fusion.1), channel_id=1, source_target_pairs={{0,4},{2,6},{4,0},{6,2},{8,12},{10,14},{12,8},{14,10},{1,5},{3,7},... | collective-permute-start | bytes 442376 | tf_op jit(solution)/shard_map/ppermute | solution.py:191
  10.5 4.5 %collective-permute-done.1 = bf16[2,288,128]{2,1,0:T(8,128)(2,1)S(1)} collective-permute-done((bf16[2,288,128]{2,1,0:T(8,128)(2,1)S(1)}, bf16[2,288,128]{2,1,0:T(8,128)(2,1)S(1)}, u32[]{:S(2)}, u32[]{:S(2)}) %collective-permute-start.1) | collective-permute-done | bytes 147488 | tf_op jit(solution)/shard_map/ppermute | solution.py:191
  15.0 1.8 %collective-permute-start.3 = (bf16[4,288,128]{2,1,0:T(8,128)(2,1)S(1)}, bf16[4,288,128]{2,1,0:T(8,128)(2,1)S(1)}, u32[]{:S(2)}, u32[]{:S(2)}) collective-permute-start(bf16[4,288,128]{2,1,0:T(8,128)(2,1)S(1)} %pad_maximum_fusion.mine_ref), channel_id=1, source_target_pairs={{0,2},{2,0},{4,6},{6,4},{8,10},{10,8},{12,14},{14,12},{1,3},{3,1},... | collective-permute-start | bytes 884744 | tf_op jit(solution)/shard_map/ppermute | solution.py:191
  16.8 5.0 %collective-permute-done.3.mine_ref = bf16[4,288,128]{2,1,0:T(8,128)(2,1)S(1)} collective-permute-done((bf16[4,288,128]{2,1,0:T(8,128)(2,1)S(1)}, bf16[4,288,128]{2,1,0:T(8,128)(2,1)S(1)}, u32[]{:S(2)}, u32[]{:S(2)}) %collective-permute-start.3) | collective-permute-done | bytes 294944 | tf_op jit(solution)/shard_map/ppermute | solution.py:191
  21.8 0.0 collective-permute-start.4
  21.8 0.5 collective-permute-start.2
  22.3 0.7 %convert_element_type.3.scale_ref = f32[64,128]{1,0:T(8,128)S(1)} convert(bf16[64,128]{1,0:T(8,128)(2,1)} %param.12) | non-fusion elementwise | flops 8192 | bytes 49152 | tf_op jit(solution)/shard_map/convert_element_type | solution.py:220
  23.0 0.0 copy-start
  23.0 1.2 %copy-done = bf16[4096,128]{1,0:T(8,128)(2,1)S(1)} copy-done((bf16[4096,128]{1,0:T(8,128)(2,1)S(1)}, bf16[4096,128]{1,0:T(8,128)(2,1)}, u32[]{:S(2)}) %copy-start) | copy-done | bytes 1048600
  24.2 0.0 copy-start.1
  24.2 1.0 %copy-done.1 = s32[64,128,16]{1,2,0:T(8,128)S(1)} copy-done((s32[64,128,16]{1,2,0:T(8,128)S(1)}, s32[64,128,16]{1,2,0:T(8,128)}, u32[]{:S(2)}) %copy-start.1) | copy-done | bytes 524312
  25.3 0.0 copy-start.3
  25.3 0.8 %copy-done.3 = s32[64,128]{1,0:T(8,128)S(1)} copy-done((s32[64,128]{1,0:T(8,128)S(1)}, s32[64,128]{1,0:T(8,128)}, u32[]{:S(2)}) %copy-start.3) | copy-done | bytes 32792
  26.0 0.0 copy-start.5
  26.0 0.7 %copy-done.5 = s32[64]{0:T(128)S(1)} copy-done((s32[64]{0:T(128)S(1)}, s32[64]{0:T(128)}, u32[]{:S(2)}) %copy-start.5) | copy-done | bytes 280
  26.7 0.0 copy-start.6
  26.7 0.7 %copy-done.6 = bf16[4]{0:T(256)(128)(2,1)S(1)} copy-done((bf16[4]{0:T(256)(128)(2,1)S(1)}, bf16[4]{0:T(256)(128)(2,1)}, u32[]{:S(2)}) %copy-start.6) | copy-done | bytes 32
  27.3 13.6 %decode.1.emb_ref = bf16[64,128,128]{2,1,0:T(8,128)(2,1)S(1)} custom-call(s32[64,128]{1,0:T(8,128)S(1)} %copy-done.3, s32[64]{0:T(128)S(1)} %copy-done.5, s32[64,16,128]{2,1,0:T(8,128)S(1)} %bitcast.8, f32[64,128]{1,0:T(8,128)S(1)} %convert_element_type.3.scale_ref, bf16[4096,128]{1,0:T(8,128)(2,1)S(1)} %copy-done, bf16[1,4]{1,0:T(2,128)(2,1)S(1)} %bitcast.10), custom_call_target="tpu_custom_call" | custom-call | tf_op jit(solution)/shard_map/decode/pallas_call | solution.py:205
  40.9 0.0 collective-permute-done.4.other_ref
  40.9 4.0 %pairs.3 = f32[64,128]{1,0:T(8,128)S(1)} custom-call(s32[1]{0:T(128)} %bitcast.me_ref, s32[64]{0:T(128)S(1)} %copy-done.5, bf16[4,288,128]{2,1,0:T(8,128)(2,1)S(1)} %collective-permute-done.3.mine_ref, bf16[4,288,128]{2,1,0:T(8,128)(2,1)S(1)} %collective-permute-done.4.other_ref, bf16[64,128,128]{2,1,0:T(8,128)(2,1)S(1)} %decode.1.emb_ref), custom_call_target="tpu_custom_call" | custom-call | tf_op jit(solution)/shard_map/pairs/pallas_call | solution.py:228
  44.9 1.8 %collective-permute-start.5 = (f32[64,16]{1,0:T(8,128)S(1)}, f32[64,16]{1,0:T(8,128)S(1)}, u32[]{:S(2)}, u32[]{:S(2)}) collective-permute-start(f32[64,16]{1,0:T(8,128)S(1)} %bitcast.9), channel_id=1, source_target_pairs={{0,2},{2,0},{4,6},{6,4},{8,10},{10,8},{12,14},{14,12},{1,3},{3,1},... | collective-permute-start | bytes 12296 | tf_op jit(solution)/shard_map/ppermute | solution.py:191
  46.7 0.0 collective-permute-done.2.other_ref
  46.7 4.0 %pairs.2 = f32[64,128]{1,0:T(8,128)S(1)} custom-call(s32[1]{0:T(128)} %bitcast.me_ref, s32[64]{0:T(128)S(1)} %copy-done.5, bf16[4,288,128]{2,1,0:T(8,128)(2,1)S(1)} %pad_maximum_fusion.mine_ref, bf16[4,288,128]{2,1,0:T(8,128)(2,1)S(1)} %collective-permute-done.2.other_ref, bf16[64,128,128]{2,1,0:T(8,128)(2,1)S(1)} %decode.1.emb_ref), custom_call_target="tpu_custom_call" | custom-call | tf_op jit(solution)/shard_map/pairs/pallas_call | solution.py:228
  50.8 0.0 collective-permute-done.5
  50.8 2.0 %collective-permute-start.6 = (f32[32,16]{1,0:T(8,128)S(1)}, f32[32,16]{1,0:T(8,128)S(1)}, u32[]{:S(2)}, u32[]{:S(2)}) collective-permute-start(f32[32,16]{1,0:T(8,128)S(1)} %slice.27), channel_id=1, source_target_pairs={{0,4},{2,6},{4,0},{6,2},{8,12},{10,14},{12,8},{14,10},{1,5},{3,7},... | collective-permute-start | bytes 6152 | tf_op jit(solution)/shard_map/ppermute | solution.py:191
  52.8 1.8 %collective-permute-done.6 = f32[32,16]{1,0:T(8,128)S(1)} collective-permute-done((f32[32,16]{1,0:T(8,128)S(1)}, f32[32,16]{1,0:T(8,128)S(1)}, u32[]{:S(2)}, u32[]{:S(2)}) %collective-permute-start.6) | collective-permute-done | bytes 2080 | tf_op jit(solution)/shard_map/ppermute | solution.py:191
  54.6 3.9 %collective-permute-start.7 = (f32[16,16]{1,0:T(8,128)S(1)}, f32[16,16]{1,0:T(8,128)S(1)}, u32[]{:S(2)}, u32[]{:S(2)}) collective-permute-start(f32[16,16]{1,0:T(8,128)S(1)} %slice.29), channel_id=1, source_target_pairs={{0,8},{2,10},{4,12},{6,14},{8,0},{10,2},{12,4},{14,6},{1,9},{3,11}... | collective-permute-start | bytes 3080 | tf_op jit(solution)/shard_map/ppermute | solution.py:191
  58.5 1.6 %collective-permute-done.7 = f32[16,16]{1,0:T(8,128)S(1)} collective-permute-done((f32[16,16]{1,0:T(8,128)S(1)}, f32[16,16]{1,0:T(8,128)S(1)}, u32[]{:S(2)}, u32[]{:S(2)}) %collective-permute-start.7) | collective-permute-done | bytes 1056 | tf_op jit(solution)/shard_map/ppermute | solution.py:191
  60.1 0.0 collective-permute-start.8
  60.1 1.2 %collective-permute-done.8 = f32[16,16]{1,0:T(8,128)S(1)} collective-permute-done((f32[16,16]{1,0:T(8,128)S(1)}, f32[16,16]{1,0:T(8,128)S(1)}, u32[]{:S(2)}, u32[]{:S(2)}) %collective-permute-start.8) | collective-permute-done | bytes 1056 | tf_op jit(solution)/shard_map/ppermute | solution.py:194
  61.3 0.6 add.19
  (7 shorter events, 0.1 us)
Async XLA Ops:
  0.0 0.8 %copy-start.2 = (bf16[16,16,128]{2,1,0:T(8,128)(2,1)S(1)}, bf16[16,16,128]{2,1,0:T(8,128)(2,1)}, u32[]{:S(2)}) copy-start(bf16[16,16,128]{2,1,0:T(8,128)(2,1)} %query_ref.1) | copy-start | bytes 196612
  0.8 0.7 %copy-start.4 = (s32[16,16]{1,0:T(8,128)S(1)}, s32[16,16]{1,0:T(8,128)}, u32[]{:S(2)}) copy-start(s32[16,16]{1,0:T(8,128)} %cand_ref.1) | copy-start | bytes 3076
  1.7 8.0 %collective-permute-start = (bf16[1,288,128]{2,1,0:T(8,128)(2,1)S(1)}, bf16[1,288,128]{2,1,0:T(8,128)(2,1)S(1)}, u32[]{:S(2)}, u32[]{:S(2)}) collective-permute-start(bf16[1,288,128]{2,1,0:T(8,128)(2,1)S(1)} %bitcast.5), channel_id=1, source_target_pairs={{0,8},{2,10},{4,12},{6,14},{8,0},{10,2},{12,4},{14,6},{1,9},{3,11}... | collective-permute-start | bytes 221192 | tf_op jit(solution)/shard_map/ppermute | solution.py:191
  9.7 5.2 %collective-permute-start.1 = (bf16[2,288,128]{2,1,0:T(8,128)(2,1)S(1)}, bf16[2,288,128]{2,1,0:T(8,128)(2,1)S(1)}, u32[]{:S(2)}, u32[]{:S(2)}) collective-permute-start(bf16[2,288,128]{2,1,0:T(8,128)(2,1)S(1)} %pad_maximum_fusion.1), channel_id=1, source_target_pairs={{0,4},{2,6},{4,0},{6,2},{8,12},{10,14},{12,8},{14,10},{1,5},{3,7},... | collective-permute-start | bytes 442376 | tf_op jit(solution)/shard_map/ppermute | solution.py:191
  15.0 6.8 %collective-permute-start.3 = (bf16[4,288,128]{2,1,0:T(8,128)(2,1)S(1)}, bf16[4,288,128]{2,1,0:T(8,128)(2,1)S(1)}, u32[]{:S(2)}, u32[]{:S(2)}) collective-permute-start(bf16[4,288,128]{2,1,0:T(8,128)(2,1)S(1)} %pad_maximum_fusion.mine_ref), channel_id=1, source_target_pairs={{0,2},{2,0},{4,6},{6,4},{8,10},{10,8},{12,14},{14,12},{1,3},{3,1},... | collective-permute-start | bytes 884744 | tf_op jit(solution)/shard_map/ppermute | solution.py:191
  21.8 19.1 %collective-permute-start.4 = (bf16[4,288,128]{2,1,0:T(8,128)(2,1)S(1)}, bf16[4,288,128]{2,1,0:T(8,128)(2,1)S(1)}, u32[]{:S(2)}, u32[]{:S(2)}) collective-permute-start(bf16[4,288,128]{2,1,0:T(8,128)(2,1)S(1)} %collective-permute-done.3.mine_ref), channel_id=1, source_target_pairs={{0,1},{1,0},{2,3},{3,2},{4,5},{5,4},{6,7},{7,6},{8,9},{9,8},{10,11... | collective-permute-start | bytes 884744 | tf_op jit(solution)/shard_map/ppermute | solution.py:194
  21.8 25.0 %collective-permute-start.2 = (bf16[4,288,128]{2,1,0:T(8,128)(2,1)S(1)}, bf16[4,288,128]{2,1,0:T(8,128)(2,1)S(1)}, u32[]{:S(2)}, u32[]{:S(2)}) collective-permute-start(bf16[4,288,128]{2,1,0:T(8,128)(2,1)S(1)} %pad_maximum_fusion.mine_ref), channel_id=1, source_target_pairs={{0,1},{1,0},{2,3},{3,2},{4,5},{5,4},{6,7},{7,6},{8,9},{9,8},{10,11... | collective-permute-start | bytes 884744 | tf_op jit(solution)/shard_map/ppermute | solution.py:194
  23.0 1.2 %copy-start = (bf16[4096,128]{1,0:T(8,128)(2,1)S(1)}, bf16[4096,128]{1,0:T(8,128)(2,1)}, u32[]{:S(2)}) copy-start(bf16[4096,128]{1,0:T(8,128)(2,1)} %table_ref.1) | copy-start | bytes 3145732
  24.2 1.0 %copy-start.1 = (s32[64,128,16]{1,2,0:T(8,128)S(1)}, s32[64,128,16]{1,2,0:T(8,128)}, u32[]{:S(2)}) copy-start(s32[64,128,16]{1,2,0:T(8,128)} %param.10) | copy-start | bytes 1572868
  25.3 0.8 %copy-start.3 = (s32[64,128]{1,0:T(8,128)S(1)}, s32[64,128]{1,0:T(8,128)}, u32[]{:S(2)}) copy-start(s32[64,128]{1,0:T(8,128)} %ids_ref.1) | copy-start | bytes 98308
  26.0 0.7 %copy-start.5 = (s32[64]{0:T(128)S(1)}, s32[64]{0:T(128)}, u32[]{:S(2)}) copy-start(s32[64]{0:T(128)} %len_ref.5) | copy-start | bytes 772
  26.7 0.7 %copy-start.6 = (bf16[4]{0:T(256)(128)(2,1)S(1)}, bf16[4]{0:T(256)(128)(2,1)}, u32[]{:S(2)}) copy-start(bf16[4]{0:T(256)(128)(2,1)} %param.15) | copy-start | bytes 28
  44.9 5.8 %collective-permute-start.5 = (f32[64,16]{1,0:T(8,128)S(1)}, f32[64,16]{1,0:T(8,128)S(1)}, u32[]{:S(2)}, u32[]{:S(2)}) collective-permute-start(f32[64,16]{1,0:T(8,128)S(1)} %bitcast.9), channel_id=1, source_target_pairs={{0,2},{2,0},{4,6},{6,4},{8,10},{10,8},{12,14},{14,12},{1,3},{3,1},... | collective-permute-start | bytes 12296 | tf_op jit(solution)/shard_map/ppermute | solution.py:191
  50.8 3.8 %collective-permute-start.6 = (f32[32,16]{1,0:T(8,128)S(1)}, f32[32,16]{1,0:T(8,128)S(1)}, u32[]{:S(2)}, u32[]{:S(2)}) collective-permute-start(f32[32,16]{1,0:T(8,128)S(1)} %slice.27), channel_id=1, source_target_pairs={{0,4},{2,6},{4,0},{6,2},{8,12},{10,14},{12,8},{14,10},{1,5},{3,7},... | collective-permute-start | bytes 6152 | tf_op jit(solution)/shard_map/ppermute | solution.py:191
  54.6 5.5 %collective-permute-start.7 = (f32[16,16]{1,0:T(8,128)S(1)}, f32[16,16]{1,0:T(8,128)S(1)}, u32[]{:S(2)}, u32[]{:S(2)}) collective-permute-start(f32[16,16]{1,0:T(8,128)S(1)} %slice.29), channel_id=1, source_target_pairs={{0,8},{2,10},{4,12},{6,14},{8,0},{10,2},{12,4},{14,6},{1,9},{3,11}... | collective-permute-start | bytes 3080 | tf_op jit(solution)/shard_map/ppermute | solution.py:191
  60.1 1.2 %collective-permute-start.8 = (f32[16,16]{1,0:T(8,128)S(1)}, f32[16,16]{1,0:T(8,128)S(1)}, u32[]{:S(2)}, u32[]{:S(2)}) collective-permute-start(f32[16,16]{1,0:T(8,128)S(1)} %slice_add_fusion.2), channel_id=1, source_target_pairs={{0,1},{1,0},{2,3},{3,2},{4,5},{5,4},{6,7},{7,6},{8,9},{9,8},{10,11... | collective-permute-start | bytes 3080 | tf_op jit(solution)/shard_map/ppermute | solution.py:194

commit v2 on v1

v2 whole, which is shorter than its diff:
```python
import functools

import jax
import jax.numpy as jnp
from jax import lax
from jax.experimental import pallas as pl
from jax.experimental.pallas import tpu as pltpu
from jax.sharding import PartitionSpec as P

masked_floor = -1000000000.0
VMEM = pltpu.VMEM
SMEM = pltpu.SMEM
LIMIT = pltpu.CompilerParams(vmem_limit_bytes=40 * 2**20)


def iota(shape, dim):
    return lax.broadcasted_iota(jnp.int32, shape, dim)


def ones_where(mask):
    return jnp.where(mask, 1.0, 0.0).astype(jnp.bfloat16)


def dot(a, b, contract=((1,), (0,))):
    return lax.dot_general(a, b, (contract, ((), ())), preferred_element_type=jnp.float32)


def spread(feature, words, per):
    return per * (feature % words) + feature // words


def pack_kernel(words, passages, query_hbm, cand_hbm, out_ref, query_ref, cand_ref, sems):
    copies = [
        pltpu.make_async_copy(query_hbm, query_ref, sems.at[0]),
        pltpu.make_async_copy(cand_hbm, cand_ref, sems.at[1]),
    ]
    for c in copies:
        c.start()
    count, tokens, width = query_ref.shape
    per = width // words
    order = ones_where(iota((width, width), 0) == spread(iota((width, width), 1), words, per))
    picks = cand_ref.shape[1]
    repeat = ones_where(iota((picks, width), 0) == iota((picks, width), 1) % picks)
    for c in copies:
        c.wait()
    flat = query_ref[...].reshape(count * tokens, width)
    rows = count * tokens
    out_ref[0:rows, :] = dot(flat, order).astype(jnp.bfloat16)
    ids = cand_ref[...]
    owner = ids // passages
    local = ids - owner * passages
    for i, part in enumerate((owner, local)):
        part = part.astype(jnp.float32).astype(jnp.bfloat16)
        out_ref[rows + i * count : rows + (i + 1) * count, :] = dot(part, repeat).astype(jnp.bfloat16)


WIDE = 4


def decode_kernel(first, start, stop, *refs):
    if first:
        ids_hbm, words_hbm, scale_hbm, bucket_hbm, table_hbm, out_ref, wide = refs[:7]
        rest = refs[7:]
    else:
        ids_hbm, words_hbm, scale_hbm, bucket_hbm, wide, _, out_ref = refs[:7]
        rest = refs[7:]
    rows, ids_ref, words_ref, scale_bf, scale_ref, bucket_ref, sems = rest[:7]
    mine = pl.ds(start, stop - start)
    copies = [
        pltpu.make_async_copy(ids_hbm.at[mine], ids_ref, sems.at[0]),
        pltpu.make_async_copy(words_hbm.at[mine], words_ref, sems.at[1]),
        pltpu.make_async_copy(scale_hbm, scale_bf, sems.at[2]),
        pltpu.make_async_copy(bucket_hbm, bucket_ref, sems.at[3]),
    ]
    if first:
        table_ref = rest[7]
        parts = 4
        size = table_ref.shape[0] // parts
        loads = [
            pltpu.make_async_copy(
                table_hbm.at[pl.ds(i * size, size)], table_ref.at[pl.ds(i * size, size)], sems.at[4 + i]
            )
            for i in range(parts)
        ]
        for c in loads + copies:
            c.start()
        chunk = 256
        for i in range(parts):
            loads[i].wait()

            def widen(j, _):
                r = pl.ds(pl.multiple_of(i * size + j * chunk, chunk), chunk)
                wide[r, :] = table_ref[r, :].astype(jnp.float32)
                return 0

            lax.fori_loop(0, size // chunk, widen, 0)
    else:
        for c in copies:
            c.start()
    for c in copies:
        c.wait()
    scale_ref[...] = scale_bf[...].astype(jnp.float32)
    slots = ids_ref.shape[1]
    width = wide.shape[1]
    words = words_ref.shape[1]
    per = width // words
    order = ones_where(iota((width, width), 1) == spread(iota((width, width), 0), words, per))
    levels = [
        jnp.broadcast_to(bucket_ref[0:1, i : i + 1].astype(jnp.float32), (words, slots * WIDE))
        for i in range(4)
    ]

    def fetch(p, buf):
        for u in range(WIDE):
            for g in range(slots // 16):
                got = jnp.concatenate(
                    [wide[pl.ds(ids_ref[p + u, g * 16 + i], 1), :] for i in range(16)], axis=0
                )
                r = u * slots + g * 16
                rows[buf, r : r + 16, :] = got.astype(jnp.bfloat16)
                yield

    def build(p, buf, fetching):
        packed = jnp.concatenate([words_ref[p + u] for u in range(WIDE)], axis=1)
        centre = dot(order, rows[buf], ((1,), (1,)))
        parts = []
        for k in range(per):
            for _ in range(WIDE):
                next(fetching, None)
            low = (packed & (1 << (2 * k))) != 0
            high = (packed & (2 << (2 * k))) != 0
            parts.append(
                jnp.where(
                    high,
                    jnp.where(low, levels[3], levels[2]),
                    jnp.where(low, levels[1], levels[0]),
                )
            )
        value = jnp.concatenate(parts, axis=0)
        scale = jnp.concatenate([scale_ref[pl.ds(start + p + u, 1), :] for u in range(WIDE)], axis=1)
        raw = centre + scale * value
        inverse = lax.rsqrt(jnp.sum(raw * raw, axis=0, keepdims=True) + 1e-06)
        out = (raw * inverse).astype(jnp.bfloat16)
        for u in range(WIDE):
            out_ref[start + p + u] = out[:, u * slots : (u + 1) * slots]
        for _ in fetching:
            pass

    for _ in fetch(0, 0):
        pass

    def step(i, _):
        p = 2 * WIDE * i
        build(p, 0, fetch(p + WIDE, 1))
        build(p + WIDE, 1, fetch(p + 2 * WIDE, 0))
        return 0

    last = stop - start - 2 * WIDE
    lax.fori_loop(0, last // (2 * WIDE), step, 0)
    build(last, 0, fetch(last + WIDE, 1))
    build(last + WIDE, 1, iter(()))


def slot_kernel(queries, picks, capacity, rows_ref, slot_ref, rank_ref):
    blocks = rows_ref.shape[0]
    width = rows_ref.shape[2]
    body_rows = rows_ref.shape[1] - 2 * queries
    groups = width // picks
    rows = blocks * queries
    me = lax.axis_index("shard") * lax.axis_size("sub") + lax.axis_index("sub")
    owner = rows_ref[:, body_rows : body_rows + queries, :].reshape(rows, width).astype(jnp.float32)
    local = (
        rows_ref[:, body_rows + queries : body_rows + 2 * queries, :]
        .reshape(rows, width)
        .astype(jnp.float32)
    )
    here = owner == jnp.full((rows, width), me, jnp.int32).astype(jnp.float32)
    here_bf = ones_where(here)
    li = iota((width, width), 0)
    lj = iota((width, width), 1)
    before_lane = ones_where((li < picks) & (li < lj % picks))
    whole_row = ones_where(li < picks)
    ri = iota((rows, rows), 0)
    rj = iota((rows, rows), 1)
    before_row = ones_where((ri // queries == rj // queries) & (rj < ri))
    totals = dot(here_bf, whole_row).astype(jnp.bfloat16)
    rank = dot(here_bf, before_lane) + dot(before_row, totals)
    rank = rank.astype(jnp.int32)
    rank_ref[...] = jnp.where(here, rank, -1)
    lane_group = iota((rows, width), 1) // picks
    which = (iota((rows, width), 0) % queries).astype(jnp.float32)
    padded = slot_ref.shape[0] // 2
    collect = ones_where(iota((padded, rows), 0) == iota((padded, rows), 1) // queries)
    slot_q = jnp.zeros((padded, width), jnp.float32)
    slot_p = jnp.zeros((padded, width), jnp.float32)
    for i in range(-(-capacity // groups)):
        chosen = here & (rank == i * groups + lane_group)
        to_slot = ones_where(lj == i * groups + li // picks)
        got_q = dot(collect, jnp.where(chosen, which, 0.0).astype(jnp.bfloat16))
        got_p = dot(collect, jnp.where(chosen, local, 0.0).astype(jnp.bfloat16))
        slot_q += dot(got_q.astype(jnp.bfloat16), to_slot)
        slot_p += dot(got_p.astype(jnp.bfloat16), to_slot)
    slot_ref[0:padded, :] = slot_q.astype(jnp.int32)
    slot_ref[padded : 2 * padded, :] = slot_p.astype(jnp.int32)


def pair_kernel(
    queries, picks, capacity, len_hbm, slot_ref, rank_ref, mine_ref, other_ref, emb_ref, out_ref, slot_s, len_s, score, sems
):
    copies = [
        pltpu.make_async_copy(slot_ref, slot_s, sems.at[0]),
        pltpu.make_async_copy(len_hbm, len_s, sems.at[1]),
    ]
    for c in copies:
        c.start()
    for c in copies:
        c.wait()
    blocks = mine_ref.shape[0]
    width = mine_ref.shape[2]
    tokens = (mine_ref.shape[1] - 2 * queries) // queries
    padded = slot_s.shape[0] // 2
    full_tokens = 2 * tokens
    lane = iota((full_tokens, width), 1)

    def block(b, _):
        best_all = jnp.zeros((full_tokens, width), jnp.float32)
        for s in range(capacity):
            p = slot_s[padded + b, s]
            r = pl.ds(pl.multiple_of(slot_s[b, s] * tokens, tokens), tokens)
            rows_q = jnp.concatenate([mine_ref[b, r, :], other_ref[b, r, :]], axis=0)
            similar = dot(rows_q, emb_ref[p])
            similar = jnp.where(lane < len_s[p], similar, masked_floor)
            best = jnp.max(similar, axis=1, keepdims=True)
            best_all = jnp.where(lane == s, best, best_all)
        score[pl.ds(b, 1), :] = jnp.sum(best_all, axis=0, keepdims=True) * (1.0 / full_tokens)
        return 0

    lax.fori_loop(0, blocks, block, 0)
    groups = width // picks
    lane_group = iota((queries, width), 1) // picks
    for c in range(0, blocks, groups):
        out = jnp.zeros((queries, width), jnp.float32)
        for b in range(c, min(c + groups, blocks)):
            rank = rank_ref[b * queries : (b + 1) * queries, :]
            line = jnp.broadcast_to(score[b : b + 1, :], (queries, width))
            line = jnp.take_along_axis(line, jnp.maximum(rank, 0), axis=1)
            out = jnp.where((rank >= 0) & (lane_group == b - c), line, out)
        out_ref[:, c * picks : c * picks + width] = out


def whole(n, *spaces):
    return [pl.BlockSpec(memory_space=s) for s in spaces] * n


def body(queries, candidates, residuals, centroid_ids, block_scales, lengths, centroids, bucket_weights):
    shards = lax.axis_size("shard")
    halves = lax.axis_size("sub")
    query_count, picks = candidates.shape
    tokens, width = queries.shape[1:]
    passages, slots, words = residuals.shape
    capacity = max(2, 2 * query_count * picks // (shards * halves))

    def swap_shard(x, d):
        return lax.ppermute(x, "shard", [(i, i ^ d) for i in range(shards)])

    def swap_sub(x):
        return lax.ppermute(x, "sub", [(i, i ^ 1) for i in range(halves)])

    payload = pl.pallas_call(
        functools.partial(pack_kernel, words, passages),
        out_shape=jax.ShapeDtypeStruct((query_count * (tokens + 2), width), jnp.bfloat16),
        in_specs=whole(2, pltpu.HBM),
        out_specs=pl.BlockSpec(memory_space=VMEM),
        scratch_shapes=[
            VMEM(queries.shape, queries.dtype),
            VMEM(candidates.shape, candidates.dtype),
            pltpu.SemaphoreType.DMA((2,)),
        ],
        compiler_params=LIMIT,
        name="pack",
    )(queries, candidates)

    stored = (
        centroid_ids,
        jnp.swapaxes(residuals, 1, 2),
        block_scales,
        bucket_weights.reshape(1, 4),
    )
    emb_shape = jax.ShapeDtypeStruct((passages, width, slots), jnp.bfloat16)
    wide_shape = jax.ShapeDtypeStruct(centroids.shape, jnp.float32)

    def decode(start, stop, wide, embedded):
        first = embedded is None
        extra = (centroids,) if first else (wide, embedded)
        return pl.pallas_call(
            functools.partial(decode_kernel, first, start, stop),
            out_shape=(emb_shape, wide_shape) if first else emb_shape,
            in_specs=whole(5, pltpu.HBM) if first else whole(4, pltpu.HBM) + whole(2, VMEM),
            out_specs=(pl.BlockSpec(memory_space=VMEM),) * 2 if first else pl.BlockSpec(memory_space=VMEM),
            scratch_shapes=[
                VMEM((2, WIDE * slots, width), jnp.bfloat16),
                SMEM((stop - start, slots), jnp.int32),
                VMEM((stop - start, words, slots), jnp.int32),
                VMEM(block_scales.shape, block_scales.dtype),
                VMEM(block_scales.shape, jnp.float32),
                VMEM((1, 4), bucket_weights.dtype),
                pltpu.SemaphoreType.DMA((8 if first else 4,)),
            ]
            + ([VMEM(centroids.shape, centroids.dtype)] if first else []),
            input_output_aliases={} if first else {5: 0},
            compiler_params=LIMIT,
            cost_estimate=pl.CostEstimate(
                flops=(stop - start) * 2 * 10**8, bytes_accessed=0, transcendentals=0
            ),
            name="decode",
        )(*stored, *extra)

    def find(mine):
        blocks = mine.shape[0]
        padded = -(-blocks // 8) * 8
        return pl.pallas_call(
            functools.partial(slot_kernel, query_count, picks, capacity),
            out_shape=(
                jax.ShapeDtypeStruct((2 * padded, width), jnp.int32),
                jax.ShapeDtypeStruct((blocks * query_count, width), jnp.int32),
            ),
            in_specs=whole(1, VMEM),
            out_specs=(pl.BlockSpec(memory_space=VMEM),) * 2,
            compiler_params=LIMIT,
            cost_estimate=pl.CostEstimate(flops=10**9, bytes_accessed=0, transcendentals=0),
            name="slots",
        )(mine)

    def score(found, mine, other):
        blocks = mine.shape[0]
        padded = -(-blocks // 8) * 8
        lanes = -(-blocks * picks // width) * width
        return pl.pallas_call(
            functools.partial(pair_kernel, query_count, picks, capacity),
            out_shape=jax.ShapeDtypeStruct((query_count, lanes), jnp.float32),
            in_specs=whole(1, pltpu.HBM) + whole(5, VMEM),
            out_specs=pl.BlockSpec(memory_space=VMEM),
            scratch_shapes=[
                SMEM((2 * padded, width), jnp.int32),
                SMEM(lengths.shape, jnp.int32),
                VMEM((padded, width), jnp.float32),
                pltpu.SemaphoreType.DMA((2,)),
            ],
            compiler_params=LIMIT,
            cost_estimate=pl.CostEstimate(flops=3 * 10**9, bytes_accessed=0, transcendentals=0),
            name="pairs",
        )(lengths, *found, mine, other, embedded)[:, : blocks * picks]

    steps = []
    d = shards // 2
    while d >= 1:
        steps.append(d)
        d //= 2
    unit = 2 * WIDE
    cuts = [passages // unit * i // len(steps) * unit for i in range(len(steps) + 1)]
    held = payload[None]
    wide = embedded = None
    for i, d in enumerate(steps):
        moved = swap_shard(held, d)
        if cuts[i] < cuts[i + 1]:
            if embedded is None:
                embedded, wide = decode(cuts[i], cuts[i + 1], None, None)
            else:
                embedded = decode(cuts[i], cuts[i + 1], wide, embedded)
        if d > 1:
            moved, embedded = lax.optimization_barrier((moved, embedded))
            held = jnp.concatenate([held, moved], axis=0)
        else:
            far = moved
    near_scores = score(find(held), held, swap_sub(held))
    far, near_scores = lax.optimization_barrier((far, near_scores))
    far_scores = score(find(far), far, swap_sub(far))
    total = near_scores + swap_shard(far_scores, 1)
    for d in reversed(steps[:-1]):
        half = total.shape[1] // 2
        total = total[:, :half] + swap_shard(total[:, half:], d)
    return total + swap_sub(total)


def solution(mesh):
    return jax.shard_map(
        body,
        mesh=mesh,
        in_specs=(
            P(("groups", "shard"), "sub", None),
            P(("groups", "shard"), None),
            P(("shard", "sub"), None, None),
            P(("shard", "sub"), None),
            P(("shard", "sub"), None),
            P(("shard", "sub")),
            P(),
            P(),
        ),
        out_specs=P(("groups", "shard"), None),
        check_vma=False,
    )
```

time: 62.3 us -> 46.5 us (0.75)
  waiting for transfers between devices: 18 us -> 11 us
  Pallas kernels: 21.8 us -> 17.5 us
  starting transfers between devices: 14.8 us -> 10.7 us
  other arithmetic: 1.38 us -> 0.66 us
    ppermute x6, waiting for transfers between devices: 16.9 us -> 9.03 us  [swap_shard(): return lax.ppermute(x, 'shard', [(i, i ^ d) for i in range(shards)])]
    ppermute x6, starting transfers between devices: 14.2 us -> 10.6 us  [swap_shard(): return lax.ppermute(x, 'shard', [(i, i ^ d) for i in range(shards)])]
    pallas_call x2, Pallas kernels: 8.03 us -> 5.44 us  [score(): pl.pallas_call(functools.partial(pair_kernel, query_count, picks, capacit...]
    pallas_call x1 -> x5, Pallas kernels: 13.6 us -> 11.8 us  [the longest x3 10.3 us: decode(): pl.pallas_call(functools.partial(decode_kernel, first, start, stop), out_...]
    ppermute x3, waiting for transfers between devices: 1.17 us -> 1.98 us  [swap_sub(): return lax.ppermute(x, 'sub', [(i, i ^ 1) for i in range(halves)])]
    convert_element_type x1 -> x0, other arithmetic: 0.72 us -> none  [body(): block_scales.astype(jnp.float32)]
    unnamed x14 -> x16, local copies, waits for them, and re-layouts: 5.87 us -> 5.94 us
  transfers between devices with their start and end apart: 9 -> 9, of which waited for: 6 -> 6; matrix products, arithmetic and copies ran while one was open for 1% -> 0% of each run, Pallas kernels for 35% -> 32%
where the time goes in v2:
time: 46.5 us; the launch traced here: 46.1 us
  Pallas kernels  17.5 us (38%)
  waiting for transfers between devices  11 us (24%)
  starting transfers between devices  10.7 us (23%)
  local copies, waits for them, and re-layouts  6.09 us (13%)
  other arithmetic  0.66 us (1%)
    ppermute x6, starting transfers between devices, swap_shard(): return lax.ppermute(x, 'shard', [(i, i ^ d) for i in range(shards)])  10.6 us
    pallas_call x3, Pallas kernels, decode(): pl.pallas_call(functools.partial(decode_kernel, first, start, stop), out_...  10.3 us
    ppermute x6, waiting for transfers between devices, swap_shard(): return lax.ppermute(x, 'shard', [(i, i ^ d) for i in range(shards)])  9.03 us
    unnamed x16, local copies, waits for them, and re-layouts  5.94 us
    pallas_call x2, Pallas kernels, score(): pl.pallas_call(functools.partial(pair_kernel, query_count, picks, capacit...  5.44 us
    ppermute x3, waiting for transfers between devices, swap_sub(): return lax.ppermute(x, 'sub', [(i, i ^ 1) for i in range(halves)])  1.98 us
    pallas_call x2, Pallas kernels, find(): pl.pallas_call(functools.partial(slot_kernel, query_count, picks, capacit...  1.55 us
  transfers between devices with their start and end apart: 9, of which 6 were waited for; matrix products, arithmetic and copies ran while one was open for 0% of the time, Pallas kernels for 32%

profile of v2, /device:TPU:0, one launch (start us, length us, event | category | flops | bytes accessed | tf_op | source)
XLA Modules:
  0.0 46.1 jit_solution(583775051467832334)
XLA Ops:
  0.0 0.0 copy-start
  0.0 0.8 %copy-done = bf16[16,16,128]{2,1,0:T(8,128)(2,1)S(1)} copy-done((bf16[16,16,128]{2,1,0:T(8,128)(2,1)S(1)}, bf16[16,16,128]{2,1,0:T(8,128)(2,1)}, u32[]{:S(2)}) %copy-start) | copy-done | bytes 65560
  0.8 0.0 copy-start.1
  0.8 0.7 %copy-done.1 = s32[16,16]{1,0:T(8,128)S(1)} copy-done((s32[16,16]{1,0:T(8,128)S(1)}, s32[16,16]{1,0:T(8,128)}, u32[]{:S(2)}) %copy-start.1) | copy-done | bytes 1048
  1.5 0.2 pack.1
  1.8 4.1 %collective-permute-start = (bf16[1,288,128]{2,1,0:T(8,128)(2,1)S(1)}, bf16[1,288,128]{2,1,0:T(8,128)(2,1)S(1)}, u32[]{:S(2)}, u32[]{:S(2)}) collective-permute-start(bf16[1,288,128]{2,1,0:T(8,128)(2,1)S(1)} %bitcast.5), channel_id=1, source_target_pairs={{0,8},{2,10},{4,12},{6,14},{8,0},{10,2},{12,4},{14,6},{1,9},{3,11}... | collective-permute-start | bytes 221192 | tf_op jit(solution)/shard_map/ppermute | solution.py:264
  5.9 0.0 copy-start.2
  5.9 1.2 %copy-done.2 = bf16[4096,128]{1,0:T(8,128)(2,1)S(1)} copy-done((bf16[4096,128]{1,0:T(8,128)(2,1)S(1)}, bf16[4096,128]{1,0:T(8,128)(2,1)}, u32[]{:S(2)}) %copy-start.2) | copy-done | bytes 1048600
  7.1 0.0 copy-start.3
  7.1 1.0 %copy-done.3 = s32[64,128,16]{1,2,0:T(8,128)S(1)} copy-done((s32[64,128,16]{1,2,0:T(8,128)S(1)}, s32[64,128,16]{1,2,0:T(8,128)}, u32[]{:S(2)}) %copy-start.3) | copy-done | bytes 524312
  8.2 0.0 copy-start.4
  8.2 0.8 %copy-done.4 = s32[64,128]{1,0:T(8,128)S(1)} copy-done((s32[64,128]{1,0:T(8,128)S(1)}, s32[64,128]{1,0:T(8,128)}, u32[]{:S(2)}) %copy-start.4) | copy-done | bytes 32792
  8.9 0.0 copy-start.5
  8.9 0.7 %copy-done.5 = bf16[64,128]{1,0:T(8,128)(2,1)S(1)} copy-done((bf16[64,128]{1,0:T(8,128)(2,1)S(1)}, bf16[64,128]{1,0:T(8,128)(2,1)}, u32[]{:S(2)}) %copy-start.5) | copy-done | bytes 16408
  9.6 0.0 copy-start.6
  9.6 0.7 %copy-done.6 = bf16[4]{0:T(256)(128)(2,1)S(1)} copy-done((bf16[4]{0:T(256)(128)(2,1)S(1)}, bf16[4]{0:T(256)(128)(2,1)}, u32[]{:S(2)}) %copy-start.6) | copy-done | bytes 32
  10.3 2.5 %decode.3 = (bf16[64,128,128]{2,1,0:T(8,128)(2,1)S(1)}, f32[4096,128]{1,0:T(8,128)S(1)}) custom-call(s32[64,128]{1,0:T(8,128)S(1)} %copy-done.4, s32[64,16,128]{2,1,0:T(8,128)S(1)} %bitcast.9, bf16[64,128]{1,0:T(8,128)(2,1)S(1)} %copy-done.5, bf16[1,4]{1,0:T(2,128)(2,1)S(1)} %bitcast.13, bf16[4096,128]{1,0:T(8,128)(2,1)S(1)} %copy-done.2), custom_call_target="tpu_custom_call" | custom-call | flops 3200000000 | tf_op jit(solution)/shard_map/decode/pallas_call | solution.py:295
  12.8 0.0 collective-permute-done
  12.8 1.6 %collective-permute-start.1 = (bf16[2,288,128]{2,1,0:T(8,128)(2,1)S(1)}, bf16[2,288,128]{2,1,0:T(8,128)(2,1)S(1)}, u32[]{:S(2)}, u32[]{:S(2)}) collective-permute-start(bf16[2,288,128]{2,1,0:T(8,128)(2,1)S(1)} %pad_maximum_fusion.1), channel_id=1, source_target_pairs={{0,4},{2,6},{4,0},{6,2},{8,12},{10,14},{12,8},{14,10},{1,5},{3,7},... | collective-permute-start | bytes 442376 | tf_op jit(solution)/shard_map/ppermute | solution.py:264
  14.5 3.9 %decode.4.refs_5_ = bf16[64,128,128]{2,1,0:T(8,128)(2,1)S(1)} custom-call(s32[64,128]{1,0:T(8,128)S(1)} %copy-done.4, s32[64,16,128]{2,1,0:T(8,128)S(1)} %bitcast.10, bf16[64,128]{1,0:T(8,128)(2,1)S(1)} %copy-done.5, bf16[1,4]{1,0:T(2,128)(2,1)S(1)} %bitcast.14, f32[4096,128]{1,0:T(8,128)S(1)} %get-tuple-element.19.refs_4_, ...), custom_call_target="tpu_custom_call", output_to_operand_aliasing={{}: (5, {})} | custom-call | flops 4800000000 | tf_op jit(solution)/shard_map/decode/pallas_call | solution.py:295
  18.4 0.0 collective-permute-done.1
  18.4 0.1 collective-permute-start.3
  18.5 1.6 %collective-permute-start.2 = (bf16[4,288,128]{2,1,0:T(8,128)(2,1)S(1)}, bf16[4,288,128]{2,1,0:T(8,128)(2,1)S(1)}, u32[]{:S(2)}, u32[]{:S(2)}) collective-permute-start(bf16[4,288,128]{2,1,0:T(8,128)(2,1)S(1)} %pad_maximum_fusion.rows_ref.mine_ref), channel_id=1, source_target_pairs={{0,2},{2,0},{4,6},{6,4},{8,10},{10,8},{12,14},{14,12},{1,3},{3,1},... | collective-permute-start | bytes 884744 | tf_op jit(solution)/shard_map/ppermute | solution.py:264
  20.1 3.9 %decode.5.emb_ref = bf16[64,128,128]{2,1,0:T(8,128)(2,1)S(1)} custom-call(s32[64,128]{1,0:T(8,128)S(1)} %copy-done.4, s32[64,16,128]{2,1,0:T(8,128)S(1)} %bitcast.11, bf16[64,128]{1,0:T(8,128)(2,1)S(1)} %copy-done.5, bf16[1,4]{1,0:T(2,128)(2,1)S(1)} %bitcast.15, f32[4096,128]{1,0:T(8,128)S(1)} %get-tuple-element.19.refs_4_, ...), custom_call_target="tpu_custom_call", output_to_operand_aliasing={{}: (5, {})} | custom-call | flops 4800000000 | tf_op jit(solution)/shard_map/decode/pallas_call | solution.py:295
  24.0 0.0 copy-start.7
  24.0 0.8 %slots.2 = (s32[16,128]{1,0:T(8,128)S(1)}, s32[64,128]{1,0:T(8,128)S(1)}) custom-call(bf16[4,288,128]{2,1,0:T(8,128)(2,1)S(1)} %pad_maximum_fusion.rows_ref.mine_ref), custom_call_target="tpu_custom_call" | custom-call | flops 1000000000 | tf_op jit(solution)/shard_map/slots/pallas_call | solution.py:321
  24.8 0.0 collective-permute-done.3.other_ref
  24.8 0.0 copy-done.7
  24.8 2.7 %pairs.2 = f32[16,128]{1,0:T(8,128)S(1)} custom-call(s32[64]{0:T(128)S(1)} %copy-done.7, s32[16,128]{1,0:T(8,128)S(1)} %get-tuple-element.22.slot_ref, s32[64,128]{1,0:T(8,128)S(1)} %get-tuple-element.23.rank_ref, bf16[4,288,128]{2,1,0:T(8,128)(2,1)S(1)} %pad_maximum_fusion.rows_ref.mine_ref, bf16[4,288,128]{2,1,0:T(8,128)(2,1)S(1)} %collective-permute-done.3.other_ref, ...), custom_call_target="tpu_custom_call" | custom-call | flops 3000000000 | tf_op jit(solution)/shard_map/pairs/pallas_call | solution.py:338
  27.5 0.4 collective-permute-done.2.rows_ref.mine_ref
  27.9 0.0 collective-permute-start.4
  28.0 0.8 %slots.3 = (s32[16,128]{1,0:T(8,128)S(1)}, s32[64,128]{1,0:T(8,128)S(1)}) custom-call(bf16[4,288,128]{2,1,0:T(8,128)(2,1)S(1)} %collective-permute-done.2.rows_ref.mine_ref), custom_call_target="tpu_custom_call" | custom-call | flops 1000000000 | tf_op jit(solution)/shard_map/slots/pallas_call | solution.py:321
  28.7 0.8 %collective-permute-done.4.other_ref = bf16[4,288,128]{2,1,0:T(8,128)(2,1)S(1)} collective-permute-done((bf16[4,288,128]{2,1,0:T(8,128)(2,1)S(1)}, bf16[4,288,128]{2,1,0:T(8,128)(2,1)S(1)}, u32[]{:S(2)}, u32[]{:S(2)}) %collective-permute-start.4) | collective-permute-done | bytes 294944 | tf_op jit(solution)/shard_map/ppermute | solution.py:267
  29.5 2.7 %pairs.3 = f32[16,128]{1,0:T(8,128)S(1)} custom-call(s32[64]{0:T(128)S(1)} %copy-done.7, s32[16,128]{1,0:T(8,128)S(1)} %get-tuple-element.27.slot_ref, s32[64,128]{1,0:T(8,128)S(1)} %get-tuple-element.28.rank_ref, bf16[4,288,128]{2,1,0:T(8,128)(2,1)S(1)} %collective-permute-done.2.rows_ref.mine_ref, ...), custom_call_target="tpu_custom_call" | custom-call | flops 3000000000 | tf_op jit(solution)/shard_map/pairs/pallas_call | solution.py:338
  32.2 1.6 %collective-permute-start.5 = (f32[16,64]{1,0:T(8,128)S(1)}, f32[16,64]{1,0:T(8,128)S(1)}, u32[]{:S(2)}, u32[]{:S(2)}) collective-permute-start(f32[16,64]{1,0:T(8,128)S(1)} %bitcast.12), channel_id=1, source_target_pairs={{0,2},{2,0},{4,6},{6,4},{8,10},{10,8},{12,14},{14,12},{1,3},{3,1},... | collective-permute-start | bytes 12296 | tf_op jit(solution)/shard_map/ppermute | solution.py:264
  33.8 2.1 %collective-permute-done.5 = f32[16,64]{1,0:T(8,128)S(1)} collective-permute-done((f32[16,64]{1,0:T(8,128)S(1)}, f32[16,64]{1,0:T(8,128)S(1)}, u32[]{:S(2)}, u32[]{:S(2)}) %collective-permute-start.5) | collective-permute-done | bytes 4128 | tf_op jit(solution)/shard_map/ppermute | solution.py:264
  36.0 0.1 slice.27
  36.0 1.4 %collective-permute-start.6 = (f32[16,32]{1,0:T(8,128)S(1)}, f32[16,32]{1,0:T(8,128)S(1)}, u32[]{:S(2)}, u32[]{:S(2)}) collective-permute-start(f32[16,32]{1,0:T(8,128)S(1)} %slice.27), channel_id=1, source_target_pairs={{0,4},{2,6},{4,0},{6,2},{8,12},{10,14},{12,8},{14,10},{1,5},{3,7},... | collective-permute-start | bytes 6152 | tf_op jit(solution)/shard_map/ppermute | solution.py:264
  37.4 2.3 %collective-permute-done.6 = f32[16,32]{1,0:T(8,128)S(1)} collective-permute-done((f32[16,32]{1,0:T(8,128)S(1)}, f32[16,32]{1,0:T(8,128)S(1)}, u32[]{:S(2)}, u32[]{:S(2)}) %collective-permute-start.6) | collective-permute-done | bytes 2080 | tf_op jit(solution)/shard_map/ppermute | solution.py:264
  39.7 0.1 slice.29
  39.8 0.3 collective-permute-start.7
  40.1 4.2 %collective-permute-done.7 = f32[16,16]{1,0:T(8,128)S(1)} collective-permute-done((f32[16,16]{1,0:T(8,128)S(1)}, f32[16,16]{1,0:T(8,128)S(1)}, u32[]{:S(2)}, u32[]{:S(2)}) %collective-permute-start.7) | collective-permute-done | bytes 1056 | tf_op jit(solution)/shard_map/ppermute | solution.py:264
  44.3 0.0 collective-permute-start.8
  44.3 1.2 %collective-permute-done.8 = f32[16,16]{1,0:T(8,128)S(1)} collective-permute-done((f32[16,16]{1,0:T(8,128)S(1)}, f32[16,16]{1,0:T(8,128)S(1)}, u32[]{:S(2)}, u32[]{:S(2)}) %collective-permute-start.8) | collective-permute-done | bytes 1056 | tf_op jit(solution)/shard_map/ppermute | solution.py:267
  45.5 0.6 %add.15 = f32[16,16]{1,0:T(8,128)} add(f32[16,16]{1,0:T(8,128)S(1)} %slice_add_fusion, f32[16,16]{1,0:T(8,128)S(1)} %collective-permute-done.8) | non-fusion elementwise | flops 256 | bytes 3072 | tf_op jit(solution)/shard_map/add | solution.py:382
  (5 shorter events, 0.1 us)
Async XLA Ops:
  0.0 0.8 %copy-start = (bf16[16,16,128]{2,1,0:T(8,128)(2,1)S(1)}, bf16[16,16,128]{2,1,0:T(8,128)(2,1)}, u32[]{:S(2)}) copy-start(bf16[16,16,128]{2,1,0:T(8,128)(2,1)} %query_hbm.1) | copy-start | bytes 196612
  0.8 0.7 %copy-start.1 = (s32[16,16]{1,0:T(8,128)S(1)}, s32[16,16]{1,0:T(8,128)}, u32[]{:S(2)}) copy-start(s32[16,16]{1,0:T(8,128)} %cand_hbm.1) | copy-start | bytes 3076
  1.8 11.0 %collective-permute-start = (bf16[1,288,128]{2,1,0:T(8,128)(2,1)S(1)}, bf16[1,288,128]{2,1,0:T(8,128)(2,1)S(1)}, u32[]{:S(2)}, u32[]{:S(2)}) collective-permute-start(bf16[1,288,128]{2,1,0:T(8,128)(2,1)S(1)} %bitcast.5), channel_id=1, source_target_pairs={{0,8},{2,10},{4,12},{6,14},{8,0},{10,2},{12,4},{14,6},{1,9},{3,11}... | collective-permute-start | bytes 221192 | tf_op jit(solution)/shard_map/ppermute | solution.py:264
  5.9 1.2 %copy-start.2 = (bf16[4096,128]{1,0:T(8,128)(2,1)S(1)}, bf16[4096,128]{1,0:T(8,128)(2,1)}, u32[]{:S(2)}) copy-start(bf16[4096,128]{1,0:T(8,128)(2,1)} %refs_4_.1) | copy-start | bytes 3145732
  7.1 1.0 %copy-start.3 = (s32[64,128,16]{1,2,0:T(8,128)S(1)}, s32[64,128,16]{1,2,0:T(8,128)}, u32[]{:S(2)}) copy-start(s32[64,128,16]{1,2,0:T(8,128)} %param.10) | copy-start | bytes 1572868
  8.2 0.8 %copy-start.4 = (s32[64,128]{1,0:T(8,128)S(1)}, s32[64,128]{1,0:T(8,128)}, u32[]{:S(2)}) copy-start(s32[64,128]{1,0:T(8,128)} %refs_0_.5) | copy-start | bytes 98308
  8.9 0.7 %copy-start.5 = (bf16[64,128]{1,0:T(8,128)(2,1)S(1)}, bf16[64,128]{1,0:T(8,128)(2,1)}, u32[]{:S(2)}) copy-start(bf16[64,128]{1,0:T(8,128)(2,1)} %refs_2_.5) | copy-start | bytes 49156
  9.6 0.7 %copy-start.6 = (bf16[4]{0:T(256)(128)(2,1)S(1)}, bf16[4]{0:T(256)(128)(2,1)}, u32[]{:S(2)}) copy-start(bf16[4]{0:T(256)(128)(2,1)} %param.15) | copy-start | bytes 28
  12.8 5.6 %collective-permute-start.1 = (bf16[2,288,128]{2,1,0:T(8,128)(2,1)S(1)}, bf16[2,288,128]{2,1,0:T(8,128)(2,1)S(1)}, u32[]{:S(2)}, u32[]{:S(2)}) collective-permute-start(bf16[2,288,128]{2,1,0:T(8,128)(2,1)S(1)} %pad_maximum_fusion.1), channel_id=1, source_target_pairs={{0,4},{2,6},{4,0},{6,2},{8,12},{10,14},{12,8},{14,10},{1,5},{3,7},... | collective-permute-start | bytes 442376 | tf_op jit(solution)/shard_map/ppermute | solution.py:264
  18.4 6.4 %collective-permute-start.3 = (bf16[4,288,128]{2,1,0:T(8,128)(2,1)S(1)}, bf16[4,288,128]{2,1,0:T(8,128)(2,1)S(1)}, u32[]{:S(2)}, u32[]{:S(2)}) collective-permute-start(bf16[4,288,128]{2,1,0:T(8,128)(2,1)S(1)} %pad_maximum_fusion.rows_ref.mine_ref), channel_id=1, source_target_pairs={{0,1},{1,0},{2,3},{3,2},{4,5},{5,4},{6,7},{7,6},{8,9},{9,8},{10,11... | collective-permute-start | bytes 884744 | tf_op jit(solution)/shard_map/ppermute | solution.py:267
  18.5 9.4 %collective-permute-start.2 = (bf16[4,288,128]{2,1,0:T(8,128)(2,1)S(1)}, bf16[4,288,128]{2,1,0:T(8,128)(2,1)S(1)}, u32[]{:S(2)}, u32[]{:S(2)}) collective-permute-start(bf16[4,288,128]{2,1,0:T(8,128)(2,1)S(1)} %pad_maximum_fusion.rows_ref.mine_ref), channel_id=1, source_target_pairs={{0,2},{2,0},{4,6},{6,4},{8,10},{10,8},{12,14},{14,12},{1,3},{3,1},... | collective-permute-start | bytes 884744 | tf_op jit(solution)/shard_map/ppermute | solution.py:264
  24.0 0.8 %copy-start.7 = (s32[64]{0:T(128)S(1)}, s32[64]{0:T(128)}, u32[]{:S(2)}) copy-start(s32[64]{0:T(128)} %len_hbm.3) | copy-start | bytes 772
  27.9 1.6 %collective-permute-start.4 = (bf16[4,288,128]{2,1,0:T(8,128)(2,1)S(1)}, bf16[4,288,128]{2,1,0:T(8,128)(2,1)S(1)}, u32[]{:S(2)}, u32[]{:S(2)}) collective-permute-start(bf16[4,288,128]{2,1,0:T(8,128)(2,1)S(1)} %collective-permute-done.2.rows_ref.mine_ref), channel_id=1, source_target_pairs={{0,1},{1,0},{2,3},{3,2},{4,5},{5,4},{6,7},{7,6},{8,9},{9,8},{10,11... | collective-permute-start | bytes 884744 | tf_op jit(solution)/shard_map/ppermute | solution.py:267
  32.2 3.7 %collective-permute-start.5 = (f32[16,64]{1,0:T(8,128)S(1)}, f32[16,64]{1,0:T(8,128)S(1)}, u32[]{:S(2)}, u32[]{:S(2)}) collective-permute-start(f32[16,64]{1,0:T(8,128)S(1)} %bitcast.12), channel_id=1, source_target_pairs={{0,2},{2,0},{4,6},{6,4},{8,10},{10,8},{12,14},{14,12},{1,3},{3,1},... | collective-permute-start | bytes 12296 | tf_op jit(solution)/shard_map/ppermute | solution.py:264
  36.0 3.7 %collective-permute-start.6 = (f32[16,32]{1,0:T(8,128)S(1)}, f32[16,32]{1,0:T(8,128)S(1)}, u32[]{:S(2)}, u32[]{:S(2)}) collective-permute-start(f32[16,32]{1,0:T(8,128)S(1)} %slice.27), channel_id=1, source_target_pairs={{0,4},{2,6},{4,0},{6,2},{8,12},{10,14},{12,8},{14,10},{1,5},{3,7},... | collective-permute-start | bytes 6152 | tf_op jit(solution)/shard_map/ppermute | solution.py:264
  39.8 4.6 %collective-permute-start.7 = (f32[16,16]{1,0:T(8,128)S(1)}, f32[16,16]{1,0:T(8,128)S(1)}, u32[]{:S(2)}, u32[]{:S(2)}) collective-permute-start(f32[16,16]{1,0:T(8,128)S(1)} %slice.29), channel_id=1, source_target_pairs={{0,8},{2,10},{4,12},{6,14},{8,0},{10,2},{12,4},{14,6},{1,9},{3,11}... | collective-permute-start | bytes 3080 | tf_op jit(solution)/shard_map/ppermute | solution.py:264
  44.3 1.2 %collective-permute-start.8 = (f32[16,16]{1,0:T(8,128)S(1)}, f32[16,16]{1,0:T(8,128)S(1)}, u32[]{:S(2)}, u32[]{:S(2)}) collective-permute-start(f32[16,16]{1,0:T(8,128)S(1)} %slice_add_fusion), channel_id=1, source_target_pairs={{0,1},{1,0},{2,3},{3,2},{4,5},{5,4},{6,7},{7,6},{8,9},{9,8},{10,11... | collective-permute-start | bytes 3080 | tf_op jit(solution)/shard_map/ppermute | solution.py:267

commit v3 on v2

--- a/solution.py
+++ b/solution.py
@@ -156,7 +156,8 @@
         return 0
 
     last = stop - start - 2 * WIDE
-    lax.fori_loop(0, last // (2 * WIDE), step, 0)
+    for i in range(last // (2 * WIDE)):
+        step(i, 0)
     build(last, 0, fetch(last + WIDE, 1))
     build(last + WIDE, 1, iter(()))
 
@@ -220,18 +221,28 @@
     tokens = (mine_ref.shape[1] - 2 * queries) // queries
     padded = slot_s.shape[0] // 2
     full_tokens = 2 * tokens
-    lane = iota((full_tokens, width), 1)
+    slots = emb_ref.shape[2]
+    lane = iota((full_tokens, slots), 1)
+    spot = iota((full_tokens, width), 1)
 
     def block(b, _):
         best_all = jnp.zeros((full_tokens, width), jnp.float32)
-        for s in range(capacity):
-            p = slot_s[padded + b, s]
-            r = pl.ds(pl.multiple_of(slot_s[b, s] * tokens, tokens), tokens)
-            rows_q = jnp.concatenate([mine_ref[b, r, :], other_ref[b, r, :]], axis=0)
-            similar = dot(rows_q, emb_ref[p])
-            similar = jnp.where(lane < len_s[p], similar, masked_floor)
-            best = jnp.max(similar, axis=1, keepdims=True)
-            best_all = jnp.where(lane == s, best, best_all)
+        for s in range(0, capacity, 2):
+            asked = []
+            kept = []
+            stored = []
+            for j in range(s, s + 2):
+                p = slot_s[padded + b, j]
+                r = pl.ds(pl.multiple_of(slot_s[b, j] * tokens, tokens), tokens)
+                asked += [mine_ref[b, r, :], other_ref[b, r, :]]
+                stored.append(emb_ref[p])
+                kept.append(len_s[p])
+            both = dot(jnp.concatenate(asked, axis=0), jnp.concatenate(stored, axis=1))
+            for j in range(2):
+                similar = both[j * full_tokens : (j + 1) * full_tokens, j * slots : (j + 1) * slots]
+                similar = jnp.where(lane < kept[j], similar, masked_floor)
+                best = jnp.max(similar, axis=1, keepdims=True)
+                best_all = jnp.where(spot == s + j, best, best_all)
         score[pl.ds(b, 1), :] = jnp.sum(best_all, axis=0, keepdims=True) * (1.0 / full_tokens)
         return 0
 
@@ -277,6 +288,7 @@
             pltpu.SemaphoreType.DMA((2,)),
         ],
         compiler_params=LIMIT,
+        cost_estimate=pl.CostEstimate(flops=6 * 10**9, bytes_accessed=0, transcendentals=0),
         name="pack",
     )(queries, candidates)
 
@@ -290,9 +302,11 @@
     wide_shape = jax.ShapeDtypeStruct(centroids.shape, jnp.float32)
 
     def decode(start, stop, wide, embedded):
+        if start == stop:
+            return embedded, wide
         first = embedded is None
         extra = (centroids,) if first else (wide, embedded)
-        return pl.pallas_call(
+        out = pl.pallas_call(
             functools.partial(decode_kernel, first, start, stop),
             out_shape=(emb_shape, wide_shape) if first else emb_shape,
             in_specs=whole(5, pltpu.HBM) if first else whole(4, pltpu.HBM) + whole(2, VMEM),
@@ -314,6 +328,7 @@
             ),
             name="decode",
         )(*stored, *extra)
+        return out if first else (out, wide)
 
     def find(mine):
         blocks = mine.shape[0]
@@ -357,23 +372,26 @@
         steps.append(d)
         d //= 2
     unit = 2 * WIDE
-    cuts = [passages // unit * i // len(steps) * unit for i in range(len(steps) + 1)]
+    units = passages // unit
+    parts = len(steps)
+    cuts = [-(-units * i // parts) * unit for i in range(parts + 1)]
     held = payload[None]
     wide = embedded = None
-    for i, d in enumerate(steps):
+    for i, d in enumerate(steps[:-2]):
         moved = swap_shard(held, d)
-        if cuts[i] < cuts[i + 1]:
-            if embedded is None:
-                embedded, wide = decode(cuts[i], cuts[i + 1], None, None)
-            else:
-                embedded = decode(cuts[i], cuts[i + 1], wide, embedded)
-        if d > 1:
-            moved, embedded = lax.optimization_barrier((moved, embedded))
-            held = jnp.concatenate([held, moved], axis=0)
-        else:
-            far = moved
-    near_scores = score(find(held), held, swap_sub(held))
-    far, near_scores = lax.optimization_barrier((far, near_scores))
+        embedded, wide = decode(cuts[i], cuts[i + 1], wide, embedded)
+        moved, embedded = lax.optimization_barrier((moved, embedded))
+        held = jnp.concatenate([held, moved], axis=0)
+    moved = swap_shard(held, steps[-2])
+    far_a = swap_shard(held, 1)
+    embedded, wide = decode(cuts[-3], cuts[-2], wide, embedded)
+    moved, embedded = lax.optimization_barrier((moved, embedded))
+    far_b = swap_shard(moved, 1)
+    embedded, wide = decode(cuts[-2], cuts[-1], wide, embedded)
+    near = jnp.concatenate([held, moved], axis=0)
+    near_scores = score(find(near), near, swap_sub(near))
+    far_b, near_scores = lax.optimization_barrier((far_b, near_scores))
+    far = jnp.concatenate([far_a, far_b], axis=0)
     far_scores = score(find(far), far, swap_sub(far))
     total = near_scores + swap_shard(far_scores, 1)
     for d in reversed(steps[:-1]):

time: 46.5 us -> 41.3 us (0.89)
  local copies, waits for them, and re-layouts: 6.09 us -> 1.87 us
  starting transfers between devices: 10.7 us -> 13 us
  Pallas kernels: 17.5 us -> 15.7 us
  waiting for transfers between devices: 11 us -> 9.79 us
    unnamed x16 -> x17, local copies, waits for them, and re-layouts: 5.94 us -> 1.7 us
    ppermute x6 -> x7, starting transfers between devices: 10.6 us -> 12.4 us  [swap_shard(): return lax.ppermute(x, 'shard', [(i, i ^ d) for i in range(shards)])]
    pallas_call x3, Pallas kernels: 10.3 us -> 9.03 us  [decode(): pl.pallas_call(functools.partial(decode_kernel, first, start, stop), out_...]
    ppermute x6 -> x7, waiting for transfers between devices: 9.03 us -> 8.18 us  [swap_shard(): return lax.ppermute(x, 'shard', [(i, i ^ d) for i in range(shards)])]
    pallas_call x2, Pallas kernels: 5.44 us -> 4.82 us  [score(): pl.pallas_call(functools.partial(pair_kernel, query_count, picks, capacit...]
    ppermute x3, starting transfers between devices: 0.08 us -> 0.57 us  [swap_sub(): return lax.ppermute(x, 'sub', [(i, i ^ 1) for i in range(halves)])]
  transfers between devices with their start and end apart: 9 -> 10, of which waited for: 6 -> 7; matrix products, arithmetic and copies ran while one was open for 0% -> 0% of each run, Pallas kernels for 32% -> 32%
where the time goes in v3:
time: 41.3 us; the launch traced here: 41.1 us
  Pallas kernels  15.7 us (38%)
  starting transfers between devices  13 us (31%)
  waiting for transfers between devices  9.79 us (24%)
  local copies, waits for them, and re-layouts  1.87 us (5%)
  other arithmetic  0.66 us (2%)
    ppermute x7, starting transfers between devices, swap_shard(): return lax.ppermute(x, 'shard', [(i, i ^ d) for i in range(shards)])  12.4 us
    pallas_call x3, Pallas kernels, decode(): pl.pallas_call(functools.partial(decode_kernel, first, start, stop), out_...  9.03 us
    ppermute x7, waiting for transfers between devices, swap_shard(): return lax.ppermute(x, 'shard', [(i, i ^ d) for i in range(shards)])  8.18 us
    pallas_call x2, Pallas kernels, score(): pl.pallas_call(functools.partial(pair_kernel, query_count, picks, capacit...  4.82 us
    unnamed x17, local copies, waits for them, and re-layouts  1.7 us
    ppermute x3, waiting for transfers between devices, swap_sub(): return lax.ppermute(x, 'sub', [(i, i ^ 1) for i in range(halves)])  1.61 us
    pallas_call x2, Pallas kernels, find(): pl.pallas_call(functools.partial(slot_kernel, query_count, picks, capacit...  1.55 us
  transfers between devices with their start and end apart: 10, of which 7 were waited for; matrix products, arithmetic and copies ran while one was open for 0% of the time, Pallas kernels for 32%

profile of v3, /device:TPU:0, one launch (start us, length us, event | category | flops | bytes accessed | tf_op | source)
XLA Modules:
  0.0 41.1 jit_solution(8796235693311255973)
XLA Ops:
  0.0 0.0 copy-start
  0.0 0.0 copy-start.1
  0.0 0.0 copy-start.2
  0.0 1.0 %copy-done.2 = bf16[16,16,128]{2,1,0:T(8,128)(2,1)S(1)} copy-done((bf16[16,16,128]{2,1,0:T(8,128)(2,1)S(1)}, bf16[16,16,128]{2,1,0:T(8,128)(2,1)}, u32[]{:S(2)}) %copy-start.2) | copy-done | bytes 65560
  1.0 0.0 copy-start.5
  1.0 0.7 %copy-done.5 = s32[16,16]{1,0:T(8,128)S(1)} copy-done((s32[16,16]{1,0:T(8,128)S(1)}, s32[16,16]{1,0:T(8,128)}, u32[]{:S(2)}) %copy-start.5) | copy-done | bytes 1048
  1.7 0.0 copy-start.3
  1.7 0.0 copy-start.4
  1.7 0.0 copy-start.6
  1.7 0.3 pack.1
  2.0 4.1 %collective-permute-start = (bf16[1,288,128]{2,1,0:T(8,128)(2,1)S(1)}, bf16[1,288,128]{2,1,0:T(8,128)(2,1)S(1)}, u32[]{:S(2)}, u32[]{:S(2)}) collective-permute-start(bf16[1,288,128]{2,1,0:T(8,128)(2,1)S(1)} %bitcast.5), channel_id=1, source_target_pairs={{0,8},{2,10},{4,12},{6,14},{8,0},{10,2},{12,4},{14,6},{1,9},{3,11}... | collective-permute-start | bytes 221192 | tf_op jit(solution)/shard_map/ppermute | solution.py:275
  6.0 0.0 copy-done
  6.1 0.0 copy-done.1
  6.1 0.0 copy-done.3
  6.1 0.0 copy-done.4
  6.1 0.0 copy-done.6
  6.1 3.4 %decode.3 = (bf16[64,128,128]{2,1,0:T(8,128)(2,1)S(1)}, f32[4096,128]{1,0:T(8,128)S(1)}) custom-call(s32[64,128]{1,0:T(8,128)S(1)} %copy-done.3, s32[64,16,128]{2,1,0:T(8,128)S(1)} %bitcast.9, bf16[64,128]{1,0:T(8,128)(2,1)S(1)} %copy-done.4, bf16[1,4]{1,0:T(2,128)(2,1)S(1)} %bitcast.13, bf16[4096,128]{1,0:T(8,128)(2,1)S(1)} %copy-done), custom_call_target="tpu_custom_call" | custom-call | flops 4800000000 | tf_op jit(solution)/shard_map/decode/pallas_call | solution.py:309
  9.5 0.5 %collective-permute-done = bf16[1,288,128]{2,1,0:T(8,128)(2,1)S(1)} collective-permute-done((bf16[1,288,128]{2,1,0:T(8,128)(2,1)S(1)}, bf16[1,288,128]{2,1,0:T(8,128)(2,1)S(1)}, u32[]{:S(2)}, u32[]{:S(2)}) %collective-permute-start) | collective-permute-done | bytes 73760 | tf_op jit(solution)/shard_map/ppermute | solution.py:275
  10.0 1.8 %collective-permute-start.4 = (bf16[2,288,128]{2,1,0:T(8,128)(2,1)S(1)}, bf16[2,288,128]{2,1,0:T(8,128)(2,1)S(1)}, u32[]{:S(2)}, u32[]{:S(2)}) collective-permute-start(bf16[2,288,128]{2,1,0:T(8,128)(2,1)S(1)} %pad_maximum_fusion.1), channel_id=1, source_target_pairs={{0,2},{2,0},{4,6},{6,4},{8,10},{10,8},{12,14},{14,12},{1,3},{3,1},... | collective-permute-start | bytes 442376 | tf_op jit(solution)/shard_map/ppermute | solution.py:275
  11.8 0.9 %collective-permute-start.1 = (bf16[2,288,128]{2,1,0:T(8,128)(2,1)S(1)}, bf16[2,288,128]{2,1,0:T(8,128)(2,1)S(1)}, u32[]{:S(2)}, u32[]{:S(2)}) collective-permute-start(bf16[2,288,128]{2,1,0:T(8,128)(2,1)S(1)} %pad_maximum_fusion.1), channel_id=1, source_target_pairs={{0,4},{2,6},{4,0},{6,2},{8,12},{10,14},{12,8},{14,10},{1,5},{3,7},... | collective-permute-start | bytes 442376 | tf_op jit(solution)/shard_map/ppermute | solution.py:275
  12.6 3.3 %decode.4.refs_5_ = bf16[64,128,128]{2,1,0:T(8,128)(2,1)S(1)} custom-call(s32[64,128]{1,0:T(8,128)S(1)} %copy-done.3, s32[64,16,128]{2,1,0:T(8,128)S(1)} %bitcast.10, bf16[64,128]{1,0:T(8,128)(2,1)S(1)} %copy-done.4, bf16[1,4]{1,0:T(2,128)(2,1)S(1)} %bitcast.14, f32[4096,128]{1,0:T(8,128)S(1)} %get-tuple-element.19.refs_4_, ...), custom_call_target="tpu_custom_call", output_to_operand_aliasing={{}: (5, {})} | custom-call | flops 4800000000 | tf_op jit(solution)/shard_map/decode/pallas_call | solution.py:309
  15.9 1.0 %collective-permute-done.1 = bf16[2,288,128]{2,1,0:T(8,128)(2,1)S(1)} collective-permute-done((bf16[2,288,128]{2,1,0:T(8,128)(2,1)S(1)}, bf16[2,288,128]{2,1,0:T(8,128)(2,1)S(1)}, u32[]{:S(2)}, u32[]{:S(2)}) %collective-permute-start.1) | collective-permute-done | bytes 147488 | tf_op jit(solution)/shard_map/ppermute | solution.py:275
  17.0 0.4 collective-permute-start.2
  17.3 0.0 collective-permute-start.3
  17.3 0.8 %slots.2 = (s32[16,128]{1,0:T(8,128)S(1)}, s32[64,128]{1,0:T(8,128)S(1)}) custom-call(bf16[4,288,128]{2,1,0:T(8,128)(2,1)S(1)} %pad_maximum_fusion.rows_ref.mine_ref), custom_call_target="tpu_custom_call" | custom-call | flops 1000000000 | tf_op jit(solution)/shard_map/slots/pallas_call | solution.py:336
  18.1 0.0 collective-permute-done.4
  18.1 0.0 copy-start.7
  18.1 2.4 %decode.5.emb_ref = bf16[64,128,128]{2,1,0:T(8,128)(2,1)S(1)} custom-call(s32[64,128]{1,0:T(8,128)S(1)} %copy-done.3, s32[64,16,128]{2,1,0:T(8,128)S(1)} %bitcast.11, bf16[64,128]{1,0:T(8,128)(2,1)S(1)} %copy-done.4, bf16[1,4]{1,0:T(2,128)(2,1)S(1)} %bitcast.15, f32[4096,128]{1,0:T(8,128)S(1)} %get-tuple-element.19.refs_4_, ...), custom_call_target="tpu_custom_call", output_to_operand_aliasing={{}: (5, {})} | custom-call | flops 3200000000 | tf_op jit(solution)/shard_map/decode/pallas_call | solution.py:309
  20.5 0.0 collective-permute-done.3.other_ref
  20.6 0.0 copy-done.7
  20.6 2.4 %pairs.2 = f32[16,128]{1,0:T(8,128)S(1)} custom-call(s32[64]{0:T(128)S(1)} %copy-done.7, s32[16,128]{1,0:T(8,128)S(1)} %get-tuple-element.22.slot_ref, s32[64,128]{1,0:T(8,128)S(1)} %get-tuple-element.23.rank_ref, bf16[4,288,128]{2,1,0:T(8,128)(2,1)S(1)} %pad_maximum_fusion.rows_ref.mine_ref, bf16[4,288,128]{2,1,0:T(8,128)(2,1)S(1)} %collective-permute-done.3.other_ref, ...), custom_call_target="tpu_custom_call" | custom-call | flops 3000000000 | tf_op jit(solution)/shard_map/pairs/pallas_call | solution.py:353
  23.0 0.0 collective-permute-done.2
  23.0 0.6 %collective-permute-start.5 = (bf16[4,288,128]{2,1,0:T(8,128)(2,1)S(1)}, bf16[4,288,128]{2,1,0:T(8,128)(2,1)S(1)}, u32[]{:S(2)}, u32[]{:S(2)}) collective-permute-start(bf16[4,288,128]{2,1,0:T(8,128)(2,1)S(1)} %constant_dynamic-update-slice_fusion.rows_ref.mine_ref), channel_id=1, source_target_pairs={{0,1},{1,0},{2,3},{3,2},{4,5},{5,4},{6,7},{7,6},{8,9},{9,8},{10,11... | collective-permute-start | bytes 884744 | tf_op jit(solution)/shard_map/ppermute | solution.py:278
  23.6 0.8 %slots.3 = (s32[16,128]{1,0:T(8,128)S(1)}, s32[64,128]{1,0:T(8,128)S(1)}) custom-call(bf16[4,288,128]{2,1,0:T(8,128)(2,1)S(1)} %constant_dynamic-update-slice_fusion.rows_ref.mine_ref), custom_call_target="tpu_custom_call" | custom-call | flops 1000000000 | tf_op jit(solution)/shard_map/slots/pallas_call | solution.py:336
  24.4 0.4 %collective-permute-done.5.other_ref = bf16[4,288,128]{2,1,0:T(8,128)(2,1)S(1)} collective-permute-done((bf16[4,288,128]{2,1,0:T(8,128)(2,1)S(1)}, bf16[4,288,128]{2,1,0:T(8,128)(2,1)S(1)}, u32[]{:S(2)}, u32[]{:S(2)}) %collective-permute-start.5) | collective-permute-done | bytes 294944 | tf_op jit(solution)/shard_map/ppermute | solution.py:278
  24.8 2.4 %pairs.3 = f32[16,128]{1,0:T(8,128)S(1)} custom-call(s32[64]{0:T(128)S(1)} %copy-done.7, s32[16,128]{1,0:T(8,128)S(1)} %get-tuple-element.27.slot_ref, s32[64,128]{1,0:T(8,128)S(1)} %get-tuple-element.28.rank_ref, bf16[4,288,128]{2,1,0:T(8,128)(2,1)S(1)} %constant_dynamic-update-slice_fusion.rows_ref.mine_ref, ...), custom_call_target="tpu_custom_call" | custom-call | flops 3000000000 | tf_op jit(solution)/shard_map/pairs/pallas_call | solution.py:353
  27.2 1.8 %collective-permute-start.6 = (f32[16,64]{1,0:T(8,128)S(1)}, f32[16,64]{1,0:T(8,128)S(1)}, u32[]{:S(2)}, u32[]{:S(2)}) collective-permute-start(f32[16,64]{1,0:T(8,128)S(1)} %bitcast.12), channel_id=1, source_target_pairs={{0,2},{2,0},{4,6},{6,4},{8,10},{10,8},{12,14},{14,12},{1,3},{3,1},... | collective-permute-start | bytes 12296 | tf_op jit(solution)/shard_map/ppermute | solution.py:275
  29.0 1.9 %collective-permute-done.6 = f32[16,64]{1,0:T(8,128)S(1)} collective-permute-done((f32[16,64]{1,0:T(8,128)S(1)}, f32[16,64]{1,0:T(8,128)S(1)}, u32[]{:S(2)}, u32[]{:S(2)}) %collective-permute-start.6) | collective-permute-done | bytes 4128 | tf_op jit(solution)/shard_map/ppermute | solution.py:275
  30.9 0.1 slice.27
  31.0 1.1 %collective-permute-start.7 = (f32[16,32]{1,0:T(8,128)S(1)}, f32[16,32]{1,0:T(8,128)S(1)}, u32[]{:S(2)}, u32[]{:S(2)}) collective-permute-start(f32[16,32]{1,0:T(8,128)S(1)} %slice.27), channel_id=1, source_target_pairs={{0,4},{2,6},{4,0},{6,2},{8,12},{10,14},{12,8},{14,10},{1,5},{3,7},... | collective-permute-start | bytes 6152 | tf_op jit(solution)/shard_map/ppermute | solution.py:275
  32.1 2.6 %collective-permute-done.7 = f32[16,32]{1,0:T(8,128)S(1)} collective-permute-done((f32[16,32]{1,0:T(8,128)S(1)}, f32[16,32]{1,0:T(8,128)S(1)}, u32[]{:S(2)}, u32[]{:S(2)}) %collective-permute-start.7) | collective-permute-done | bytes 2080 | tf_op jit(solution)/shard_map/ppermute | solution.py:275
  34.7 0.1 slice.29
  34.8 2.4 %collective-permute-start.8 = (f32[16,16]{1,0:T(8,128)S(1)}, f32[16,16]{1,0:T(8,128)S(1)}, u32[]{:S(2)}, u32[]{:S(2)}) collective-permute-start(f32[16,16]{1,0:T(8,128)S(1)} %slice.29), channel_id=1, source_target_pairs={{0,8},{2,10},{4,12},{6,14},{8,0},{10,2},{12,4},{14,6},{1,9},{3,11}... | collective-permute-start | bytes 3080 | tf_op jit(solution)/shard_map/ppermute | solution.py:275
  37.2 2.2 %collective-permute-done.8 = f32[16,16]{1,0:T(8,128)S(1)} collective-permute-done((f32[16,16]{1,0:T(8,128)S(1)}, f32[16,16]{1,0:T(8,128)S(1)}, u32[]{:S(2)}, u32[]{:S(2)}) %collective-permute-start.8) | collective-permute-done | bytes 1056 | tf_op jit(solution)/shard_map/ppermute | solution.py:275
  39.3 0.0 collective-permute-start.9
  39.3 1.2 %collective-permute-done.9 = f32[16,16]{1,0:T(8,128)S(1)} collective-permute-done((f32[16,16]{1,0:T(8,128)S(1)}, f32[16,16]{1,0:T(8,128)S(1)}, u32[]{:S(2)}, u32[]{:S(2)}) %collective-permute-start.9) | collective-permute-done | bytes 1056 | tf_op jit(solution)/shard_map/ppermute | solution.py:278
  40.5 0.6 %add.15 = f32[16,16]{1,0:T(8,128)} add(f32[16,16]{1,0:T(8,128)S(1)} %slice_add_fusion, f32[16,16]{1,0:T(8,128)S(1)} %collective-permute-done.9) | non-fusion elementwise | flops 256 | bytes 3072 | tf_op jit(solution)/shard_map/add | solution.py:400
  (7 shorter events, 0.1 us)
Async XLA Ops:
  0.0 6.1 %copy-start = (bf16[4096,128]{1,0:T(8,128)(2,1)S(1)}, bf16[4096,128]{1,0:T(8,128)(2,1)}, u32[]{:S(2)}) copy-start(bf16[4096,128]{1,0:T(8,128)(2,1)} %refs_4_.1) | copy-start | bytes 3145732
  0.0 6.1 %copy-start.1 = (s32[64,128,16]{1,2,0:T(8,128)S(1)}, s32[64,128,16]{1,2,0:T(8,128)}, u32[]{:S(2)}) copy-start(s32[64,128,16]{1,2,0:T(8,128)} %param.10) | copy-start | bytes 1572868
  0.0 1.0 %copy-start.2 = (bf16[16,16,128]{2,1,0:T(8,128)(2,1)S(1)}, bf16[16,16,128]{2,1,0:T(8,128)(2,1)}, u32[]{:S(2)}) copy-start(bf16[16,16,128]{2,1,0:T(8,128)(2,1)} %query_hbm.1) | copy-start | bytes 196612
  1.0 0.7 %copy-start.5 = (s32[16,16]{1,0:T(8,128)S(1)}, s32[16,16]{1,0:T(8,128)}, u32[]{:S(2)}) copy-start(s32[16,16]{1,0:T(8,128)} %cand_hbm.1) | copy-start | bytes 3076
  1.7 4.4 %copy-start.3 = (s32[64,128]{1,0:T(8,128)S(1)}, s32[64,128]{1,0:T(8,128)}, u32[]{:S(2)}) copy-start(s32[64,128]{1,0:T(8,128)} %refs_0_.5) | copy-start | bytes 98308
  1.7 4.4 %copy-start.4 = (bf16[64,128]{1,0:T(8,128)(2,1)S(1)}, bf16[64,128]{1,0:T(8,128)(2,1)}, u32[]{:S(2)}) copy-start(bf16[64,128]{1,0:T(8,128)(2,1)} %refs_2_.5) | copy-start | bytes 49156
  1.7 4.4 %copy-start.6 = (bf16[4]{0:T(256)(128)(2,1)S(1)}, bf16[4]{0:T(256)(128)(2,1)}, u32[]{:S(2)}) copy-start(bf16[4]{0:T(256)(128)(2,1)} %param.15) | copy-start | bytes 28
  2.0 8.0 %collective-permute-start = (bf16[1,288,128]{2,1,0:T(8,128)(2,1)S(1)}, bf16[1,288,128]{2,1,0:T(8,128)(2,1)S(1)}, u32[]{:S(2)}, u32[]{:S(2)}) collective-permute-start(bf16[1,288,128]{2,1,0:T(8,128)(2,1)S(1)} %bitcast.5), channel_id=1, source_target_pairs={{0,8},{2,10},{4,12},{6,14},{8,0},{10,2},{12,4},{14,6},{1,9},{3,11}... | collective-permute-start | bytes 221192 | tf_op jit(solution)/shard_map/ppermute | solution.py:275
  10.0 8.1 %collective-permute-start.4 = (bf16[2,288,128]{2,1,0:T(8,128)(2,1)S(1)}, bf16[2,288,128]{2,1,0:T(8,128)(2,1)S(1)}, u32[]{:S(2)}, u32[]{:S(2)}) collective-permute-start(bf16[2,288,128]{2,1,0:T(8,128)(2,1)S(1)} %pad_maximum_fusion.1), channel_id=1, source_target_pairs={{0,2},{2,0},{4,6},{6,4},{8,10},{10,8},{12,14},{14,12},{1,3},{3,1},... | collective-permute-start | bytes 442376 | tf_op jit(solution)/shard_map/ppermute | solution.py:275
  11.8 5.1 %collective-permute-start.1 = (bf16[2,288,128]{2,1,0:T(8,128)(2,1)S(1)}, bf16[2,288,128]{2,1,0:T(8,128)(2,1)S(1)}, u32[]{:S(2)}, u32[]{:S(2)}) collective-permute-start(bf16[2,288,128]{2,1,0:T(8,128)(2,1)S(1)} %pad_maximum_fusion.1), channel_id=1, source_target_pairs={{0,4},{2,6},{4,0},{6,2},{8,12},{10,14},{12,8},{14,10},{1,5},{3,7},... | collective-permute-start | bytes 442376 | tf_op jit(solution)/shard_map/ppermute | solution.py:275
  17.0 6.0 %collective-permute-start.2 = (bf16[2,288,128]{2,1,0:T(8,128)(2,1)S(1)}, bf16[2,288,128]{2,1,0:T(8,128)(2,1)S(1)}, u32[]{:S(2)}, u32[]{:S(2)}) collective-permute-start(bf16[2,288,128]{2,1,0:T(8,128)(2,1)S(1)} %collective-permute-done.1), channel_id=1, source_target_pairs={{0,2},{2,0},{4,6},{6,4},{8,10},{10,8},{12,14},{14,12},{1,3},{3,1},... | collective-permute-start | bytes 442376 | tf_op jit(solution)/shard_map/ppermute | solution.py:275
  17.3 3.2 %collective-permute-start.3 = (bf16[4,288,128]{2,1,0:T(8,128)(2,1)S(1)}, bf16[4,288,128]{2,1,0:T(8,128)(2,1)S(1)}, u32[]{:S(2)}, u32[]{:S(2)}) collective-permute-start(bf16[4,288,128]{2,1,0:T(8,128)(2,1)S(1)} %pad_maximum_fusion.rows_ref.mine_ref), channel_id=1, source_target_pairs={{0,1},{1,0},{2,3},{3,2},{4,5},{5,4},{6,7},{7,6},{8,9},{9,8},{10,11... | collective-permute-start | bytes 884744 | tf_op jit(solution)/shard_map/ppermute | solution.py:278
  18.1 2.4 %copy-start.7 = (s32[64]{0:T(128)S(1)}, s32[64]{0:T(128)}, u32[]{:S(2)}) copy-start(s32[64]{0:T(128)} %len_hbm.3) | copy-start | bytes 772
  23.0 1.8 %collective-permute-start.5 = (bf16[4,288,128]{2,1,0:T(8,128)(2,1)S(1)}, bf16[4,288,128]{2,1,0:T(8,128)(2,1)S(1)}, u32[]{:S(2)}, u32[]{:S(2)}) collective-permute-start(bf16[4,288,128]{2,1,0:T(8,128)(2,1)S(1)} %constant_dynamic-update-slice_fusion.rows_ref.mine_ref), channel_id=1, source_target_pairs={{0,1},{1,0},{2,3},{3,2},{4,5},{5,4},{6,7},{7,6},{8,9},{9,8},{10,11... | collective-permute-start | bytes 884744 | tf_op jit(solution)/shard_map/ppermute | solution.py:278
  27.2 3.7 %collective-permute-start.6 = (f32[16,64]{1,0:T(8,128)S(1)}, f32[16,64]{1,0:T(8,128)S(1)}, u32[]{:S(2)}, u32[]{:S(2)}) collective-permute-start(f32[16,64]{1,0:T(8,128)S(1)} %bitcast.12), channel_id=1, source_target_pairs={{0,2},{2,0},{4,6},{6,4},{8,10},{10,8},{12,14},{14,12},{1,3},{3,1},... | collective-permute-start | bytes 12296 | tf_op jit(solution)/shard_map/ppermute | solution.py:275
  31.0 3.7 %collective-permute-start.7 = (f32[16,32]{1,0:T(8,128)S(1)}, f32[16,32]{1,0:T(8,128)S(1)}, u32[]{:S(2)}, u32[]{:S(2)}) collective-permute-start(f32[16,32]{1,0:T(8,128)S(1)} %slice.27), channel_id=1, source_target_pairs={{0,4},{2,6},{4,0},{6,2},{8,12},{10,14},{12,8},{14,10},{1,5},{3,7},... | collective-permute-start | bytes 6152 | tf_op jit(solution)/shard_map/ppermute | solution.py:275
  34.8 4.6 %collective-permute-start.8 = (f32[16,16]{1,0:T(8,128)S(1)}, f32[16,16]{1,0:T(8,128)S(1)}, u32[]{:S(2)}, u32[]{:S(2)}) collective-permute-start(f32[16,16]{1,0:T(8,128)S(1)} %slice.29), channel_id=1, source_target_pairs={{0,8},{2,10},{4,12},{6,14},{8,0},{10,2},{12,4},{14,6},{1,9},{3,11}... | collective-permute-start | bytes 3080 | tf_op jit(solution)/shard_map/ppermute | solution.py:275
  39.3 1.2 %collective-permute-start.9 = (f32[16,16]{1,0:T(8,128)S(1)}, f32[16,16]{1,0:T(8,128)S(1)}, u32[]{:S(2)}, u32[]{:S(2)}) collective-permute-start(f32[16,16]{1,0:T(8,128)S(1)} %slice_add_fusion), channel_id=1, source_target_pairs={{0,1},{1,0},{2,3},{3,2},{4,5},{5,4},{6,7},{7,6},{8,9},{9,8},{10,11... | collective-permute-start | bytes 3080 | tf_op jit(solution)/shard_map/ppermute | solution.py:278

commit v4 on v3

--- a/solution.py
+++ b/solution.py
@@ -1,4 +1,5 @@
 import functools
+import math
 
 import jax
 import jax.numpy as jnp
@@ -8,6 +9,7 @@
 from jax.sharding import PartitionSpec as P
 
 masked_floor = -1000000000.0
+UNROLLED = 128
 VMEM = pltpu.VMEM
 SMEM = pltpu.SMEM
 LIMIT = pltpu.CompilerParams(vmem_limit_bytes=40 * 2**20)
@@ -52,114 +54,6 @@
     for i, part in enumerate((owner, local)):
         part = part.astype(jnp.float32).astype(jnp.bfloat16)
         out_ref[rows + i * count : rows + (i + 1) * count, :] = dot(part, repeat).astype(jnp.bfloat16)
-
-
-WIDE = 4
-
-
-def decode_kernel(first, start, stop, *refs):
-    if first:
-        ids_hbm, words_hbm, scale_hbm, bucket_hbm, table_hbm, out_ref, wide = refs[:7]
-        rest = refs[7:]
-    else:
-        ids_hbm, words_hbm, scale_hbm, bucket_hbm, wide, _, out_ref = refs[:7]
-        rest = refs[7:]
-    rows, ids_ref, words_ref, scale_bf, scale_ref, bucket_ref, sems = rest[:7]
-    mine = pl.ds(start, stop - start)
-    copies = [
-        pltpu.make_async_copy(ids_hbm.at[mine], ids_ref, sems.at[0]),
-        pltpu.make_async_copy(words_hbm.at[mine], words_ref, sems.at[1]),
-        pltpu.make_async_copy(scale_hbm, scale_bf, sems.at[2]),
-        pltpu.make_async_copy(bucket_hbm, bucket_ref, sems.at[3]),
-    ]
-    if first:
-        table_ref = rest[7]
-        parts = 4
-        size = table_ref.shape[0] // parts
-        loads = [
-            pltpu.make_async_copy(
-                table_hbm.at[pl.ds(i * size, size)], table_ref.at[pl.ds(i * size, size)], sems.at[4 + i]
-            )
-            for i in range(parts)
-        ]
-        for c in loads + copies:
-            c.start()
-        chunk = 256
-        for i in range(parts):
-            loads[i].wait()
-
-            def widen(j, _):
-                r = pl.ds(pl.multiple_of(i * size + j * chunk, chunk), chunk)
-                wide[r, :] = table_ref[r, :].astype(jnp.float32)
-                return 0
-
-            lax.fori_loop(0, size // chunk, widen, 0)
-    else:
-        for c in copies:
-            c.start()
-    for c in copies:
-        c.wait()
-    scale_ref[...] = scale_bf[...].astype(jnp.float32)
-    slots = ids_ref.shape[1]
-    width = wide.shape[1]
-    words = words_ref.shape[1]
-    per = width // words
-    order = ones_where(iota((width, width), 1) == spread(iota((width, width), 0), words, per))
-    levels = [
-        jnp.broadcast_to(bucket_ref[0:1, i : i + 1].astype(jnp.float32), (words, slots * WIDE))
-        for i in range(4)
-    ]
-
-    def fetch(p, buf):
-        for u in range(WIDE):
-            for g in range(slots // 16):
-                got = jnp.concatenate(
-                    [wide[pl.ds(ids_ref[p + u, g * 16 + i], 1), :] for i in range(16)], axis=0
-                )
-                r = u * slots + g * 16
-                rows[buf, r : r + 16, :] = got.astype(jnp.bfloat16)
-                yield
-
-    def build(p, buf, fetching):
-        packed = jnp.concatenate([words_ref[p + u] for u in range(WIDE)], axis=1)
-        centre = dot(order, rows[buf], ((1,), (1,)))
-        parts = []
-        for k in range(per):
-            for _ in range(WIDE):
-                next(fetching, None)
-            low = (packed & (1 << (2 * k))) != 0
-            high = (packed & (2 << (2 * k))) != 0
-            parts.append(
-                jnp.where(
-                    high,
-                    jnp.where(low, levels[3], levels[2]),
-                    jnp.where(low, levels[1], levels[0]),
-                )
-            )
-        value = jnp.concatenate(parts, axis=0)
-        scale = jnp.concatenate([scale_ref[pl.ds(start + p + u, 1), :] for u in range(WIDE)], axis=1)
-        raw = centre + scale * value
-        inverse = lax.rsqrt(jnp.sum(raw * raw, axis=0, keepdims=True) + 1e-06)
-        out = (raw * inverse).astype(jnp.bfloat16)
-        for u in range(WIDE):
-            out_ref[start + p + u] = out[:, u * slots : (u + 1) * slots]
-        for _ in fetching:
-            pass
-
-    for _ in fetch(0, 0):
-        pass
-
-    def step(i, _):
-        p = 2 * WIDE * i
-        build(p, 0, fetch(p + WIDE, 1))
-        build(p + WIDE, 1, fetch(p + 2 * WIDE, 0))
-        return 0
-
-    last = stop - start - 2 * WIDE
-    for i in range(last // (2 * WIDE)):
-        step(i, 0)
-    build(last, 0, fetch(last + WIDE, 1))
-    build(last + WIDE, 1, iter(()))
 
 
 def slot_kernel(queries, picks, capacity, rows_ref, slot_ref, rank_ref):
@@ -205,15 +99,142 @@
     slot_ref[padded : 2 * padded, :] = slot_p.astype(jnp.int32)
 
 
-def pair_kernel(
-    queries, picks, capacity, len_hbm, slot_ref, rank_ref, mine_ref, other_ref, emb_ref, out_ref, slot_s, len_s, score, sems
-):
+WIDE = 4
+
+
+def decode_kernel(first, find, start, stop, *refs):
+    refs = list(refs)
+    ids_hbm, words_hbm, scale_hbm, bucket_hbm = refs[:4]
+    del refs[:4]
+    if first:
+        table_hbm = refs.pop(0)
+    else:
+        wide = refs.pop(0)
+        refs.pop(0)
+    if find is not None:
+        near_ref = refs.pop(0)
+    out_ref = refs.pop(0)
+    if first:
+        wide = refs.pop(0)
+    if find is not None:
+        slot_ref, rank_ref = refs[:2]
+        del refs[:2]
+    rest = refs
+    rows, ids_ref, words_ref, scale_bf, scale_ref, bucket_ref, sems = rest[:7]
+    mine = pl.ds(start, stop - start)
+    copies = [
+        pltpu.make_async_copy(ids_hbm.at[mine], ids_ref, sems.at[0]),
+        pltpu.make_async_copy(words_hbm.at[mine], words_ref, sems.at[1]),
+        pltpu.make_async_copy(scale_hbm, scale_bf, sems.at[2]),
+        pltpu.make_async_copy(bucket_hbm, bucket_ref, sems.at[3]),
+    ]
+    if first:
+        table_ref = rest[7]
+        parts = 4
+        size = table_ref.shape[0] // parts
+        loads = [
+            pltpu.make_async_copy(
+                table_hbm.at[pl.ds(i * size, size)], table_ref.at[pl.ds(i * size, size)], sems.at[4 + i]
+            )
+            for i in range(parts)
+        ]
+        for c in loads + copies:
+            c.start()
+        chunk = 256
+        for i in range(parts):
+            loads[i].wait()
+
+            def widen(j, _):
+                r = pl.ds(pl.multiple_of(i * size + j * chunk, chunk), chunk)
+                wide[r, :] = table_ref[r, :].astype(jnp.float32)
+                return 0
+
+            lax.fori_loop(0, size // chunk, widen, 0)
+    else:
+        for c in copies:
+            c.start()
+    for c in copies:
+        c.wait()
+    scale_ref[...] = scale_bf[...].astype(jnp.float32)
+    slots = ids_ref.shape[1]
+    width = wide.shape[1]
+    words = words_ref.shape[1]
+    per = width // words
+    order = ones_where(iota((width, width), 1) == spread(iota((width, width), 0), words, per))
+    levels = [
+        jnp.broadcast_to(bucket_ref[0:1, i : i + 1].astype(jnp.float32), (words, slots * WIDE))
+        for i in range(4)
+    ]
+
+    def fetch(p, buf):
+        for u in range(WIDE):
+            for g in range(slots // 16):
+                got = jnp.concatenate(
+                    [wide[pl.ds(ids_ref[p + u, g * 16 + i], 1), :] for i in range(16)], axis=0
+                )
+                r = u * slots + g * 16
+                rows[buf, r : r + 16, :] = got.astype(jnp.bfloat16)
+                yield
+
+    def build(p, buf, fetching):
+        packed = jnp.concatenate([words_ref[p + u] for u in range(WIDE)], axis=1)
+        centre = dot(order, rows[buf], ((1,), (1,)))
+        parts = []
+        for k in range(per):
+            for _ in range(WIDE):
+                next(fetching, None)
+            low = (packed & (1 << (2 * k))) != 0
+            high = (packed & (2 << (2 * k))) != 0
+            parts.append(
+                jnp.where(
+                    high,
+                    jnp.where(low, levels[3], levels[2]),
+                    jnp.where(low, levels[1], levels[0]),
+                )
+            )
+        value = jnp.concatenate(parts, axis=0)
+        scale = jnp.concatenate([scale_ref[pl.ds(start + p + u, 1), :] for u in range(WIDE)], axis=1)
+        raw = centre + scale * value
+        inverse = lax.rsqrt(jnp.sum(raw * raw, axis=0, keepdims=True) + 1e-06)
+        out = (raw * inverse).astype(jnp.bfloat16)
+        for u in range(WIDE):
+            out_ref[start + p + u] = out[:, u * slots : (u + 1) * slots]
+        for _ in fetching:
+            pass
+
+    for _ in fetch(0, 0):
+        pass
+    if find is not None:
+        slot_kernel(*find, near_ref, slot_ref, rank_ref)
+
+    def step(i, _):
+        p = 2 * WIDE * i
+        build(p, 0, fetch(p + WIDE, 1))
+        build(p + WIDE, 1, fetch(p + 2 * WIDE, 0))
+        return 0
+
+    last = stop - start - 2 * WIDE
+    for i in range(last // (2 * WIDE)):
+        step(i, 0)
+    build(last, 0, fetch(last + WIDE, 1))
+    build(last + WIDE, 1, iter(()))
+
+
+def pair_kernel(queries, picks, capacity, ahead, len_hbm, slot_ref, rank_ref, mine_ref, other_ref, emb_ref, *refs):
+    refs = list(refs)
+    if ahead:
+        later_ref = refs.pop(0)
+    out_ref = refs.pop(0)
+    later_out = refs[: 2 * ahead]
+    slot_s, len_s, score, sems = refs[2 * ahead :]
     copies = [
         pltpu.make_async_copy(slot_ref, slot_s, sems.at[0]),
         pltpu.make_async_copy(len_hbm, len_s, sems.at[1]),
     ]
     for c in copies:
         c.start()
+    if ahead:
+        slot_kernel(queries, picks, capacity, later_ref, *later_out)
     for c in copies:
         c.wait()
     blocks = mine_ref.shape[0]
@@ -225,7 +246,7 @@
     lane = iota((full_tokens, slots), 1)
     spot = iota((full_tokens, width), 1)
 
-    def block(b, _):
+    def block(b):
         best_all = jnp.zeros((full_tokens, width), jnp.float32)
         for s in range(0, capacity, 2):
             asked = []
@@ -244,9 +265,15 @@
                 best = jnp.max(similar, axis=1, keepdims=True)
                 best_all = jnp.where(spot == s + j, best, best_all)
         score[pl.ds(b, 1), :] = jnp.sum(best_all, axis=0, keepdims=True) * (1.0 / full_tokens)
+
+    together = math.gcd(blocks, max(1, UNROLLED // capacity))
+
+    def several(i, _):
+        for u in range(together):
+            block(i * together + u)
         return 0
 
-    lax.fori_loop(0, blocks, block, 0)
+    lax.fori_loop(0, blocks // together, several, 0)
     groups = width // picks
     lane_group = iota((queries, width), 1) // picks
     for c in range(0, blocks, groups):
@@ -301,16 +328,29 @@
     emb_shape = jax.ShapeDtypeStruct((passages, width, slots), jnp.bfloat16)
     wide_shape = jax.ShapeDtypeStruct(centroids.shape, jnp.float32)
 
-    def decode(start, stop, wide, embedded):
-        if start == stop:
-            return embedded, wide
+    def slot_shapes(blocks):
+        padded = -(-blocks // 8) * 8
+        return (
+            jax.ShapeDtypeStruct((2 * padded, width), jnp.int32),
+            jax.ShapeDtypeStruct((blocks * query_count, width), jnp.int32),
+        )
+
+    def decode(start, stop, wide, embedded, near=None):
         first = embedded is None
         extra = (centroids,) if first else (wide, embedded)
+        outs = (emb_shape, wide_shape) if first else (emb_shape,)
+        specs = whole(5, pltpu.HBM) if first else whole(4, pltpu.HBM) + whole(2, VMEM)
+        find = None
+        if near is not None:
+            find = (query_count, picks, capacity)
+            extra += (near,)
+            outs += slot_shapes(near.shape[0])
+            specs += whole(1, VMEM)
         out = pl.pallas_call(
-            functools.partial(decode_kernel, first, start, stop),
-            out_shape=(emb_shape, wide_shape) if first else emb_shape,
-            in_specs=whole(5, pltpu.HBM) if first else whole(4, pltpu.HBM) + whole(2, VMEM),
-            out_specs=(pl.BlockSpec(memory_space=VMEM),) * 2 if first else pl.BlockSpec(memory_space=VMEM),
+            functools.partial(decode_kernel, first, find, start, stop),
+            out_shape=outs,
+            in_specs=specs,
+            out_specs=(pl.BlockSpec(memory_space=VMEM),) * len(outs),
             scratch_shapes=[
                 VMEM((2, WIDE * slots, width), jnp.bfloat16),
                 SMEM((stop - start, slots), jnp.int32),
@@ -328,33 +368,22 @@
             ),
             name="decode",
         )(*stored, *extra)
-        return out if first else (out, wide)
-
-    def find(mine):
-        blocks = mine.shape[0]
-        padded = -(-blocks // 8) * 8
-        return pl.pallas_call(
-            functools.partial(slot_kernel, query_count, picks, capacity),
-            out_shape=(
-                jax.ShapeDtypeStruct((2 * padded, width), jnp.int32),
-                jax.ShapeDtypeStruct((blocks * query_count, width), jnp.int32),
-            ),
-            in_specs=whole(1, VMEM),
-            out_specs=(pl.BlockSpec(memory_space=VMEM),) * 2,
-            compiler_params=LIMIT,
-            cost_estimate=pl.CostEstimate(flops=10**9, bytes_accessed=0, transcendentals=0),
-            name="slots",
-        )(mine)
-
-    def score(found, mine, other):
+        return (out[0], out[1] if first else wide) + tuple(out[2 if first else 1 :])
+
+    def score(found, mine, other, later=None):
         blocks = mine.shape[0]
         padded = -(-blocks // 8) * 8
         lanes = -(-blocks * picks // width) * width
-        return pl.pallas_call(
-            functools.partial(pair_kernel, query_count, picks, capacity),
-            out_shape=jax.ShapeDtypeStruct((query_count, lanes), jnp.float32),
-            in_specs=whole(1, pltpu.HBM) + whole(5, VMEM),
-            out_specs=pl.BlockSpec(memory_space=VMEM),
+        outs = (jax.ShapeDtypeStruct((query_count, lanes), jnp.float32),)
+        operands = (lengths, *found, mine, other, embedded)
+        if later is not None:
+            outs += slot_shapes(later.shape[0])
+            operands += (later,)
+        out = pl.pallas_call(
+            functools.partial(pair_kernel, query_count, picks, capacity, later is not None),
+            out_shape=outs,
+            in_specs=whole(1, pltpu.HBM) + whole(len(operands) - 1, VMEM),
+            out_specs=(pl.BlockSpec(memory_space=VMEM),) * len(outs),
             scratch_shapes=[
                 SMEM((2 * padded, width), jnp.int32),
                 SMEM(lengths.shape, jnp.int32),
@@ -364,7 +393,8 @@
             compiler_params=LIMIT,
             cost_estimate=pl.CostEstimate(flops=3 * 10**9, bytes_accessed=0, transcendentals=0),
             name="pairs",
-        )(lengths, *found, mine, other, embedded)[:, : blocks * picks]
+        )(*operands)
+        return out[0][:, : blocks * picks], out[1:]
 
     steps = []
     d = shards // 2
@@ -374,25 +404,27 @@
     unit = 2 * WIDE
     units = passages // unit
     parts = len(steps)
-    cuts = [-(-units * i // parts) * unit for i in range(parts + 1)]
+    cuts = [(2 * units * i + parts) // (2 * parts) * unit for i in range(parts + 1)]
     held = payload[None]
     wide = embedded = None
     for i, d in enumerate(steps[:-2]):
         moved = swap_shard(held, d)
-        embedded, wide = decode(cuts[i], cuts[i + 1], wide, embedded)
-        moved, embedded = lax.optimization_barrier((moved, embedded))
+        if cuts[i] < cuts[i + 1]:
+            embedded, wide = decode(cuts[i], cuts[i + 1], wide, embedded)
+            moved, embedded = lax.optimization_barrier((moved, embedded))
         held = jnp.concatenate([held, moved], axis=0)
     moved = swap_shard(held, steps[-2])
     far_a = swap_shard(held, 1)
-    embedded, wide = decode(cuts[-3], cuts[-2], wide, embedded)
-    moved, embedded = lax.optimization_barrier((moved, embedded))
+    if cuts[-3] < cuts[-2]:
+        embedded, wide = decode(cuts[-3], cuts[-2], wide, embedded)
+        moved, embedded = lax.optimization_barrier((moved, embedded))
     far_b = swap_shard(moved, 1)
-    embedded, wide = decode(cuts[-2], cuts[-1], wide, embedded)
     near = jnp.concatenate([held, moved], axis=0)
-    near_scores = score(find(near), near, swap_sub(near))
-    far_b, near_scores = lax.optimization_barrier((far_b, near_scores))
+    embedded, wide, *near_found = decode(cuts[-2], cuts[-1], wide, embedded, near)
+    far_b, embedded = lax.optimization_barrier((far_b, embedded))
     far = jnp.concatenate([far_a, far_b], axis=0)
-    far_scores = score(find(far), far, swap_sub(far))
+    near_scores, far_found = score(near_found, near, swap_sub(near), far)
+    far_scores, _ = score(far_found, far, swap_sub(far))
     total = near_scores + swap_shard(far_scores, 1)
     for d in reversed(steps[:-1]):
         half = total.shape[1] // 2

time: 41.3 us -> 39.6 us (0.959)
  Pallas kernels: 15.7 us -> 13.8 us
    pallas_call x5 -> x3, Pallas kernels: 10.6 us -> 9.57 us  [decode(): pl.pallas_call(functools.partial(decode_kernel, first, find, start, stop)...]
    pallas_call x2, Pallas kernels: 4.82 us -> 3.98 us  [score(): pl.pallas_call(functools.partial(pair_kernel, query_count, picks, capacit...]
    ppermute x7, starting transfers between devices: 12.4 us -> 12.9 us  [swap_shard(): return lax.ppermute(x, 'shard', [(i, i ^ d) for i in range(shards)])]
    ppermute x3, waiting for transfers between devices: 1.61 us -> 1.17 us  [swap_sub(): return lax.ppermute(x, 'sub', [(i, i ^ 1) for i in range(halves)])]
  transfers between devices with their start and end apart: 10 -> 10, of which waited for: 7 -> 6; matrix products, arithmetic and copies ran while one was open for 0% -> 0% of each run, Pallas kernels for 32% -> 30%
where the time goes in v4:
time: 39.6 us; the launch traced here: 39.4 us
  Pallas kernels  13.8 us (35%)
  starting transfers between devices  13.4 us (34%)
  waiting for transfers between devices  9.45 us (24%)
  local copies, waits for them, and re-layouts  1.86 us (5%)
  other arithmetic  0.66 us (2%)
    ppermute x7, starting transfers between devices, swap_shard(): return lax.ppermute(x, 'shard', [(i, i ^ d) for i in range(shards)])  12.9 us
    pallas_call x3, Pallas kernels, decode(): pl.pallas_call(functools.partial(decode_kernel, first, find, start, stop)...  9.57 us
    ppermute x7, waiting for transfers between devices, swap_shard(): return lax.ppermute(x, 'shard', [(i, i ^ d) for i in range(shards)])  8.28 us
    pallas_call x2, Pallas kernels, score(): pl.pallas_call(functools.partial(pair_kernel, query_count, picks, capacit...  3.98 us
    unnamed x17, local copies, waits for them, and re-layouts  1.69 us
    ppermute x3, waiting for transfers between devices, swap_sub(): return lax.ppermute(x, 'sub', [(i, i ^ 1) for i in range(halves)])  1.17 us
  transfers between devices with their start and end apart: 10, of which 6 were waited for; matrix products, arithmetic and copies ran while one was open for 0% of the time, Pallas kernels for 30%

profile of v4, /device:TPU:0, one launch (start us, length us, event | category | flops | bytes accessed | tf_op | source)
XLA Modules:
  0.0 39.4 jit_solution(15882201585639264815)
XLA Ops:
  0.0 0.0 copy-start.1
  0.0 0.0 copy-start
  0.0 0.0 copy-start.2
  0.0 1.0 %copy-done.2 = bf16[16,16,128]{2,1,0:T(8,128)(2,1)S(1)} copy-done((bf16[16,16,128]{2,1,0:T(8,128)(2,1)S(1)}, bf16[16,16,128]{2,1,0:T(8,128)(2,1)}, u32[]{:S(2)}) %copy-start.2) | copy-done | bytes 65560
  1.0 0.0 copy-start.5
  1.0 0.7 %copy-done.5 = s32[16,16]{1,0:T(8,128)S(1)} copy-done((s32[16,16]{1,0:T(8,128)S(1)}, s32[16,16]{1,0:T(8,128)}, u32[]{:S(2)}) %copy-start.5) | copy-done | bytes 1048
  1.7 0.0 copy-start.3
  1.7 0.0 copy-start.4
  1.7 0.0 copy-start.6
  1.7 0.3 pack.1
  2.0 4.1 %collective-permute-start = (bf16[1,288,128]{2,1,0:T(8,128)(2,1)S(1)}, bf16[1,288,128]{2,1,0:T(8,128)(2,1)S(1)}, u32[]{:S(2)}, u32[]{:S(2)}) collective-permute-start(bf16[1,288,128]{2,1,0:T(8,128)(2,1)S(1)} %bitcast.4), channel_id=1, source_target_pairs={{0,8},{2,10},{4,12},{6,14},{8,0},{10,2},{12,4},{14,6},{1,9},{3,11}... | collective-permute-start | bytes 221192 | tf_op jit(solution)/shard_map/ppermute | solution.py:302
  6.0 0.0 copy-done.1
  6.1 0.0 copy-done
  6.1 0.0 copy-done.3
  6.1 0.0 copy-done.4
  6.1 0.0 copy-done.6
  6.1 3.4 %decode.3 = (bf16[64,128,128]{2,1,0:T(8,128)(2,1)S(1)}, f32[4096,128]{1,0:T(8,128)S(1)}) custom-call(s32[64,128]{1,0:T(8,128)S(1)} %copy-done.3, s32[64,16,128]{2,1,0:T(8,128)S(1)} %bitcast.7, bf16[64,128]{1,0:T(8,128)(2,1)S(1)} %copy-done.4, bf16[1,4]{1,0:T(2,128)(2,1)S(1)} %bitcast.11, bf16[4096,128]{1,0:T(8,128)(2,1)S(1)} %copy-done), custom_call_target="tpu_custom_call" | custom-call | flops 4800000000 | tf_op jit(solution)/shard_map/decode/pallas_call | solution.py:349
  9.5 0.5 %collective-permute-done = bf16[1,288,128]{2,1,0:T(8,128)(2,1)S(1)} collective-permute-done((bf16[1,288,128]{2,1,0:T(8,128)(2,1)S(1)}, bf16[1,288,128]{2,1,0:T(8,128)(2,1)S(1)}, u32[]{:S(2)}, u32[]{:S(2)}) %collective-permute-start) | collective-permute-done | bytes 73760 | tf_op jit(solution)/shard_map/ppermute | solution.py:302
  10.0 1.1 %collective-permute-start.1 = (bf16[2,288,128]{2,1,0:T(8,128)(2,1)S(1)}, bf16[2,288,128]{2,1,0:T(8,128)(2,1)S(1)}, u32[]{:S(2)}, u32[]{:S(2)}) collective-permute-start(bf16[2,288,128]{2,1,0:T(8,128)(2,1)S(1)} %pad_maximum_fusion.1), channel_id=1, source_target_pairs={{0,4},{2,6},{4,0},{6,2},{8,12},{10,14},{12,8},{14,10},{1,5},{3,7},... | collective-permute-start | bytes 442376 | tf_op jit(solution)/shard_map/ppermute | solution.py:302
  11.1 1.5 %collective-permute-start.4 = (bf16[2,288,128]{2,1,0:T(8,128)(2,1)S(1)}, bf16[2,288,128]{2,1,0:T(8,128)(2,1)S(1)}, u32[]{:S(2)}, u32[]{:S(2)}) collective-permute-start(bf16[2,288,128]{2,1,0:T(8,128)(2,1)S(1)} %pad_maximum_fusion.1), channel_id=1, source_target_pairs={{0,2},{2,0},{4,6},{6,4},{8,10},{10,8},{12,14},{14,12},{1,3},{3,1},... | collective-permute-start | bytes 442376 | tf_op jit(solution)/shard_map/ppermute | solution.py:302
  12.6 2.4 %decode.4.refs_5_ = bf16[64,128,128]{2,1,0:T(8,128)(2,1)S(1)} custom-call(s32[64,128]{1,0:T(8,128)S(1)} %copy-done.3, s32[64,16,128]{2,1,0:T(8,128)S(1)} %bitcast.8, bf16[64,128]{1,0:T(8,128)(2,1)S(1)} %copy-done.4, bf16[1,4]{1,0:T(2,128)(2,1)S(1)} %bitcast.12, f32[4096,128]{1,0:T(8,128)S(1)} %get-tuple-element.19.refs_4_, ...), custom_call_target="tpu_custom_call", output_to_operand_aliasing={{}: (5, {})} | custom-call | flops 3200000000 | tf_op jit(solution)/shard_map/decode/pallas_call | solution.py:349
  15.0 0.1 collective-permute-done.1
  15.2 0.0 copy-start.7
  15.2 1.8 %collective-permute-start.3 = (bf16[2,288,128]{2,1,0:T(8,128)(2,1)S(1)}, bf16[2,288,128]{2,1,0:T(8,128)(2,1)S(1)}, u32[]{:S(2)}, u32[]{:S(2)}) collective-permute-start(bf16[2,288,128]{2,1,0:T(8,128)(2,1)S(1)} %collective-permute-done.1), channel_id=1, source_target_pairs={{0,2},{2,0},{4,6},{6,4},{8,10},{10,8},{12,14},{14,12},{1,3},{3,1},... | collective-permute-start | bytes 442376 | tf_op jit(solution)/shard_map/ppermute | solution.py:302
  17.0 0.0 collective-permute-start.2
  17.0 3.8 %decode.5 = (bf16[64,128,128]{2,1,0:T(8,128)(2,1)S(1)}, s32[16,128]{1,0:T(8,128)S(1)}, s32[64,128]{1,0:T(8,128)S(1)}) custom-call(s32[64,128]{1,0:T(8,128)S(1)} %copy-done.3, s32[64,16,128]{2,1,0:T(8,128)S(1)} %bitcast.9, bf16[64,128]{1,0:T(8,128)(2,1)S(1)} %copy-done.4, bf16[1,4]{1,0:T(2,128)(2,1)S(1)} %bitcast.13, ...), custom_call_target="tpu_custom_call", output_to_operand_aliasing={{0}: (5, {})} | custom-call | flops 4800000000 | tf_op jit(solution)/shard_map/decode/pallas_call | solution.py:349
  20.8 0.0 collective-permute-done.4
  20.9 0.0 collective-permute-done.3
  20.9 0.6 %collective-permute-start.5 = (bf16[4,288,128]{2,1,0:T(8,128)(2,1)S(1)}, bf16[4,288,128]{2,1,0:T(8,128)(2,1)S(1)}, u32[]{:S(2)}, u32[]{:S(2)}) collective-permute-start(bf16[4,288,128]{2,1,0:T(8,128)(2,1)S(1)} %constant_dynamic-update-slice_fusion.refs_0_.mine_ref), channel_id=1, source_target_pairs={{0,1},{1,0},{2,3},{3,2},{4,5},{5,4},{6,7},{7,6},{8,9},{9,8},{10,11... | collective-permute-start | bytes 884744 | tf_op jit(solution)/shard_map/ppermute | solution.py:305
  21.5 0.0 collective-permute-done.2.other_ref
  21.5 0.0 copy-done.7
  21.5 2.1 %pairs.2 = (f32[16,128]{1,0:T(8,128)S(1)}, s32[16,128]{1,0:T(8,128)S(1)}, s32[64,128]{1,0:T(8,128)S(1)}) custom-call(s32[64]{0:T(128)S(1)} %copy-done.7, s32[16,128]{1,0:T(8,128)S(1)} %get-tuple-element.25.slot_ref, s32[64,128]{1,0:T(8,128)S(1)} %get-tuple-element.26.rank_ref, bf16[4,288,128]{2,1,0:T(8,128)(2,1)S(1)} %pad_maximum_fusion.refs_6_.mine_ref, ...), custom_call_target="tpu_custom_call" | custom-call | flops 3000000000 | tf_op jit(solution)/shard_map/pairs/pallas_call | solution.py:382
  23.6 0.0 collective-permute-done.5.other_ref
  23.6 1.9 %pairs.3 = f32[16,128]{1,0:T(8,128)S(1)} custom-call(s32[64]{0:T(128)S(1)} %copy-done.7, s32[16,128]{1,0:T(8,128)S(1)} %get-tuple-element.31.slot_ref, s32[64,128]{1,0:T(8,128)S(1)} %get-tuple-element.32.rank_ref, bf16[4,288,128]{2,1,0:T(8,128)(2,1)S(1)} %constant_dynamic-update-slice_fusion.refs_0_.mine_ref, ...), custom_call_target="tpu_custom_call" | custom-call | flops 3000000000 | tf_op jit(solution)/shard_map/pairs/pallas_call | solution.py:382
  25.5 0.9 %collective-permute-start.6 = (f32[16,64]{1,0:T(8,128)S(1)}, f32[16,64]{1,0:T(8,128)S(1)}, u32[]{:S(2)}, u32[]{:S(2)}) collective-permute-start(f32[16,64]{1,0:T(8,128)S(1)} %bitcast.10), channel_id=1, source_target_pairs={{0,2},{2,0},{4,6},{6,4},{8,10},{10,8},{12,14},{14,12},{1,3},{3,1},... | collective-permute-start | bytes 12296 | tf_op jit(solution)/shard_map/ppermute | solution.py:302
  26.4 2.9 %collective-permute-done.6 = f32[16,64]{1,0:T(8,128)S(1)} collective-permute-done((f32[16,64]{1,0:T(8,128)S(1)}, f32[16,64]{1,0:T(8,128)S(1)}, u32[]{:S(2)}, u32[]{:S(2)}) %collective-permute-start.6) | collective-permute-done | bytes 4128 | tf_op jit(solution)/shard_map/ppermute | solution.py:302
  29.2 0.1 slice.26
  29.3 1.0 %collective-permute-start.7 = (f32[16,32]{1,0:T(8,128)S(1)}, f32[16,32]{1,0:T(8,128)S(1)}, u32[]{:S(2)}, u32[]{:S(2)}) collective-permute-start(f32[16,32]{1,0:T(8,128)S(1)} %slice.26), channel_id=1, source_target_pairs={{0,4},{2,6},{4,0},{6,2},{8,12},{10,14},{12,8},{14,10},{1,5},{3,7},... | collective-permute-start | bytes 6152 | tf_op jit(solution)/shard_map/ppermute | solution.py:302
  30.3 2.6 %collective-permute-done.7 = f32[16,32]{1,0:T(8,128)S(1)} collective-permute-done((f32[16,32]{1,0:T(8,128)S(1)}, f32[16,32]{1,0:T(8,128)S(1)}, u32[]{:S(2)}, u32[]{:S(2)}) %collective-permute-start.7) | collective-permute-done | bytes 2080 | tf_op jit(solution)/shard_map/ppermute | solution.py:302
  33.0 0.1 slice.28
  33.0 2.4 %collective-permute-start.8 = (f32[16,16]{1,0:T(8,128)S(1)}, f32[16,16]{1,0:T(8,128)S(1)}, u32[]{:S(2)}, u32[]{:S(2)}) collective-permute-start(f32[16,16]{1,0:T(8,128)S(1)} %slice.28), channel_id=1, source_target_pairs={{0,8},{2,10},{4,12},{6,14},{8,0},{10,2},{12,4},{14,6},{1,9},{3,11}... | collective-permute-start | bytes 3080 | tf_op jit(solution)/shard_map/ppermute | solution.py:302
  35.5 2.1 %collective-permute-done.8 = f32[16,16]{1,0:T(8,128)S(1)} collective-permute-done((f32[16,16]{1,0:T(8,128)S(1)}, f32[16,16]{1,0:T(8,128)S(1)}, u32[]{:S(2)}, u32[]{:S(2)}) %collective-permute-start.8) | collective-permute-done | bytes 1056 | tf_op jit(solution)/shard_map/ppermute | solution.py:302
  37.6 0.0 collective-permute-start.9
  37.6 1.2 %collective-permute-done.9 = f32[16,16]{1,0:T(8,128)S(1)} collective-permute-done((f32[16,16]{1,0:T(8,128)S(1)}, f32[16,16]{1,0:T(8,128)S(1)}, u32[]{:S(2)}, u32[]{:S(2)}) %collective-permute-start.9) | collective-permute-done | bytes 1056 | tf_op jit(solution)/shard_map/ppermute | solution.py:305
  38.8 0.6 %add.15 = f32[16,16]{1,0:T(8,128)} add(f32[16,16]{1,0:T(8,128)S(1)} %slice_add_fusion, f32[16,16]{1,0:T(8,128)S(1)} %collective-permute-done.9) | non-fusion elementwise | flops 256 | bytes 3072 | tf_op jit(solution)/shard_map/add | solution.py:432
  (7 shorter events, 0.1 us)
Async XLA Ops:
  0.0 6.1 %copy-start.1 = (s32[64,128,16]{1,2,0:T(8,128)S(1)}, s32[64,128,16]{1,2,0:T(8,128)}, u32[]{:S(2)}) copy-start(s32[64,128,16]{1,2,0:T(8,128)} %param.10) | copy-start | bytes 1572868
  0.0 6.1 %copy-start = (bf16[4096,128]{1,0:T(8,128)(2,1)S(1)}, bf16[4096,128]{1,0:T(8,128)(2,1)}, u32[]{:S(2)}) copy-start(bf16[4096,128]{1,0:T(8,128)(2,1)} %refs_4_.1) | copy-start | bytes 3145732
  0.0 1.0 %copy-start.2 = (bf16[16,16,128]{2,1,0:T(8,128)(2,1)S(1)}, bf16[16,16,128]{2,1,0:T(8,128)(2,1)}, u32[]{:S(2)}) copy-start(bf16[16,16,128]{2,1,0:T(8,128)(2,1)} %query_hbm.1) | copy-start | bytes 196612
  1.0 0.7 %copy-start.5 = (s32[16,16]{1,0:T(8,128)S(1)}, s32[16,16]{1,0:T(8,128)}, u32[]{:S(2)}) copy-start(s32[16,16]{1,0:T(8,128)} %cand_hbm.1) | copy-start | bytes 3076
  1.7 4.4 %copy-start.3 = (s32[64,128]{1,0:T(8,128)S(1)}, s32[64,128]{1,0:T(8,128)}, u32[]{:S(2)}) copy-start(s32[64,128]{1,0:T(8,128)} %refs_0_.5) | copy-start | bytes 98308
  1.7 4.4 %copy-start.4 = (bf16[64,128]{1,0:T(8,128)(2,1)S(1)}, bf16[64,128]{1,0:T(8,128)(2,1)}, u32[]{:S(2)}) copy-start(bf16[64,128]{1,0:T(8,128)(2,1)} %refs_2_.5) | copy-start | bytes 49156
  1.7 4.4 %copy-start.6 = (bf16[4]{0:T(256)(128)(2,1)S(1)}, bf16[4]{0:T(256)(128)(2,1)}, u32[]{:S(2)}) copy-start(bf16[4]{0:T(256)(128)(2,1)} %param.15) | copy-start | bytes 28
  2.0 8.0 %collective-permute-start = (bf16[1,288,128]{2,1,0:T(8,128)(2,1)S(1)}, bf16[1,288,128]{2,1,0:T(8,128)(2,1)S(1)}, u32[]{:S(2)}, u32[]{:S(2)}) collective-permute-start(bf16[1,288,128]{2,1,0:T(8,128)(2,1)S(1)} %bitcast.4), channel_id=1, source_target_pairs={{0,8},{2,10},{4,12},{6,14},{8,0},{10,2},{12,4},{14,6},{1,9},{3,11}... | collective-permute-start | bytes 221192 | tf_op jit(solution)/shard_map/ppermute | solution.py:302
  10.0 5.2 %collective-permute-start.1 = (bf16[2,288,128]{2,1,0:T(8,128)(2,1)S(1)}, bf16[2,288,128]{2,1,0:T(8,128)(2,1)S(1)}, u32[]{:S(2)}, u32[]{:S(2)}) collective-permute-start(bf16[2,288,128]{2,1,0:T(8,128)(2,1)S(1)} %pad_maximum_fusion.1), channel_id=1, source_target_pairs={{0,4},{2,6},{4,0},{6,2},{8,12},{10,14},{12,8},{14,10},{1,5},{3,7},... | collective-permute-start | bytes 442376 | tf_op jit(solution)/shard_map/ppermute | solution.py:302
  11.1 9.7 %collective-permute-start.4 = (bf16[2,288,128]{2,1,0:T(8,128)(2,1)S(1)}, bf16[2,288,128]{2,1,0:T(8,128)(2,1)S(1)}, u32[]{:S(2)}, u32[]{:S(2)}) collective-permute-start(bf16[2,288,128]{2,1,0:T(8,128)(2,1)S(1)} %pad_maximum_fusion.1), channel_id=1, source_target_pairs={{0,2},{2,0},{4,6},{6,4},{8,10},{10,8},{12,14},{14,12},{1,3},{3,1},... | collective-permute-start | bytes 442376 | tf_op jit(solution)/shard_map/ppermute | solution.py:302
  15.2 6.3 %copy-start.7 = (s32[64]{0:T(128)S(1)}, s32[64]{0:T(128)}, u32[]{:S(2)}) copy-start(s32[64]{0:T(128)} %len_hbm.3) | copy-start | bytes 772
  15.2 5.6 %collective-permute-start.3 = (bf16[2,288,128]{2,1,0:T(8,128)(2,1)S(1)}, bf16[2,288,128]{2,1,0:T(8,128)(2,1)S(1)}, u32[]{:S(2)}, u32[]{:S(2)}) collective-permute-start(bf16[2,288,128]{2,1,0:T(8,128)(2,1)S(1)} %collective-permute-done.1), channel_id=1, source_target_pairs={{0,2},{2,0},{4,6},{6,4},{8,10},{10,8},{12,14},{14,12},{1,3},{3,1},... | collective-permute-start | bytes 442376 | tf_op jit(solution)/shard_map/ppermute | solution.py:302
  17.0 4.5 %collective-permute-start.2 = (bf16[4,288,128]{2,1,0:T(8,128)(2,1)S(1)}, bf16[4,288,128]{2,1,0:T(8,128)(2,1)S(1)}, u32[]{:S(2)}, u32[]{:S(2)}) collective-permute-start(bf16[4,288,128]{2,1,0:T(8,128)(2,1)S(1)} %pad_maximum_fusion.refs_6_.mine_ref), channel_id=1, source_target_pairs={{0,1},{1,0},{2,3},{3,2},{4,5},{5,4},{6,7},{7,6},{8,9},{9,8},{10,11... | collective-permute-start | bytes 884744 | tf_op jit(solution)/shard_map/ppermute | solution.py:305
  20.9 2.6 %collective-permute-start.5 = (bf16[4,288,128]{2,1,0:T(8,128)(2,1)S(1)}, bf16[4,288,128]{2,1,0:T(8,128)(2,1)S(1)}, u32[]{:S(2)}, u32[]{:S(2)}) collective-permute-start(bf16[4,288,128]{2,1,0:T(8,128)(2,1)S(1)} %constant_dynamic-update-slice_fusion.refs_0_.mine_ref), channel_id=1, source_target_pairs={{0,1},{1,0},{2,3},{3,2},{4,5},{5,4},{6,7},{7,6},{8,9},{9,8},{10,11... | collective-permute-start | bytes 884744 | tf_op jit(solution)/shard_map/ppermute | solution.py:305
  25.5 3.7 %collective-permute-start.6 = (f32[16,64]{1,0:T(8,128)S(1)}, f32[16,64]{1,0:T(8,128)S(1)}, u32[]{:S(2)}, u32[]{:S(2)}) collective-permute-start(f32[16,64]{1,0:T(8,128)S(1)} %bitcast.10), channel_id=1, source_target_pairs={{0,2},{2,0},{4,6},{6,4},{8,10},{10,8},{12,14},{14,12},{1,3},{3,1},... | collective-permute-start | bytes 12296 | tf_op jit(solution)/shard_map/ppermute | solution.py:302
  29.3 3.7 %collective-permute-start.7 = (f32[16,32]{1,0:T(8,128)S(1)}, f32[16,32]{1,0:T(8,128)S(1)}, u32[]{:S(2)}, u32[]{:S(2)}) collective-permute-start(f32[16,32]{1,0:T(8,128)S(1)} %slice.26), channel_id=1, source_target_pairs={{0,4},{2,6},{4,0},{6,2},{8,12},{10,14},{12,8},{14,10},{1,5},{3,7},... | collective-permute-start | bytes 6152 | tf_op jit(solution)/shard_map/ppermute | solution.py:302
  33.0 4.6 %collective-permute-start.8 = (f32[16,16]{1,0:T(8,128)S(1)}, f32[16,16]{1,0:T(8,128)S(1)}, u32[]{:S(2)}, u32[]{:S(2)}) collective-permute-start(f32[16,16]{1,0:T(8,128)S(1)} %slice.28), channel_id=1, source_target_pairs={{0,8},{2,10},{4,12},{6,14},{8,0},{10,2},{12,4},{14,6},{1,9},{3,11}... | collective-permute-start | bytes 3080 | tf_op jit(solution)/shard_map/ppermute | solution.py:302
  37.6 1.2 %collective-permute-start.9 = (f32[16,16]{1,0:T(8,128)S(1)}, f32[16,16]{1,0:T(8,128)S(1)}, u32[]{:S(2)}, u32[]{:S(2)}) collective-permute-start(f32[16,16]{1,0:T(8,128)S(1)} %slice_add_fusion), channel_id=1, source_target_pairs={{0,1},{1,0},{2,3},{3,2},{4,5},{5,4},{6,7},{7,6},{8,9},{9,8},{10,11... | collective-permute-start | bytes 3080 | tf_op jit(solution)/shard_map/ppermute | solution.py:305

commit v5 on v4

--- a/solution.py
+++ b/solution.py
@@ -104,10 +104,10 @@
 
 def decode_kernel(first, find, start, stop, *refs):
     refs = list(refs)
-    ids_hbm, words_hbm, scale_hbm, bucket_hbm = refs[:4]
+    ids_all, words_ref, scale_bf, bucket_ref = refs[:4]
     del refs[:4]
     if first:
-        table_hbm = refs.pop(0)
+        table_ref = refs.pop(0)
     else:
         wide = refs.pop(0)
         refs.pop(0)
@@ -119,43 +119,22 @@
     if find is not None:
         slot_ref, rank_ref = refs[:2]
         del refs[:2]
-    rest = refs
-    rows, ids_ref, words_ref, scale_bf, scale_ref, bucket_ref, sems = rest[:7]
-    mine = pl.ds(start, stop - start)
-    copies = [
-        pltpu.make_async_copy(ids_hbm.at[mine], ids_ref, sems.at[0]),
-        pltpu.make_async_copy(words_hbm.at[mine], words_ref, sems.at[1]),
-        pltpu.make_async_copy(scale_hbm, scale_bf, sems.at[2]),
-        pltpu.make_async_copy(bucket_hbm, bucket_ref, sems.at[3]),
-    ]
+    rows, ids_ref, scale_ref, sem = refs
+    copy = pltpu.make_async_copy(ids_all.at[pl.ds(start, stop - start)], ids_ref, sem)
+    copy.start()
+    scale_ref[...] = scale_bf[...].astype(jnp.float32)
     if first:
-        table_ref = rest[7]
-        parts = 4
-        size = table_ref.shape[0] // parts
-        loads = [
-            pltpu.make_async_copy(
-                table_hbm.at[pl.ds(i * size, size)], table_ref.at[pl.ds(i * size, size)], sems.at[4 + i]
-            )
-            for i in range(parts)
-        ]
-        for c in loads + copies:
-            c.start()
-        chunk = 256
-        for i in range(parts):
-            loads[i].wait()
-
-            def widen(j, _):
-                r = pl.ds(pl.multiple_of(i * size + j * chunk, chunk), chunk)
-                wide[r, :] = table_ref[r, :].astype(jnp.float32)
-                return 0
-
-            lax.fori_loop(0, size // chunk, widen, 0)
-    else:
-        for c in copies:
-            c.start()
-    for c in copies:
-        c.wait()
-    scale_ref[...] = scale_bf[...].astype(jnp.float32)
+        chunk = 512
+
+        def widen(j, _):
+            r = pl.ds(pl.multiple_of(j * chunk, chunk), chunk)
+            wide[r, :] = table_ref[r, :].astype(jnp.float32)
+            return 0
+
+        lax.fori_loop(0, table_ref.shape[0] // chunk, widen, 0)
+    if find is not None:
+        slot_kernel(*find, near_ref, slot_ref, rank_ref)
+    copy.wait()
     slots = ids_ref.shape[1]
     width = wide.shape[1]
     words = words_ref.shape[1]
@@ -177,7 +156,7 @@
                 yield
 
     def build(p, buf, fetching):
-        packed = jnp.concatenate([words_ref[p + u] for u in range(WIDE)], axis=1)
+        packed = jnp.concatenate([words_ref[start + p + u] for u in range(WIDE)], axis=1)
         centre = dot(order, rows[buf], ((1,), (1,)))
         parts = []
         for k in range(per):
@@ -204,8 +183,6 @@
 
     for _ in fetch(0, 0):
         pass
-    if find is not None:
-        slot_kernel(*find, near_ref, slot_ref, rank_ref)
 
     def step(i, _):
         p = 2 * WIDE * i
@@ -339,7 +316,7 @@
         first = embedded is None
         extra = (centroids,) if first else (wide, embedded)
         outs = (emb_shape, wide_shape) if first else (emb_shape,)
-        specs = whole(5, pltpu.HBM) if first else whole(4, pltpu.HBM) + whole(2, VMEM)
+        specs = whole(4 + len(extra), VMEM)
         find = None
         if near is not None:
             find = (query_count, picks, capacity)
@@ -354,13 +331,9 @@
             scratch_shapes=[
                 VMEM((2, WIDE * slots, width), jnp.bfloat16),
                 SMEM((stop - start, slots), jnp.int32),
-                VMEM((stop - start, words, slots), jnp.int32),
-                VMEM(block_scales.shape, block_scales.dtype),
                 VMEM(block_scales.shape, jnp.float32),
-                VMEM((1, 4), bucket_weights.dtype),
-                pltpu.SemaphoreType.DMA((8 if first else 4,)),
-            ]
-            + ([VMEM(centroids.shape, centroids.dtype)] if first else []),
+                pltpu.SemaphoreType.DMA,
+            ],
             input_output_aliases={} if first else {5: 0},
             compiler_params=LIMIT,
             cost_estimate=pl.CostEstimate(

time: 39.6 us -> 39 us (0.985)
  Pallas kernels: 13.8 us -> 13.1 us
    pallas_call x3, Pallas kernels: 9.57 us -> 8.84 us  [decode(): pl.pallas_call(functools.partial(decode_kernel, first, find, start, stop)...]
  transfers between devices with their start and end apart: 10 -> 10, of which waited for: 6 -> 7; matrix products, arithmetic and copies ran while one was open for 0% -> 0% of each run, Pallas kernels for 30% -> 28%
where the time goes in v5:
time: 39 us; the launch traced here: 38.8 us
  starting transfers between devices  13.6 us (35%)
  Pallas kernels  13.1 us (34%)
  waiting for transfers between devices  9.46 us (24%)
  local copies, waits for them, and re-layouts  1.86 us (5%)
  other arithmetic  0.66 us (2%)
    ppermute x7, starting transfers between devices, swap_shard(): return lax.ppermute(x, 'shard', [(i, i ^ d) for i in range(shards)])  13.1 us
    pallas_call x3, Pallas kernels, decode(): pl.pallas_call(functools.partial(decode_kernel, first, find, start, stop)...  8.84 us
    ppermute x7, waiting for transfers between devices, swap_shard(): return lax.ppermute(x, 'shard', [(i, i ^ d) for i in range(shards)])  8.28 us
    pallas_call x2, Pallas kernels, score(): pl.pallas_call(functools.partial(pair_kernel, query_count, picks, capacit...  3.96 us
    unnamed x17, local copies, waits for them, and re-layouts  1.69 us
    ppermute x3, waiting for transfers between devices, swap_sub(): return lax.ppermute(x, 'sub', [(i, i ^ 1) for i in range(halves)])  1.17 us
  transfers between devices with their start and end apart: 10, of which 7 were waited for; matrix products, arithmetic and copies ran while one was open for 0% of the time, Pallas kernels for 28%

profile of v5, /device:TPU:0, one launch (start us, length us, event | category | flops | bytes accessed | tf_op | source)
XLA Modules:
  0.0 38.8 jit_solution(8066760757966620806)
XLA Ops:
  0.0 0.0 copy-start.1
  0.0 0.0 copy-start
  0.0 0.0 copy-start.2
  0.0 1.0 %copy-done.2 = bf16[16,16,128]{2,1,0:T(8,128)(2,1)S(1)} copy-done((bf16[16,16,128]{2,1,0:T(8,128)(2,1)S(1)}, bf16[16,16,128]{2,1,0:T(8,128)(2,1)}, u32[]{:S(2)}) %copy-start.2) | copy-done | bytes 65560
  1.0 0.0 copy-start.5
  1.0 0.7 %copy-done.5 = s32[16,16]{1,0:T(8,128)S(1)} copy-done((s32[16,16]{1,0:T(8,128)S(1)}, s32[16,16]{1,0:T(8,128)}, u32[]{:S(2)}) %copy-start.5) | copy-done | bytes 1048
  1.7 0.0 copy-start.3
  1.7 0.0 copy-start.4
  1.7 0.0 copy-start.6
  1.7 0.3 pack.1
  2.0 4.1 %collective-permute-start = (bf16[1,288,128]{2,1,0:T(8,128)(2,1)S(1)}, bf16[1,288,128]{2,1,0:T(8,128)(2,1)S(1)}, u32[]{:S(2)}, u32[]{:S(2)}) collective-permute-start(bf16[1,288,128]{2,1,0:T(8,128)(2,1)S(1)} %bitcast.4), channel_id=1, source_target_pairs={{0,8},{2,10},{4,12},{6,14},{8,0},{10,2},{12,4},{14,6},{1,9},{3,11}... | collective-permute-start | bytes 221192 | tf_op jit(solution)/shard_map/ppermute | solution.py:279
  6.0 0.0 copy-done.1
  6.1 0.0 copy-done
  6.1 0.0 copy-done.3
  6.1 0.0 copy-done.4
  6.1 0.0 copy-done.6
  6.1 3.2 %decode.3 = (bf16[64,128,128]{2,1,0:T(8,128)(2,1)S(1)}, f32[4096,128]{1,0:T(8,128)S(1)}) custom-call(s32[64,128]{1,0:T(8,128)S(1)} %copy-done.3, s32[64,16,128]{2,1,0:T(8,128)S(1)} %bitcast.7, bf16[64,128]{1,0:T(8,128)(2,1)S(1)} %copy-done.4, bf16[1,4]{1,0:T(2,128)(2,1)S(1)} %bitcast.11, bf16[4096,128]{1,0:T(8,128)(2,1)S(1)} %copy-done), custom_call_target="tpu_custom_call" | custom-call | flops 4800000000 | tf_op jit(solution)/shard_map/decode/pallas_call | solution.py:326
  9.3 0.7 %collective-permute-done = bf16[1,288,128]{2,1,0:T(8,128)(2,1)S(1)} collective-permute-done((bf16[1,288,128]{2,1,0:T(8,128)(2,1)S(1)}, bf16[1,288,128]{2,1,0:T(8,128)(2,1)S(1)}, u32[]{:S(2)}, u32[]{:S(2)}) %collective-permute-start) | collective-permute-done | bytes 73760 | tf_op jit(solution)/shard_map/ppermute | solution.py:279
  10.0 1.0 %collective-permute-start.1 = (bf16[2,288,128]{2,1,0:T(8,128)(2,1)S(1)}, bf16[2,288,128]{2,1,0:T(8,128)(2,1)S(1)}, u32[]{:S(2)}, u32[]{:S(2)}) collective-permute-start(bf16[2,288,128]{2,1,0:T(8,128)(2,1)S(1)} %pad_maximum_fusion.1), channel_id=1, source_target_pairs={{0,4},{2,6},{4,0},{6,2},{8,12},{10,14},{12,8},{14,10},{1,5},{3,7},... | collective-permute-start | bytes 442376 | tf_op jit(solution)/shard_map/ppermute | solution.py:279
  11.0 1.5 %collective-permute-start.4 = (bf16[2,288,128]{2,1,0:T(8,128)(2,1)S(1)}, bf16[2,288,128]{2,1,0:T(8,128)(2,1)S(1)}, u32[]{:S(2)}, u32[]{:S(2)}) collective-permute-start(bf16[2,288,128]{2,1,0:T(8,128)(2,1)S(1)} %pad_maximum_fusion.1), channel_id=1, source_target_pairs={{0,2},{2,0},{4,6},{6,4},{8,10},{10,8},{12,14},{14,12},{1,3},{3,1},... | collective-permute-start | bytes 442376 | tf_op jit(solution)/shard_map/ppermute | solution.py:279
  12.5 2.4 %decode.4.refs_5_ = bf16[64,128,128]{2,1,0:T(8,128)(2,1)S(1)} custom-call(s32[64,128]{1,0:T(8,128)S(1)} %copy-done.3, s32[64,16,128]{2,1,0:T(8,128)S(1)} %bitcast.8, bf16[64,128]{1,0:T(8,128)(2,1)S(1)} %copy-done.4, bf16[1,4]{1,0:T(2,128)(2,1)S(1)} %bitcast.12, f32[4096,128]{1,0:T(8,128)S(1)} %get-tuple-element.19.refs_4_, ...), custom_call_target="tpu_custom_call", output_to_operand_aliasing={{}: (5, {})} | custom-call | flops 3200000000 | tf_op jit(solution)/shard_map/decode/pallas_call | solution.py:326
  14.8 0.3 collective-permute-done.1
  15.2 0.0 copy-start.7
  15.2 1.8 %collective-permute-start.3 = (bf16[2,288,128]{2,1,0:T(8,128)(2,1)S(1)}, bf16[2,288,128]{2,1,0:T(8,128)(2,1)S(1)}, u32[]{:S(2)}, u32[]{:S(2)}) collective-permute-start(bf16[2,288,128]{2,1,0:T(8,128)(2,1)S(1)} %collective-permute-done.1), channel_id=1, source_target_pairs={{0,2},{2,0},{4,6},{6,4},{8,10},{10,8},{12,14},{14,12},{1,3},{3,1},... | collective-permute-start | bytes 442376 | tf_op jit(solution)/shard_map/ppermute | solution.py:279
  17.0 0.0 collective-permute-start.2
  17.0 3.3 %decode.5 = (bf16[64,128,128]{2,1,0:T(8,128)(2,1)S(1)}, s32[16,128]{1,0:T(8,128)S(1)}, s32[64,128]{1,0:T(8,128)S(1)}) custom-call(s32[64,128]{1,0:T(8,128)S(1)} %copy-done.3, s32[64,16,128]{2,1,0:T(8,128)S(1)} %bitcast.9, bf16[64,128]{1,0:T(8,128)(2,1)S(1)} %copy-done.4, bf16[1,4]{1,0:T(2,128)(2,1)S(1)} %bitcast.13, ...), custom_call_target="tpu_custom_call", output_to_operand_aliasing={{0}: (5, {})} | custom-call | flops 4800000000 | tf_op jit(solution)/shard_map/decode/pallas_call | solution.py:326
  20.3 0.0 collective-permute-done.4
  20.3 0.1 collective-permute-done.3
  20.5 0.5 %collective-permute-start.5 = (bf16[4,288,128]{2,1,0:T(8,128)(2,1)S(1)}, bf16[4,288,128]{2,1,0:T(8,128)(2,1)S(1)}, u32[]{:S(2)}, u32[]{:S(2)}) collective-permute-start(bf16[4,288,128]{2,1,0:T(8,128)(2,1)S(1)} %constant_dynamic-update-slice_fusion.refs_0_.mine_ref), channel_id=1, source_target_pairs={{0,1},{1,0},{2,3},{3,2},{4,5},{5,4},{6,7},{7,6},{8,9},{9,8},{10,11... | collective-permute-start | bytes 884744 | tf_op jit(solution)/shard_map/ppermute | solution.py:282
  21.0 0.0 collective-permute-done.2.other_ref
  21.0 0.0 copy-done.7
  21.0 2.1 %pairs.2 = (f32[16,128]{1,0:T(8,128)S(1)}, s32[16,128]{1,0:T(8,128)S(1)}, s32[64,128]{1,0:T(8,128)S(1)}) custom-call(s32[64]{0:T(128)S(1)} %copy-done.7, s32[16,128]{1,0:T(8,128)S(1)} %get-tuple-element.25.slot_ref, s32[64,128]{1,0:T(8,128)S(1)} %get-tuple-element.26.rank_ref, bf16[4,288,128]{2,1,0:T(8,128)(2,1)S(1)} %pad_maximum_fusion.refs_6_.mine_ref, ...), custom_call_target="tpu_custom_call" | custom-call | flops 3000000000 | tf_op jit(solution)/shard_map/pairs/pallas_call | solution.py:355
  23.0 0.0 collective-permute-done.5.other_ref
  23.0 1.9 %pairs.3 = f32[16,128]{1,0:T(8,128)S(1)} custom-call(s32[64]{0:T(128)S(1)} %copy-done.7, s32[16,128]{1,0:T(8,128)S(1)} %get-tuple-element.31.slot_ref, s32[64,128]{1,0:T(8,128)S(1)} %get-tuple-element.32.rank_ref, bf16[4,288,128]{2,1,0:T(8,128)(2,1)S(1)} %constant_dynamic-update-slice_fusion.refs_0_.mine_ref, ...), custom_call_target="tpu_custom_call" | custom-call | flops 3000000000 | tf_op jit(solution)/shard_map/pairs/pallas_call | solution.py:355
  25.0 1.4 %collective-permute-start.6 = (f32[16,64]{1,0:T(8,128)S(1)}, f32[16,64]{1,0:T(8,128)S(1)}, u32[]{:S(2)}, u32[]{:S(2)}) collective-permute-start(f32[16,64]{1,0:T(8,128)S(1)} %bitcast.10), channel_id=1, source_target_pairs={{0,2},{2,0},{4,6},{6,4},{8,10},{10,8},{12,14},{14,12},{1,3},{3,1},... | collective-permute-start | bytes 12296 | tf_op jit(solution)/shard_map/ppermute | solution.py:279
  26.4 2.3 %collective-permute-done.6 = f32[16,64]{1,0:T(8,128)S(1)} collective-permute-done((f32[16,64]{1,0:T(8,128)S(1)}, f32[16,64]{1,0:T(8,128)S(1)}, u32[]{:S(2)}, u32[]{:S(2)}) %collective-permute-start.6) | collective-permute-done | bytes 4128 | tf_op jit(solution)/shard_map/ppermute | solution.py:279
  28.7 0.1 slice.26
  28.8 0.9 %collective-permute-start.7 = (f32[16,32]{1,0:T(8,128)S(1)}, f32[16,32]{1,0:T(8,128)S(1)}, u32[]{:S(2)}, u32[]{:S(2)}) collective-permute-start(f32[16,32]{1,0:T(8,128)S(1)} %slice.26), channel_id=1, source_target_pairs={{0,4},{2,6},{4,0},{6,2},{8,12},{10,14},{12,8},{14,10},{1,5},{3,7},... | collective-permute-start | bytes 6152 | tf_op jit(solution)/shard_map/ppermute | solution.py:279
  29.7 2.7 %collective-permute-done.7 = f32[16,32]{1,0:T(8,128)S(1)} collective-permute-done((f32[16,32]{1,0:T(8,128)S(1)}, f32[16,32]{1,0:T(8,128)S(1)}, u32[]{:S(2)}, u32[]{:S(2)}) %collective-permute-start.7) | collective-permute-done | bytes 2080 | tf_op jit(solution)/shard_map/ppermute | solution.py:279
  32.4 0.1 slice.28
  32.5 2.4 %collective-permute-start.8 = (f32[16,16]{1,0:T(8,128)S(1)}, f32[16,16]{1,0:T(8,128)S(1)}, u32[]{:S(2)}, u32[]{:S(2)}) collective-permute-start(f32[16,16]{1,0:T(8,128)S(1)} %slice.28), channel_id=1, source_target_pairs={{0,8},{2,10},{4,12},{6,14},{8,0},{10,2},{12,4},{14,6},{1,9},{3,11}... | collective-permute-start | bytes 3080 | tf_op jit(solution)/shard_map/ppermute | solution.py:279
  34.9 2.1 %collective-permute-done.8 = f32[16,16]{1,0:T(8,128)S(1)} collective-permute-done((f32[16,16]{1,0:T(8,128)S(1)}, f32[16,16]{1,0:T(8,128)S(1)}, u32[]{:S(2)}, u32[]{:S(2)}) %collective-permute-start.8) | collective-permute-done | bytes 1056 | tf_op jit(solution)/shard_map/ppermute | solution.py:279
  37.0 0.0 collective-permute-start.9
  37.0 1.2 %collective-permute-done.9 = f32[16,16]{1,0:T(8,128)S(1)} collective-permute-done((f32[16,16]{1,0:T(8,128)S(1)}, f32[16,16]{1,0:T(8,128)S(1)}, u32[]{:S(2)}, u32[]{:S(2)}) %collective-permute-start.9) | collective-permute-done | bytes 1056 | tf_op jit(solution)/shard_map/ppermute | solution.py:282
  38.2 0.6 %add.15 = f32[16,16]{1,0:T(8,128)} add(f32[16,16]{1,0:T(8,128)S(1)} %slice_add_fusion, f32[16,16]{1,0:T(8,128)S(1)} %collective-permute-done.9) | non-fusion elementwise | flops 256 | bytes 3072 | tf_op jit(solution)/shard_map/add | solution.py:405
  (7 shorter events, 0.1 us)
Async XLA Ops:
  0.0 6.1 %copy-start.1 = (s32[64,128,16]{1,2,0:T(8,128)S(1)}, s32[64,128,16]{1,2,0:T(8,128)}, u32[]{:S(2)}) copy-start(s32[64,128,16]{1,2,0:T(8,128)} %param.10) | copy-start | bytes 1572868
  0.0 6.1 %copy-start = (bf16[4096,128]{1,0:T(8,128)(2,1)S(1)}, bf16[4096,128]{1,0:T(8,128)(2,1)}, u32[]{:S(2)}) copy-start(bf16[4096,128]{1,0:T(8,128)(2,1)} %refs_4_.1) | copy-start | bytes 3145732
  0.0 1.0 %copy-start.2 = (bf16[16,16,128]{2,1,0:T(8,128)(2,1)S(1)}, bf16[16,16,128]{2,1,0:T(8,128)(2,1)}, u32[]{:S(2)}) copy-start(bf16[16,16,128]{2,1,0:T(8,128)(2,1)} %query_hbm.1) | copy-start | bytes 196612
  1.0 0.7 %copy-start.5 = (s32[16,16]{1,0:T(8,128)S(1)}, s32[16,16]{1,0:T(8,128)}, u32[]{:S(2)}) copy-start(s32[16,16]{1,0:T(8,128)} %cand_hbm.1) | copy-start | bytes 3076
  1.7 4.4 %copy-start.3 = (s32[64,128]{1,0:T(8,128)S(1)}, s32[64,128]{1,0:T(8,128)}, u32[]{:S(2)}) copy-start(s32[64,128]{1,0:T(8,128)} %refs_0_.5) | copy-start | bytes 98308
  1.7 4.4 %copy-start.4 = (bf16[64,128]{1,0:T(8,128)(2,1)S(1)}, bf16[64,128]{1,0:T(8,128)(2,1)}, u32[]{:S(2)}) copy-start(bf16[64,128]{1,0:T(8,128)(2,1)} %refs_2_.5) | copy-start | bytes 49156
  1.7 4.4 %copy-start.6 = (bf16[4]{0:T(256)(128)(2,1)S(1)}, bf16[4]{0:T(256)(128)(2,1)}, u32[]{:S(2)}) copy-start(bf16[4]{0:T(256)(128)(2,1)} %param.15) | copy-start | bytes 28
  2.0 8.0 %collective-permute-start = (bf16[1,288,128]{2,1,0:T(8,128)(2,1)S(1)}, bf16[1,288,128]{2,1,0:T(8,128)(2,1)S(1)}, u32[]{:S(2)}, u32[]{:S(2)}) collective-permute-start(bf16[1,288,128]{2,1,0:T(8,128)(2,1)S(1)} %bitcast.4), channel_id=1, source_target_pairs={{0,8},{2,10},{4,12},{6,14},{8,0},{10,2},{12,4},{14,6},{1,9},{3,11}... | collective-permute-start | bytes 221192 | tf_op jit(solution)/shard_map/ppermute | solution.py:279
  10.0 5.2 %collective-permute-start.1 = (bf16[2,288,128]{2,1,0:T(8,128)(2,1)S(1)}, bf16[2,288,128]{2,1,0:T(8,128)(2,1)S(1)}, u32[]{:S(2)}, u32[]{:S(2)}) collective-permute-start(bf16[2,288,128]{2,1,0:T(8,128)(2,1)S(1)} %pad_maximum_fusion.1), channel_id=1, source_target_pairs={{0,4},{2,6},{4,0},{6,2},{8,12},{10,14},{12,8},{14,10},{1,5},{3,7},... | collective-permute-start | bytes 442376 | tf_op jit(solution)/shard_map/ppermute | solution.py:279
  11.0 9.3 %collective-permute-start.4 = (bf16[2,288,128]{2,1,0:T(8,128)(2,1)S(1)}, bf16[2,288,128]{2,1,0:T(8,128)(2,1)S(1)}, u32[]{:S(2)}, u32[]{:S(2)}) collective-permute-start(bf16[2,288,128]{2,1,0:T(8,128)(2,1)S(1)} %pad_maximum_fusion.1), channel_id=1, source_target_pairs={{0,2},{2,0},{4,6},{6,4},{8,10},{10,8},{12,14},{14,12},{1,3},{3,1},... | collective-permute-start | bytes 442376 | tf_op jit(solution)/shard_map/ppermute | solution.py:279
  15.2 5.7 %copy-start.7 = (s32[64]{0:T(128)S(1)}, s32[64]{0:T(128)}, u32[]{:S(2)}) copy-start(s32[64]{0:T(128)} %len_hbm.3) | copy-start | bytes 772
  15.2 5.2 %collective-permute-start.3 = (bf16[2,288,128]{2,1,0:T(8,128)(2,1)S(1)}, bf16[2,288,128]{2,1,0:T(8,128)(2,1)S(1)}, u32[]{:S(2)}, u32[]{:S(2)}) collective-permute-start(bf16[2,288,128]{2,1,0:T(8,128)(2,1)S(1)} %collective-permute-done.1), channel_id=1, source_target_pairs={{0,2},{2,0},{4,6},{6,4},{8,10},{10,8},{12,14},{14,12},{1,3},{3,1},... | collective-permute-start | bytes 442376 | tf_op jit(solution)/shard_map/ppermute | solution.py:279
  17.0 3.9 %collective-permute-start.2 = (bf16[4,288,128]{2,1,0:T(8,128)(2,1)S(1)}, bf16[4,288,128]{2,1,0:T(8,128)(2,1)S(1)}, u32[]{:S(2)}, u32[]{:S(2)}) collective-permute-start(bf16[4,288,128]{2,1,0:T(8,128)(2,1)S(1)} %pad_maximum_fusion.refs_6_.mine_ref), channel_id=1, source_target_pairs={{0,1},{1,0},{2,3},{3,2},{4,5},{5,4},{6,7},{7,6},{8,9},{9,8},{10,11... | collective-permute-start | bytes 884744 | tf_op jit(solution)/shard_map/ppermute | solution.py:282
  20.5 2.6 %collective-permute-start.5 = (bf16[4,288,128]{2,1,0:T(8,128)(2,1)S(1)}, bf16[4,288,128]{2,1,0:T(8,128)(2,1)S(1)}, u32[]{:S(2)}, u32[]{:S(2)}) collective-permute-start(bf16[4,288,128]{2,1,0:T(8,128)(2,1)S(1)} %constant_dynamic-update-slice_fusion.refs_0_.mine_ref), channel_id=1, source_target_pairs={{0,1},{1,0},{2,3},{3,2},{4,5},{5,4},{6,7},{7,6},{8,9},{9,8},{10,11... | collective-permute-start | bytes 884744 | tf_op jit(solution)/shard_map/ppermute | solution.py:282
  25.0 3.7 %collective-permute-start.6 = (f32[16,64]{1,0:T(8,128)S(1)}, f32[16,64]{1,0:T(8,128)S(1)}, u32[]{:S(2)}, u32[]{:S(2)}) collective-permute-start(f32[16,64]{1,0:T(8,128)S(1)} %bitcast.10), channel_id=1, source_target_pairs={{0,2},{2,0},{4,6},{6,4},{8,10},{10,8},{12,14},{14,12},{1,3},{3,1},... | collective-permute-start | bytes 12296 | tf_op jit(solution)/shard_map/ppermute | solution.py:279
  28.8 3.7 %collective-permute-start.7 = (f32[16,32]{1,0:T(8,128)S(1)}, f32[16,32]{1,0:T(8,128)S(1)}, u32[]{:S(2)}, u32[]{:S(2)}) collective-permute-start(f32[16,32]{1,0:T(8,128)S(1)} %slice.26), channel_id=1, source_target_pairs={{0,4},{2,6},{4,0},{6,2},{8,12},{10,14},{12,8},{14,10},{1,5},{3,7},... | collective-permute-start | bytes 6152 | tf_op jit(solution)/shard_map/ppermute | solution.py:279
  32.5 4.6 %collective-permute-start.8 = (f32[16,16]{1,0:T(8,128)S(1)}, f32[16,16]{1,0:T(8,128)S(1)}, u32[]{:S(2)}, u32[]{:S(2)}) collective-permute-start(f32[16,16]{1,0:T(8,128)S(1)} %slice.28), channel_id=1, source_target_pairs={{0,8},{2,10},{4,12},{6,14},{8,0},{10,2},{12,4},{14,6},{1,9},{3,11}... | collective-permute-start | bytes 3080 | tf_op jit(solution)/shard_map/ppermute | solution.py:279
  37.0 1.2 %collective-permute-start.9 = (f32[16,16]{1,0:T(8,128)S(1)}, f32[16,16]{1,0:T(8,128)S(1)}, u32[]{:S(2)}, u32[]{:S(2)}) collective-permute-start(f32[16,16]{1,0:T(8,128)S(1)} %slice_add_fusion), channel_id=1, source_target_pairs={{0,1},{1,0},{2,3},{3,2},{4,5},{5,4},{6,7},{7,6},{8,9},{9,8},{10,11... | collective-permute-start | bytes 3080 | tf_op jit(solution)/shard_map/ppermute | solution.py:282

commit v6 on v5

--- a/solution.py
+++ b/solution.py
@@ -42,7 +42,6 @@
     per = width // words
     order = ones_where(iota((width, width), 0) == spread(iota((width, width), 1), words, per))
     picks = cand_ref.shape[1]
-    repeat = ones_where(iota((picks, width), 0) == iota((picks, width), 1) % picks)
     for c in copies:
         c.wait()
     flat = query_ref[...].reshape(count * tokens, width)
@@ -51,28 +50,29 @@
     ids = cand_ref[...]
     owner = ids // passages
     local = ids - owner * passages
+    row = iota((picks, width), 0)
+    lane = iota((picks, width), 1)
+    tile = jnp.zeros((count, width), jnp.float32)
     for i, part in enumerate((owner, local)):
-        part = part.astype(jnp.float32).astype(jnp.bfloat16)
-        out_ref[rows + i * count : rows + (i + 1) * count, :] = dot(part, repeat).astype(jnp.bfloat16)
+        place = ones_where(lane == row + i * picks)
+        tile += dot(part.astype(jnp.float32).astype(jnp.bfloat16), place)
+    out_ref[rows : rows + count, :] = tile.astype(jnp.bfloat16)
 
 
 def slot_kernel(queries, picks, capacity, rows_ref, slot_ref, rank_ref):
     blocks = rows_ref.shape[0]
     width = rows_ref.shape[2]
-    body_rows = rows_ref.shape[1] - 2 * queries
+    body_rows = rows_ref.shape[1] - queries
     groups = width // picks
     rows = blocks * queries
     me = lax.axis_index("shard") * lax.axis_size("sub") + lax.axis_index("sub")
-    owner = rows_ref[:, body_rows : body_rows + queries, :].reshape(rows, width).astype(jnp.float32)
-    local = (
-        rows_ref[:, body_rows + queries : body_rows + 2 * queries, :]
-        .reshape(rows, width)
-        .astype(jnp.float32)
-    )
+    ids = rows_ref[:, body_rows:, :].reshape(rows, width)
+    li = iota((width, width), 0)
+    lj = iota((width, width), 1)
+    owner = dot(ids, ones_where(li == lj % picks))
+    local = dot(ids, ones_where(li == picks + lj % picks))
     here = owner == jnp.full((rows, width), me, jnp.int32).astype(jnp.float32)
     here_bf = ones_where(here)
-    li = iota((width, width), 0)
-    lj = iota((width, width), 1)
     before_lane = ones_where((li < picks) & (li < lj % picks))
     whole_row = ones_where(li < picks)
     ri = iota((rows, rows), 0)
@@ -102,7 +102,7 @@
 WIDE = 4
 
 
-def decode_kernel(first, find, start, stop, *refs):
+def decode_kernel(first, start, stop, *refs):
     refs = list(refs)
     ids_all, words_ref, scale_bf, bucket_ref = refs[:4]
     del refs[:4]
@@ -111,14 +111,9 @@
     else:
         wide = refs.pop(0)
         refs.pop(0)
-    if find is not None:
-        near_ref = refs.pop(0)
     out_ref = refs.pop(0)
     if first:
         wide = refs.pop(0)
-    if find is not None:
-        slot_ref, rank_ref = refs[:2]
-        del refs[:2]
     rows, ids_ref, scale_ref, sem = refs
     copy = pltpu.make_async_copy(ids_all.at[pl.ds(start, stop - start)], ids_ref, sem)
     copy.start()
@@ -132,8 +127,6 @@
             return 0
 
         lax.fori_loop(0, table_ref.shape[0] // chunk, widen, 0)
-    if find is not None:
-        slot_kernel(*find, near_ref, slot_ref, rank_ref)
     copy.wait()
     slots = ids_ref.shape[1]
     width = wide.shape[1]
@@ -216,7 +209,7 @@
         c.wait()
     blocks = mine_ref.shape[0]
     width = mine_ref.shape[2]
-    tokens = (mine_ref.shape[1] - 2 * queries) // queries
+    tokens = (mine_ref.shape[1] - queries) // queries
     padded = slot_s.shape[0] // 2
     full_tokens = 2 * tokens
     slots = emb_ref.shape[2]
@@ -283,7 +276,7 @@
 
     payload = pl.pallas_call(
         functools.partial(pack_kernel, words, passages),
-        out_shape=jax.ShapeDtypeStruct((query_count * (tokens + 2), width), jnp.bfloat16),
+        out_shape=jax.ShapeDtypeStruct((query_count * (tokens + 1), width), jnp.bfloat16),
         in_specs=whole(2, pltpu.HBM),
         out_specs=pl.BlockSpec(memory_space=VMEM),
         scratch_shapes=[
@@ -312,19 +305,13 @@
             jax.ShapeDtypeStruct((blocks * query_count, width), jnp.int32),
         )
 
-    def decode(start, stop, wide, embedded, near=None):
+    def decode(start, stop, wide, embedded):
         first = embedded is None
         extra = (centroids,) if first else (wide, embedded)
         outs = (emb_shape, wide_shape) if first else (emb_shape,)
         specs = whole(4 + len(extra), VMEM)
-        find = None
-        if near is not None:
-            find = (query_count, picks, capacity)
-            extra += (near,)
-            outs += slot_shapes(near.shape[0])
-            specs += whole(1, VMEM)
         out = pl.pallas_call(
-            functools.partial(decode_kernel, first, find, start, stop),
+            functools.partial(decode_kernel, first, start, stop),
             out_shape=outs,
             in_specs=specs,
             out_specs=(pl.BlockSpec(memory_space=VMEM),) * len(outs),
@@ -341,7 +328,18 @@
             ),
             name="decode",
         )(*stored, *extra)
-        return (out[0], out[1] if first else wide) + tuple(out[2 if first else 1 :])
+        return out[0], out[1] if first else wide
+
+    def find(mine):
+        return pl.pallas_call(
+            functools.partial(slot_kernel, query_count, picks, capacity),
+            out_shape=slot_shapes(mine.shape[0]),
+            in_specs=whole(1, VMEM),
+            out_specs=(pl.BlockSpec(memory_space=VMEM),) * 2,
+            compiler_params=LIMIT,
+            cost_estimate=pl.CostEstimate(flops=10**9, bytes_accessed=0, transcendentals=0),
+            name="slots",
+        )(mine)
 
     def score(found, mine, other, later=None):
         blocks = mine.shape[0]
@@ -377,7 +375,7 @@
     unit = 2 * WIDE
     units = passages // unit
     parts = len(steps)
-    cuts = [(2 * units * i + parts) // (2 * parts) * unit for i in range(parts + 1)]
+    cuts = [0] + [units * (i + 2) // (parts + 1) * unit for i in range(parts)]
     held = payload[None]
     wide = embedded = None
     for i, d in enumerate(steps[:-2]):
@@ -393,11 +391,12 @@
         moved, embedded = lax.optimization_barrier((moved, embedded))
     far_b = swap_shard(moved, 1)
     near = jnp.concatenate([held, moved], axis=0)
-    embedded, wide, *near_found = decode(cuts[-2], cuts[-1], wide, embedded, near)
+    near_other = swap_sub(near)
+    embedded, wide = decode(cuts[-2], cuts[-1], wide, embedded)
     far_b, embedded = lax.optimization_barrier((far_b, embedded))
     far = jnp.concatenate([far_a, far_b], axis=0)
-    near_scores, far_found = score(near_found, near, swap_sub(near), far)
-    far_scores, _ = score(far_found, far, swap_sub(far))
+    far_scores, near_found = score(find(far), far, swap_sub(far), near)
+    near_scores, _ = score(near_found, near, near_other)
     total = near_scores + swap_shard(far_scores, 1)
     for d in reversed(steps[:-1]):
         half = total.shape[1] // 2

time: 39 us -> 38.6 us (0.990)
  waiting for transfers between devices: 9.46 us -> 8.25 us
  Pallas kernels: 13.1 us -> 13.9 us
    ppermute x7, waiting for transfers between devices: 8.28 us -> 7.01 us  [swap_shard(): return lax.ppermute(x, 'shard', [(i, i ^ d) for i in range(shards)])]
    pallas_call x3 -> x4, Pallas kernels: 8.84 us -> 9.54 us  [the longest x3 8.66 us: decode(): pl.pallas_call(functools.partial(decode_kernel, first, start, stop), out_...]
  transfers between devices with their start and end apart: 10 -> 10, of which waited for: 7 -> 6; matrix products, arithmetic and copies ran while one was open for 0% -> 0% of each run, Pallas kernels for 28% -> 35%
where the time goes in v6:
time: 38.6 us; the launch traced here: 38.4 us
  Pallas kernels  13.9 us (36%)
  starting transfers between devices  13.6 us (35%)
  waiting for transfers between devices  8.25 us (21%)
  local copies, waits for them, and re-layouts  1.86 us (5%)
  other arithmetic  0.66 us (2%)
    ppermute x7, starting transfers between devices, swap_shard(): return lax.ppermute(x, 'shard', [(i, i ^ d) for i in range(shards)])  13 us
    pallas_call x3, Pallas kernels, decode(): pl.pallas_call(functools.partial(decode_kernel, first, start, stop), out_...  8.66 us
    ppermute x7, waiting for transfers between devices, swap_shard(): return lax.ppermute(x, 'shard', [(i, i ^ d) for i in range(shards)])  7.01 us
    pallas_call x2, Pallas kernels, score(): pl.pallas_call(functools.partial(pair_kernel, query_count, picks, capacit...  4.06 us
    unnamed x17, local copies, waits for them, and re-layouts  1.69 us
    ppermute x3, waiting for transfers between devices, swap_sub(): return lax.ppermute(x, 'sub', [(i, i ^ 1) for i in range(halves)])  1.24 us
    pallas_call x1, Pallas kernels, find(): pl.pallas_call(functools.partial(slot_kernel, query_count, picks, capacit...  0.88 us
  transfers between devices with their start and end apart: 10, of which 6 were waited for; matrix products, arithmetic and copies ran while one was open for 0% of the time, Pallas kernels for 35%

profile of v6, /device:TPU:0, one launch (start us, length us, event | category | flops | bytes accessed | tf_op | source)
XLA Modules:
  0.0 38.4 jit_solution(5684365316612528373)
XLA Ops:
  0.0 0.0 copy-start
  0.0 0.0 copy-start.1
  0.0 0.0 copy-start.2
  0.0 1.0 %copy-done.2 = bf16[16,16,128]{2,1,0:T(8,128)(2,1)S(1)} copy-done((bf16[16,16,128]{2,1,0:T(8,128)(2,1)S(1)}, bf16[16,16,128]{2,1,0:T(8,128)(2,1)}, u32[]{:S(2)}) %copy-start.2) | copy-done | bytes 65560
  1.0 0.0 copy-start.5
  1.0 0.7 %copy-done.5 = s32[16,16]{1,0:T(8,128)S(1)} copy-done((s32[16,16]{1,0:T(8,128)S(1)}, s32[16,16]{1,0:T(8,128)}, u32[]{:S(2)}) %copy-start.5) | copy-done | bytes 1048
  1.7 0.0 copy-start.3
  1.7 0.0 copy-start.4
  1.7 0.0 copy-start.6
  1.7 0.3 pack.1
  2.0 4.1 %collective-permute-start = (bf16[1,272,128]{2,1,0:T(8,128)(2,1)S(1)}, bf16[1,272,128]{2,1,0:T(8,128)(2,1)S(1)}, u32[]{:S(2)}, u32[]{:S(2)}) collective-permute-start(bf16[1,272,128]{2,1,0:T(8,128)(2,1)S(1)} %bitcast.4), channel_id=1, source_target_pairs={{0,8},{2,10},{4,12},{6,14},{8,0},{10,2},{12,4},{14,6},{1,9},{3,11}... | collective-permute-start | bytes 208904 | tf_op jit(solution)/shard_map/ppermute | solution.py:272
  6.1 0.0 copy-done
  6.1 0.0 copy-done.1
  6.1 0.0 copy-done.3
  6.1 0.0 copy-done.4
  6.1 0.0 copy-done.6
  6.1 4.0 %decode.3 = (bf16[64,128,128]{2,1,0:T(8,128)(2,1)S(1)}, f32[4096,128]{1,0:T(8,128)S(1)}) custom-call(s32[64,128]{1,0:T(8,128)S(1)} %copy-done.3, s32[64,16,128]{2,1,0:T(8,128)S(1)} %bitcast.7, bf16[64,128]{1,0:T(8,128)(2,1)S(1)} %copy-done.4, bf16[1,4]{1,0:T(2,128)(2,1)S(1)} %bitcast.11, bf16[4096,128]{1,0:T(8,128)(2,1)S(1)} %copy-done), custom_call_target="tpu_custom_call" | custom-call | flops 6400000000 | tf_op jit(solution)/shard_map/decode/pallas_call | solution.py:313
  10.0 0.0 collective-permute-done
  10.1 1.6 %collective-permute-start.2 = (bf16[2,272,128]{2,1,0:T(8,128)(2,1)S(1)}, bf16[2,272,128]{2,1,0:T(8,128)(2,1)S(1)}, u32[]{:S(2)}, u32[]{:S(2)}) collective-permute-start(bf16[2,272,128]{2,1,0:T(8,128)(2,1)S(1)} %pad_maximum_fusion.1), channel_id=1, source_target_pairs={{0,4},{2,6},{4,0},{6,2},{8,12},{10,14},{12,8},{14,10},{1,5},{3,7},... | collective-permute-start | bytes 417800 | tf_op jit(solution)/shard_map/ppermute | solution.py:272
  11.7 1.5 %collective-permute-start.1 = (bf16[2,272,128]{2,1,0:T(8,128)(2,1)S(1)}, bf16[2,272,128]{2,1,0:T(8,128)(2,1)S(1)}, u32[]{:S(2)}, u32[]{:S(2)}) collective-permute-start(bf16[2,272,128]{2,1,0:T(8,128)(2,1)S(1)} %pad_maximum_fusion.1), channel_id=1, source_target_pairs={{0,2},{2,0},{4,6},{6,4},{8,10},{10,8},{12,14},{14,12},{1,3},{3,1},... | collective-permute-start | bytes 417800 | tf_op jit(solution)/shard_map/ppermute | solution.py:272
  13.2 2.4 %decode.4.refs_5_ = bf16[64,128,128]{2,1,0:T(8,128)(2,1)S(1)} custom-call(s32[64,128]{1,0:T(8,128)S(1)} %copy-done.3, s32[64,16,128]{2,1,0:T(8,128)S(1)} %bitcast.8, bf16[64,128]{1,0:T(8,128)(2,1)S(1)} %copy-done.4, bf16[1,4]{1,0:T(2,128)(2,1)S(1)} %bitcast.12, f32[4096,128]{1,0:T(8,128)S(1)} %get-tuple-element.20.refs_4_, ...), custom_call_target="tpu_custom_call", output_to_operand_aliasing={{}: (5, {})} | custom-call | flops 3200000000 | tf_op jit(solution)/shard_map/decode/pallas_call | solution.py:313
  15.6 0.0 collective-permute-done.2
  15.6 1.2 %collective-permute-start.3 = (bf16[2,272,128]{2,1,0:T(8,128)(2,1)S(1)}, bf16[2,272,128]{2,1,0:T(8,128)(2,1)S(1)}, u32[]{:S(2)}, u32[]{:S(2)}) collective-permute-start(bf16[2,272,128]{2,1,0:T(8,128)(2,1)S(1)} %collective-permute-done.2), channel_id=1, source_target_pairs={{0,2},{2,0},{4,6},{6,4},{8,10},{10,8},{12,14},{14,12},{1,3},{3,1},... | collective-permute-start | bytes 417800 | tf_op jit(solution)/shard_map/ppermute | solution.py:272
  16.8 2.3 %decode.5.emb_ref = bf16[64,128,128]{2,1,0:T(8,128)(2,1)S(1)} custom-call(s32[64,128]{1,0:T(8,128)S(1)} %copy-done.3, s32[64,16,128]{2,1,0:T(8,128)S(1)} %bitcast.9, bf16[64,128]{1,0:T(8,128)(2,1)S(1)} %copy-done.4, bf16[1,4]{1,0:T(2,128)(2,1)S(1)} %bitcast.13, f32[4096,128]{1,0:T(8,128)S(1)} %get-tuple-element.20.refs_4_, ...), custom_call_target="tpu_custom_call", output_to_operand_aliasing={{}: (5, {})} | custom-call | flops 3200000000 | tf_op jit(solution)/shard_map/decode/pallas_call | solution.py:313
  19.1 0.0 collective-permute-done.1
  19.2 1.5 %collective-permute-done.3 = bf16[2,272,128]{2,1,0:T(8,128)(2,1)S(1)} collective-permute-done((bf16[2,272,128]{2,1,0:T(8,128)(2,1)S(1)}, bf16[2,272,128]{2,1,0:T(8,128)(2,1)S(1)}, u32[]{:S(2)}, u32[]{:S(2)}) %collective-permute-start.3) | collective-permute-done | bytes 139296 | tf_op jit(solution)/shard_map/ppermute | solution.py:272
  20.7 0.0 copy-start.7
  20.8 0.1 collective-permute-start.4
  20.9 0.6 %collective-permute-start.5 = (bf16[4,272,128]{2,1,0:T(8,128)(2,1)S(1)}, bf16[4,272,128]{2,1,0:T(8,128)(2,1)S(1)}, u32[]{:S(2)}, u32[]{:S(2)}) collective-permute-start(bf16[4,272,128]{2,1,0:T(8,128)(2,1)S(1)} %pad_maximum_fusion.refs_0_.mine_ref), channel_id=1, source_target_pairs={{0,1},{1,0},{2,3},{3,2},{4,5},{5,4},{6,7},{7,6},{8,9},{9,8},{10,11... | collective-permute-start | bytes 835592 | tf_op jit(solution)/shard_map/ppermute | solution.py:275
  21.4 0.9 %slots.1 = (s32[16,128]{1,0:T(8,128)S(1)}, s32[64,128]{1,0:T(8,128)S(1)}) custom-call(bf16[4,272,128]{2,1,0:T(8,128)(2,1)S(1)} %constant_dynamic-update-slice_fusion.rows_ref.mine_ref), custom_call_target="tpu_custom_call" | custom-call | flops 1000000000 | tf_op jit(solution)/shard_map/slots/pallas_call | solution.py:334
  22.3 0.1 collective-permute-done.4.other_ref
  22.4 0.0 copy-done.7
  22.4 2.2 %pairs.2 = (f32[16,128]{1,0:T(8,128)S(1)}, s32[16,128]{1,0:T(8,128)S(1)}, s32[64,128]{1,0:T(8,128)S(1)}) custom-call(s32[64]{0:T(128)S(1)} %copy-done.7, s32[16,128]{1,0:T(8,128)S(1)} %get-tuple-element.25.slot_ref, s32[64,128]{1,0:T(8,128)S(1)} %get-tuple-element.26.rank_ref, bf16[4,272,128]{2,1,0:T(8,128)(2,1)S(1)} %constant_dynamic-update-slice_fusion.rows_ref.mine_ref, ...), custom_call_target="tpu_custom_call" | custom-call | flops 3000000000 | tf_op jit(solution)/shard_map/pairs/pallas_call | solution.py:353
  24.6 1.2 %collective-permute-start.6 = (f32[16,64]{1,0:T(8,128)S(1)}, f32[16,64]{1,0:T(8,128)S(1)}, u32[]{:S(2)}, u32[]{:S(2)}) collective-permute-start(f32[16,64]{1,0:T(8,128)S(1)} %bitcast.10), channel_id=1, source_target_pairs={{0,2},{2,0},{4,6},{6,4},{8,10},{10,8},{12,14},{14,12},{1,3},{3,1},... | collective-permute-start | bytes 12296 | tf_op jit(solution)/shard_map/ppermute | solution.py:272
  25.8 0.0 collective-permute-done.5.other_ref
  25.8 1.9 %pairs.3 = f32[16,128]{1,0:T(8,128)S(1)} custom-call(s32[64]{0:T(128)S(1)} %copy-done.7, s32[16,128]{1,0:T(8,128)S(1)} %get-tuple-element.28.slot_ref, s32[64,128]{1,0:T(8,128)S(1)} %get-tuple-element.29.rank_ref, bf16[4,272,128]{2,1,0:T(8,128)(2,1)S(1)} %pad_maximum_fusion.refs_0_.mine_ref, bf16[4,272,128]{2,1,0:T(8,128)(2,1)S(1)} %collective-permute-done.5.other_ref, ...), custom_call_target="tpu_custom_call" | custom-call | flops 3000000000 | tf_op jit(solution)/shard_map/pairs/pallas_call | solution.py:353
  27.7 0.6 %collective-permute-done.6 = f32[16,64]{1,0:T(8,128)S(1)} collective-permute-done((f32[16,64]{1,0:T(8,128)S(1)}, f32[16,64]{1,0:T(8,128)S(1)}, u32[]{:S(2)}, u32[]{:S(2)}) %collective-permute-start.6) | collective-permute-done | bytes 4128 | tf_op jit(solution)/shard_map/ppermute | solution.py:272
  28.3 0.1 slice.26
  28.4 1.2 %collective-permute-start.7 = (f32[16,32]{1,0:T(8,128)S(1)}, f32[16,32]{1,0:T(8,128)S(1)}, u32[]{:S(2)}, u32[]{:S(2)}) collective-permute-start(f32[16,32]{1,0:T(8,128)S(1)} %slice.26), channel_id=1, source_target_pairs={{0,4},{2,6},{4,0},{6,2},{8,12},{10,14},{12,8},{14,10},{1,5},{3,7},... | collective-permute-start | bytes 6152 | tf_op jit(solution)/shard_map/ppermute | solution.py:272
  29.5 2.5 %collective-permute-done.7 = f32[16,32]{1,0:T(8,128)S(1)} collective-permute-done((f32[16,32]{1,0:T(8,128)S(1)}, f32[16,32]{1,0:T(8,128)S(1)}, u32[]{:S(2)}, u32[]{:S(2)}) %collective-permute-start.7) | collective-permute-done | bytes 2080 | tf_op jit(solution)/shard_map/ppermute | solution.py:272
  32.0 0.1 slice.28
  32.1 2.2 %collective-permute-start.8 = (f32[16,16]{1,0:T(8,128)S(1)}, f32[16,16]{1,0:T(8,128)S(1)}, u32[]{:S(2)}, u32[]{:S(2)}) collective-permute-start(f32[16,16]{1,0:T(8,128)S(1)} %slice.28), channel_id=1, source_target_pairs={{0,8},{2,10},{4,12},{6,14},{8,0},{10,2},{12,4},{14,6},{1,9},{3,11}... | collective-permute-start | bytes 3080 | tf_op jit(solution)/shard_map/ppermute | solution.py:272
  34.3 2.3 %collective-permute-done.8 = f32[16,16]{1,0:T(8,128)S(1)} collective-permute-done((f32[16,16]{1,0:T(8,128)S(1)}, f32[16,16]{1,0:T(8,128)S(1)}, u32[]{:S(2)}, u32[]{:S(2)}) %collective-permute-start.8) | collective-permute-done | bytes 1056 | tf_op jit(solution)/shard_map/ppermute | solution.py:272
  36.7 0.0 collective-permute-start.9
  36.7 1.2 %collective-permute-done.9 = f32[16,16]{1,0:T(8,128)S(1)} collective-permute-done((f32[16,16]{1,0:T(8,128)S(1)}, f32[16,16]{1,0:T(8,128)S(1)}, u32[]{:S(2)}, u32[]{:S(2)}) %collective-permute-start.9) | collective-permute-done | bytes 1056 | tf_op jit(solution)/shard_map/ppermute | solution.py:275
  37.8 0.6 %add.15 = f32[16,16]{1,0:T(8,128)} add(f32[16,16]{1,0:T(8,128)S(1)} %slice_add_fusion, f32[16,16]{1,0:T(8,128)S(1)} %collective-permute-done.9) | non-fusion elementwise | flops 256 | bytes 3072 | tf_op jit(solution)/shard_map/add | solution.py:404
  (7 shorter events, 0.1 us)
Async XLA Ops:
  0.0 6.1 %copy-start = (bf16[4096,128]{1,0:T(8,128)(2,1)S(1)}, bf16[4096,128]{1,0:T(8,128)(2,1)}, u32[]{:S(2)}) copy-start(bf16[4096,128]{1,0:T(8,128)(2,1)} %refs_4_.1) | copy-start | bytes 3145732
  0.0 6.1 %copy-start.1 = (s32[64,128,16]{1,2,0:T(8,128)S(1)}, s32[64,128,16]{1,2,0:T(8,128)}, u32[]{:S(2)}) copy-start(s32[64,128,16]{1,2,0:T(8,128)} %param.10) | copy-start | bytes 1572868
  0.0 1.0 %copy-start.2 = (bf16[16,16,128]{2,1,0:T(8,128)(2,1)S(1)}, bf16[16,16,128]{2,1,0:T(8,128)(2,1)}, u32[]{:S(2)}) copy-start(bf16[16,16,128]{2,1,0:T(8,128)(2,1)} %query_hbm.1) | copy-start | bytes 196612
  1.0 0.7 %copy-start.5 = (s32[16,16]{1,0:T(8,128)S(1)}, s32[16,16]{1,0:T(8,128)}, u32[]{:S(2)}) copy-start(s32[16,16]{1,0:T(8,128)} %cand_hbm.1) | copy-start | bytes 3076
  1.7 4.4 %copy-start.3 = (s32[64,128]{1,0:T(8,128)S(1)}, s32[64,128]{1,0:T(8,128)}, u32[]{:S(2)}) copy-start(s32[64,128]{1,0:T(8,128)} %refs_0_.5) | copy-start | bytes 98308
  1.7 4.4 %copy-start.4 = (bf16[64,128]{1,0:T(8,128)(2,1)S(1)}, bf16[64,128]{1,0:T(8,128)(2,1)}, u32[]{:S(2)}) copy-start(bf16[64,128]{1,0:T(8,128)(2,1)} %refs_2_.5) | copy-start | bytes 49156
  1.7 4.4 %copy-start.6 = (bf16[4]{0:T(256)(128)(2,1)S(1)}, bf16[4]{0:T(256)(128)(2,1)}, u32[]{:S(2)}) copy-start(bf16[4]{0:T(256)(128)(2,1)} %param.15) | copy-start | bytes 28
  2.0 8.1 %collective-permute-start = (bf16[1,272,128]{2,1,0:T(8,128)(2,1)S(1)}, bf16[1,272,128]{2,1,0:T(8,128)(2,1)S(1)}, u32[]{:S(2)}, u32[]{:S(2)}) collective-permute-start(bf16[1,272,128]{2,1,0:T(8,128)(2,1)S(1)} %bitcast.4), channel_id=1, source_target_pairs={{0,8},{2,10},{4,12},{6,14},{8,0},{10,2},{12,4},{14,6},{1,9},{3,11}... | collective-permute-start | bytes 208904 | tf_op jit(solution)/shard_map/ppermute | solution.py:272
  10.1 5.5 %collective-permute-start.2 = (bf16[2,272,128]{2,1,0:T(8,128)(2,1)S(1)}, bf16[2,272,128]{2,1,0:T(8,128)(2,1)S(1)}, u32[]{:S(2)}, u32[]{:S(2)}) collective-permute-start(bf16[2,272,128]{2,1,0:T(8,128)(2,1)S(1)} %pad_maximum_fusion.1), channel_id=1, source_target_pairs={{0,4},{2,6},{4,0},{6,2},{8,12},{10,14},{12,8},{14,10},{1,5},{3,7},... | collective-permute-start | bytes 417800 | tf_op jit(solution)/shard_map/ppermute | solution.py:272
  11.7 7.4 %collective-permute-start.1 = (bf16[2,272,128]{2,1,0:T(8,128)(2,1)S(1)}, bf16[2,272,128]{2,1,0:T(8,128)(2,1)S(1)}, u32[]{:S(2)}, u32[]{:S(2)}) collective-permute-start(bf16[2,272,128]{2,1,0:T(8,128)(2,1)S(1)} %pad_maximum_fusion.1), channel_id=1, source_target_pairs={{0,2},{2,0},{4,6},{6,4},{8,10},{10,8},{12,14},{14,12},{1,3},{3,1},... | collective-permute-start | bytes 417800 | tf_op jit(solution)/shard_map/ppermute | solution.py:272
  15.6 5.1 %collective-permute-start.3 = (bf16[2,272,128]{2,1,0:T(8,128)(2,1)S(1)}, bf16[2,272,128]{2,1,0:T(8,128)(2,1)S(1)}, u32[]{:S(2)}, u32[]{:S(2)}) collective-permute-start(bf16[2,272,128]{2,1,0:T(8,128)(2,1)S(1)} %collective-permute-done.2), channel_id=1, source_target_pairs={{0,2},{2,0},{4,6},{6,4},{8,10},{10,8},{12,14},{14,12},{1,3},{3,1},... | collective-permute-start | bytes 417800 | tf_op jit(solution)/shard_map/ppermute | solution.py:272
  20.7 1.6 %copy-start.7 = (s32[64]{0:T(128)S(1)}, s32[64]{0:T(128)}, u32[]{:S(2)}) copy-start(s32[64]{0:T(128)} %len_hbm.3) | copy-start | bytes 772
  20.8 1.6 %collective-permute-start.4 = (bf16[4,272,128]{2,1,0:T(8,128)(2,1)S(1)}, bf16[4,272,128]{2,1,0:T(8,128)(2,1)S(1)}, u32[]{:S(2)}, u32[]{:S(2)}) collective-permute-start(bf16[4,272,128]{2,1,0:T(8,128)(2,1)S(1)} %constant_dynamic-update-slice_fusion.rows_ref.mine_ref), channel_id=1, source_target_pairs={{0,1},{1,0},{2,3},{3,2},{4,5},{5,4},{6,7},{7,6},{8,9},{9,8},{10,11... | collective-permute-start | bytes 835592 | tf_op jit(solution)/shard_map/ppermute | solution.py:275
  20.9 4.9 %collective-permute-start.5 = (bf16[4,272,128]{2,1,0:T(8,128)(2,1)S(1)}, bf16[4,272,128]{2,1,0:T(8,128)(2,1)S(1)}, u32[]{:S(2)}, u32[]{:S(2)}) collective-permute-start(bf16[4,272,128]{2,1,0:T(8,128)(2,1)S(1)} %pad_maximum_fusion.refs_0_.mine_ref), channel_id=1, source_target_pairs={{0,1},{1,0},{2,3},{3,2},{4,5},{5,4},{6,7},{7,6},{8,9},{9,8},{10,11... | collective-permute-start | bytes 835592 | tf_op jit(solution)/shard_map/ppermute | solution.py:275
  24.6 3.7 %collective-permute-start.6 = (f32[16,64]{1,0:T(8,128)S(1)}, f32[16,64]{1,0:T(8,128)S(1)}, u32[]{:S(2)}, u32[]{:S(2)}) collective-permute-start(f32[16,64]{1,0:T(8,128)S(1)} %bitcast.10), channel_id=1, source_target_pairs={{0,2},{2,0},{4,6},{6,4},{8,10},{10,8},{12,14},{14,12},{1,3},{3,1},... | collective-permute-start | bytes 12296 | tf_op jit(solution)/shard_map/ppermute | solution.py:272
  28.4 3.7 %collective-permute-start.7 = (f32[16,32]{1,0:T(8,128)S(1)}, f32[16,32]{1,0:T(8,128)S(1)}, u32[]{:S(2)}, u32[]{:S(2)}) collective-permute-start(f32[16,32]{1,0:T(8,128)S(1)} %slice.26), channel_id=1, source_target_pairs={{0,4},{2,6},{4,0},{6,2},{8,12},{10,14},{12,8},{14,10},{1,5},{3,7},... | collective-permute-start | bytes 6152 | tf_op jit(solution)/shard_map/ppermute | solution.py:272
  32.1 4.6 %collective-permute-start.8 = (f32[16,16]{1,0:T(8,128)S(1)}, f32[16,16]{1,0:T(8,128)S(1)}, u32[]{:S(2)}, u32[]{:S(2)}) collective-permute-start(f32[16,16]{1,0:T(8,128)S(1)} %slice.28), channel_id=1, source_target_pairs={{0,8},{2,10},{4,12},{6,14},{8,0},{10,2},{12,4},{14,6},{1,9},{3,11}... | collective-permute-start | bytes 3080 | tf_op jit(solution)/shard_map/ppermute | solution.py:272
  36.7 1.2 %collective-permute-start.9 = (f32[16,16]{1,0:T(8,128)S(1)}, f32[16,16]{1,0:T(8,128)S(1)}, u32[]{:S(2)}, u32[]{:S(2)}) collective-permute-start(f32[16,16]{1,0:T(8,128)S(1)} %slice_add_fusion), channel_id=1, source_target_pairs={{0,1},{1,0},{2,3},{3,2},{4,5},{5,4},{6,7},{7,6},{8,9},{9,8},{10,11... | collective-permute-start | bytes 3080 | tf_op jit(solution)/shard_map/ppermute | solution.py:275

commit v7 on v6

--- a/solution.py
+++ b/solution.py
@@ -31,22 +31,18 @@
     return per * (feature % words) + feature // words
 
 
-def pack_kernel(words, passages, query_hbm, cand_hbm, out_ref, query_ref, cand_ref, sems):
-    copies = [
-        pltpu.make_async_copy(query_hbm, query_ref, sems.at[0]),
-        pltpu.make_async_copy(cand_hbm, cand_ref, sems.at[1]),
-    ]
-    for c in copies:
-        c.start()
+def order_kernel(words, out_ref):
+    width = out_ref.shape[0]
+    source = spread(iota((width, width), 1), words, width // words)
+    out_ref[...] = ones_where(iota((width, width), 0) == source)
+
+
+def pack_kernel(passages, query_ref, cand_ref, order_ref, out_ref):
     count, tokens, width = query_ref.shape
-    per = width // words
-    order = ones_where(iota((width, width), 0) == spread(iota((width, width), 1), words, per))
     picks = cand_ref.shape[1]
-    for c in copies:
-        c.wait()
     flat = query_ref[...].reshape(count * tokens, width)
     rows = count * tokens
-    out_ref[0:rows, :] = dot(flat, order).astype(jnp.bfloat16)
+    out_ref[0:rows, :] = dot(flat, order_ref[...]).astype(jnp.bfloat16)
     ids = cand_ref[...]
     owner = ids // passages
     local = ids - owner * passages
@@ -274,20 +270,23 @@
     def swap_sub(x):
         return lax.ppermute(x, "sub", [(i, i ^ 1) for i in range(halves)])
 
+    order = pl.pallas_call(
+        functools.partial(order_kernel, words),
+        out_shape=jax.ShapeDtypeStruct((width, width), jnp.bfloat16),
+        out_specs=pl.BlockSpec(memory_space=VMEM),
+        compiler_params=LIMIT,
+        cost_estimate=pl.CostEstimate(flops=6 * 10**9, bytes_accessed=0, transcendentals=0),
+        name="order",
+    )()
     payload = pl.pallas_call(
-        functools.partial(pack_kernel, words, passages),
+        functools.partial(pack_kernel, passages),
         out_shape=jax.ShapeDtypeStruct((query_count * (tokens + 1), width), jnp.bfloat16),
-        in_specs=whole(2, pltpu.HBM),
+        in_specs=whole(3, VMEM),
         out_specs=pl.BlockSpec(memory_space=VMEM),
-        scratch_shapes=[
-            VMEM(queries.shape, queries.dtype),
-            VMEM(candidates.shape, candidates.dtype),
-            pltpu.SemaphoreType.DMA((2,)),
-        ],
         compiler_params=LIMIT,
         cost_estimate=pl.CostEstimate(flops=6 * 10**9, bytes_accessed=0, transcendentals=0),
         name="pack",
-    )(queries, candidates)
+    )(queries, candidates, order)
 
     stored = (
         centroid_ids,
@@ -375,7 +374,7 @@
     unit = 2 * WIDE
     units = passages // unit
     parts = len(steps)
-    cuts = [0] + [units * (i + 2) // (parts + 1) * unit for i in range(parts)]
+    cuts = [(2 * units * i + parts) // (2 * parts) * unit for i in range(parts + 1)]
     held = payload[None]
     wide = embedded = None
     for i, d in enumerate(steps[:-2]):

time: 38.6 us -> 37 us (0.959)
  waiting for transfers between devices: 8.25 us -> 6.14 us
  starting transfers between devices: 13.6 us -> 14.9 us
  local copies, waits for them, and re-layouts: 1.86 us -> 1.05 us
    ppermute x7, waiting for transfers between devices: 7.01 us -> 4.9 us  [swap_shard(): return lax.ppermute(x, 'shard', [(i, i ^ d) for i in range(shards)])]
    ppermute x7, starting transfers between devices: 13 us -> 14.3 us  [swap_shard(): return lax.ppermute(x, 'shard', [(i, i ^ d) for i in range(shards)])]
    unnamed x17, local copies, waits for them, and re-layouts: 1.69 us -> 0.88 us
  transfers between devices with their start and end apart: 10 -> 10, of which waited for: 6 -> 7; matrix products, arithmetic and copies ran while one was open for 0% -> 0% of each run, Pallas kernels for 35% -> 37%
where the time goes in v7:
time: 37 us; the launch traced here: 36.8 us
  starting transfers between devices  14.9 us (40%)
  Pallas kernels  13.9 us (38%)
  waiting for transfers between devices  6.14 us (17%)
  local copies, waits for them, and re-layouts  1.05 us (3%)
  other arithmetic  0.66 us (2%)
    ppermute x7, starting transfers between devices, swap_shard(): return lax.ppermute(x, 'shard', [(i, i ^ d) for i in range(shards)])  14.3 us
    pallas_call x3, Pallas kernels, decode(): pl.pallas_call(functools.partial(decode_kernel, first, start, stop), out_...  8.79 us
    ppermute x7, waiting for transfers between devices, swap_shard(): return lax.ppermute(x, 'shard', [(i, i ^ d) for i in range(shards)])  4.9 us
    pallas_call x2, Pallas kernels, score(): pl.pallas_call(functools.partial(pair_kernel, query_count, picks, capacit...  4.08 us
    ppermute x3, waiting for transfers between devices, swap_sub(): return lax.ppermute(x, 'sub', [(i, i ^ 1) for i in range(halves)])  1.24 us
    pallas_call x1, Pallas kernels, find(): pl.pallas_call(functools.partial(slot_kernel, query_count, picks, capacit...  0.88 us
    unnamed x17, local copies, waits for them, and re-layouts  0.88 us
  transfers between devices with their start and end apart: 10, of which 7 were waited for; matrix products, arithmetic and copies ran while one was open for 0% of the time, Pallas kernels for 37%

profile of v7, /device:TPU:0, one launch (start us, length us, event | category | flops | bytes accessed | tf_op | source)
XLA Modules:
  0.0 36.8 jit_solution(6957940626610776581)
XLA Ops:
  0.0 0.0 copy-start.5
  0.0 0.0 copy-start.2
  0.0 0.7 %copy-done.5 = s32[16,16]{1,0:T(8,128)S(1)} copy-done((s32[16,16]{1,0:T(8,128)S(1)}, s32[16,16]{1,0:T(8,128)}, u32[]{:S(2)}) %copy-start.5) | copy-done | bytes 1048
  0.7 0.2 copy-done.2
  0.9 0.0 copy-start
  0.9 0.0 copy-start.1
  0.9 0.0 copy-start.3
  0.9 0.0 copy-start.4
  0.9 0.0 copy-start.6
  0.9 0.2 pack.1
  1.0 4.1 %collective-permute-start = (bf16[1,272,128]{2,1,0:T(8,128)(2,1)S(1)}, bf16[1,272,128]{2,1,0:T(8,128)(2,1)S(1)}, u32[]{:S(2)}, u32[]{:S(2)}) collective-permute-start(bf16[1,272,128]{2,1,0:T(8,128)(2,1)S(1)} %bitcast.4), channel_id=1, source_target_pairs={{0,8},{2,10},{4,12},{6,14},{8,0},{10,2},{12,4},{14,6},{1,9},{3,11}... | collective-permute-start | bytes 208904 | tf_op jit(solution)/shard_map/ppermute | solution.py:268
  5.1 0.0 copy-done
  5.1 0.0 copy-done.1
  5.1 0.0 copy-done.3
  5.1 0.0 copy-done.4
  5.2 0.0 copy-done.6
  5.2 3.2 %decode.3 = (bf16[64,128,128]{2,1,0:T(8,128)(2,1)S(1)}, f32[4096,128]{1,0:T(8,128)S(1)}) custom-call(s32[64,128]{1,0:T(8,128)S(1)} %copy-done.3, s32[64,16,128]{2,1,0:T(8,128)S(1)} %bitcast.7, bf16[64,128]{1,0:T(8,128)(2,1)S(1)} %copy-done.4, bf16[1,4]{1,0:T(2,128)(2,1)S(1)} %bitcast.11, bf16[4096,128]{1,0:T(8,128)(2,1)S(1)} %copy-done), custom_call_target="tpu_custom_call" | custom-call | flops 4800000000 | tf_op jit(solution)/shard_map/decode/pallas_call | solution.py:312
  8.4 0.5 %collective-permute-done = bf16[1,272,128]{2,1,0:T(8,128)(2,1)S(1)} collective-permute-done((bf16[1,272,128]{2,1,0:T(8,128)(2,1)S(1)}, bf16[1,272,128]{2,1,0:T(8,128)(2,1)S(1)}, u32[]{:S(2)}, u32[]{:S(2)}) %collective-permute-start) | collective-permute-done | bytes 69664 | tf_op jit(solution)/shard_map/ppermute | solution.py:268
  8.9 1.1 %collective-permute-start.2 = (bf16[2,272,128]{2,1,0:T(8,128)(2,1)S(1)}, bf16[2,272,128]{2,1,0:T(8,128)(2,1)S(1)}, u32[]{:S(2)}, u32[]{:S(2)}) collective-permute-start(bf16[2,272,128]{2,1,0:T(8,128)(2,1)S(1)} %pad_maximum_fusion.1), channel_id=1, source_target_pairs={{0,4},{2,6},{4,0},{6,2},{8,12},{10,14},{12,8},{14,10},{1,5},{3,7},... | collective-permute-start | bytes 417800 | tf_op jit(solution)/shard_map/ppermute | solution.py:268
  10.1 1.5 %collective-permute-start.1 = (bf16[2,272,128]{2,1,0:T(8,128)(2,1)S(1)}, bf16[2,272,128]{2,1,0:T(8,128)(2,1)S(1)}, u32[]{:S(2)}, u32[]{:S(2)}) collective-permute-start(bf16[2,272,128]{2,1,0:T(8,128)(2,1)S(1)} %pad_maximum_fusion.1), channel_id=1, source_target_pairs={{0,2},{2,0},{4,6},{6,4},{8,10},{10,8},{12,14},{14,12},{1,3},{3,1},... | collective-permute-start | bytes 417800 | tf_op jit(solution)/shard_map/ppermute | solution.py:268
  11.6 2.4 %decode.4.refs_5_ = bf16[64,128,128]{2,1,0:T(8,128)(2,1)S(1)} custom-call(s32[64,128]{1,0:T(8,128)S(1)} %copy-done.3, s32[64,16,128]{2,1,0:T(8,128)S(1)} %bitcast.8, bf16[64,128]{1,0:T(8,128)(2,1)S(1)} %copy-done.4, bf16[1,4]{1,0:T(2,128)(2,1)S(1)} %bitcast.12, f32[4096,128]{1,0:T(8,128)S(1)} %get-tuple-element.20.refs_4_, ...), custom_call_target="tpu_custom_call", output_to_operand_aliasing={{}: (5, {})} | custom-call | flops 3200000000 | tf_op jit(solution)/shard_map/decode/pallas_call | solution.py:312
  13.9 0.1 collective-permute-done.2
  14.1 1.7 %collective-permute-start.3 = (bf16[2,272,128]{2,1,0:T(8,128)(2,1)S(1)}, bf16[2,272,128]{2,1,0:T(8,128)(2,1)S(1)}, u32[]{:S(2)}, u32[]{:S(2)}) collective-permute-start(bf16[2,272,128]{2,1,0:T(8,128)(2,1)S(1)} %collective-permute-done.2), channel_id=1, source_target_pairs={{0,2},{2,0},{4,6},{6,4},{8,10},{10,8},{12,14},{14,12},{1,3},{3,1},... | collective-permute-start | bytes 417800 | tf_op jit(solution)/shard_map/ppermute | solution.py:268
  15.8 3.2 %decode.5.emb_ref = bf16[64,128,128]{2,1,0:T(8,128)(2,1)S(1)} custom-call(s32[64,128]{1,0:T(8,128)S(1)} %copy-done.3, s32[64,16,128]{2,1,0:T(8,128)S(1)} %bitcast.9, bf16[64,128]{1,0:T(8,128)(2,1)S(1)} %copy-done.4, bf16[1,4]{1,0:T(2,128)(2,1)S(1)} %bitcast.13, f32[4096,128]{1,0:T(8,128)S(1)} %get-tuple-element.20.refs_4_, ...), custom_call_target="tpu_custom_call", output_to_operand_aliasing={{}: (5, {})} | custom-call | flops 4800000000 | tf_op jit(solution)/shard_map/decode/pallas_call | solution.py:312
  19.0 0.0 collective-permute-done.1
  19.0 0.1 collective-permute-done.3
  19.1 0.0 copy-start.7
  19.2 0.1 collective-permute-start.4
  19.3 0.6 %collective-permute-start.5 = (bf16[4,272,128]{2,1,0:T(8,128)(2,1)S(1)}, bf16[4,272,128]{2,1,0:T(8,128)(2,1)S(1)}, u32[]{:S(2)}, u32[]{:S(2)}) collective-permute-start(bf16[4,272,128]{2,1,0:T(8,128)(2,1)S(1)} %pad_maximum_fusion.refs_0_.mine_ref), channel_id=1, source_target_pairs={{0,1},{1,0},{2,3},{3,2},{4,5},{5,4},{6,7},{7,6},{8,9},{9,8},{10,11... | collective-permute-start | bytes 835592 | tf_op jit(solution)/shard_map/ppermute | solution.py:271
  19.8 0.9 %slots.1 = (s32[16,128]{1,0:T(8,128)S(1)}, s32[64,128]{1,0:T(8,128)S(1)}) custom-call(bf16[4,272,128]{2,1,0:T(8,128)(2,1)S(1)} %constant_dynamic-update-slice_fusion.rows_ref.mine_ref), custom_call_target="tpu_custom_call" | custom-call | flops 1000000000 | tf_op jit(solution)/shard_map/slots/pallas_call | solution.py:333
  20.7 0.1 collective-permute-done.4.other_ref
  20.8 0.0 copy-done.7
  20.8 2.2 %pairs.2 = (f32[16,128]{1,0:T(8,128)S(1)}, s32[16,128]{1,0:T(8,128)S(1)}, s32[64,128]{1,0:T(8,128)S(1)}) custom-call(s32[64]{0:T(128)S(1)} %copy-done.7, s32[16,128]{1,0:T(8,128)S(1)} %get-tuple-element.25.slot_ref, s32[64,128]{1,0:T(8,128)S(1)} %get-tuple-element.26.rank_ref, bf16[4,272,128]{2,1,0:T(8,128)(2,1)S(1)} %constant_dynamic-update-slice_fusion.rows_ref.mine_ref, ...), custom_call_target="tpu_custom_call" | custom-call | flops 3000000000 | tf_op jit(solution)/shard_map/pairs/pallas_call | solution.py:352
  23.0 1.8 %collective-permute-start.6 = (f32[16,64]{1,0:T(8,128)S(1)}, f32[16,64]{1,0:T(8,128)S(1)}, u32[]{:S(2)}, u32[]{:S(2)}) collective-permute-start(f32[16,64]{1,0:T(8,128)S(1)} %bitcast.10), channel_id=1, source_target_pairs={{0,2},{2,0},{4,6},{6,4},{8,10},{10,8},{12,14},{14,12},{1,3},{3,1},... | collective-permute-start | bytes 12296 | tf_op jit(solution)/shard_map/ppermute | solution.py:268
  24.8 0.0 collective-permute-done.5.other_ref
  24.8 1.9 %pairs.3 = f32[16,128]{1,0:T(8,128)S(1)} custom-call(s32[64]{0:T(128)S(1)} %copy-done.7, s32[16,128]{1,0:T(8,128)S(1)} %get-tuple-element.28.slot_ref, s32[64,128]{1,0:T(8,128)S(1)} %get-tuple-element.29.rank_ref, bf16[4,272,128]{2,1,0:T(8,128)(2,1)S(1)} %pad_maximum_fusion.refs_0_.mine_ref, bf16[4,272,128]{2,1,0:T(8,128)(2,1)S(1)} %collective-permute-done.5.other_ref, ...), custom_call_target="tpu_custom_call" | custom-call | flops 3000000000 | tf_op jit(solution)/shard_map/pairs/pallas_call | solution.py:352
  26.7 0.0 collective-permute-done.6
  26.7 0.1 slice.26
  26.8 1.1 %collective-permute-start.7 = (f32[16,32]{1,0:T(8,128)S(1)}, f32[16,32]{1,0:T(8,128)S(1)}, u32[]{:S(2)}, u32[]{:S(2)}) collective-permute-start(f32[16,32]{1,0:T(8,128)S(1)} %slice.26), channel_id=1, source_target_pairs={{0,4},{2,6},{4,0},{6,2},{8,12},{10,14},{12,8},{14,10},{1,5},{3,7},... | collective-permute-start | bytes 6152 | tf_op jit(solution)/shard_map/ppermute | solution.py:268
  27.9 2.5 %collective-permute-done.7 = f32[16,32]{1,0:T(8,128)S(1)} collective-permute-done((f32[16,32]{1,0:T(8,128)S(1)}, f32[16,32]{1,0:T(8,128)S(1)}, u32[]{:S(2)}, u32[]{:S(2)}) %collective-permute-start.7) | collective-permute-done | bytes 2080 | tf_op jit(solution)/shard_map/ppermute | solution.py:268
  30.4 0.1 slice.28
  30.5 2.9 %collective-permute-start.8 = (f32[16,16]{1,0:T(8,128)S(1)}, f32[16,16]{1,0:T(8,128)S(1)}, u32[]{:S(2)}, u32[]{:S(2)}) collective-permute-start(f32[16,16]{1,0:T(8,128)S(1)} %slice.28), channel_id=1, source_target_pairs={{0,8},{2,10},{4,12},{6,14},{8,0},{10,2},{12,4},{14,6},{1,9},{3,11}... | collective-permute-start | bytes 3080 | tf_op jit(solution)/shard_map/ppermute | solution.py:268
  33.4 1.7 %collective-permute-done.8 = f32[16,16]{1,0:T(8,128)S(1)} collective-permute-done((f32[16,16]{1,0:T(8,128)S(1)}, f32[16,16]{1,0:T(8,128)S(1)}, u32[]{:S(2)}, u32[]{:S(2)}) %collective-permute-start.8) | collective-permute-done | bytes 1056 | tf_op jit(solution)/shard_map/ppermute | solution.py:268
  35.1 0.0 collective-permute-start.9
  35.1 1.2 %collective-permute-done.9 = f32[16,16]{1,0:T(8,128)S(1)} collective-permute-done((f32[16,16]{1,0:T(8,128)S(1)}, f32[16,16]{1,0:T(8,128)S(1)}, u32[]{:S(2)}, u32[]{:S(2)}) %collective-permute-start.9) | collective-permute-done | bytes 1056 | tf_op jit(solution)/shard_map/ppermute | solution.py:271
  36.2 0.6 %add.15 = f32[16,16]{1,0:T(8,128)} add(f32[16,16]{1,0:T(8,128)S(1)} %slice_add_fusion, f32[16,16]{1,0:T(8,128)S(1)} %collective-permute-done.9) | non-fusion elementwise | flops 256 | bytes 3072 | tf_op jit(solution)/shard_map/add | solution.py:403
  (8 shorter events, 0.1 us)
Async XLA Ops:
  0.0 0.7 %copy-start.5 = (s32[16,16]{1,0:T(8,128)S(1)}, s32[16,16]{1,0:T(8,128)}, u32[]{:S(2)}) copy-start(s32[16,16]{1,0:T(8,128)} %cand_ref.1) | copy-start | bytes 3076
  0.0 0.9 %copy-start.2 = (bf16[16,16,128]{2,1,0:T(8,128)(2,1)S(1)}, bf16[16,16,128]{2,1,0:T(8,128)(2,1)}, u32[]{:S(2)}) copy-start(bf16[16,16,128]{2,1,0:T(8,128)(2,1)} %query_ref.1) | copy-start | bytes 196612
  0.9 4.3 %copy-start = (bf16[4096,128]{1,0:T(8,128)(2,1)S(1)}, bf16[4096,128]{1,0:T(8,128)(2,1)}, u32[]{:S(2)}) copy-start(bf16[4096,128]{1,0:T(8,128)(2,1)} %refs_4_.1) | copy-start | bytes 3145732
  0.9 4.3 %copy-start.1 = (s32[64,128,16]{1,2,0:T(8,128)S(1)}, s32[64,128,16]{1,2,0:T(8,128)}, u32[]{:S(2)}) copy-start(s32[64,128,16]{1,2,0:T(8,128)} %param.10) | copy-start | bytes 1572868
  0.9 4.3 %copy-start.3 = (s32[64,128]{1,0:T(8,128)S(1)}, s32[64,128]{1,0:T(8,128)}, u32[]{:S(2)}) copy-start(s32[64,128]{1,0:T(8,128)} %refs_0_.5) | copy-start | bytes 98308
  0.9 4.3 %copy-start.4 = (bf16[64,128]{1,0:T(8,128)(2,1)S(1)}, bf16[64,128]{1,0:T(8,128)(2,1)}, u32[]{:S(2)}) copy-start(bf16[64,128]{1,0:T(8,128)(2,1)} %refs_2_.5) | copy-start | bytes 49156
  0.9 4.3 %copy-start.6 = (bf16[4]{0:T(256)(128)(2,1)S(1)}, bf16[4]{0:T(256)(128)(2,1)}, u32[]{:S(2)}) copy-start(bf16[4]{0:T(256)(128)(2,1)} %param.15) | copy-start | bytes 28
  1.0 7.9 %collective-permute-start = (bf16[1,272,128]{2,1,0:T(8,128)(2,1)S(1)}, bf16[1,272,128]{2,1,0:T(8,128)(2,1)S(1)}, u32[]{:S(2)}, u32[]{:S(2)}) collective-permute-start(bf16[1,272,128]{2,1,0:T(8,128)(2,1)S(1)} %bitcast.4), channel_id=1, source_target_pairs={{0,8},{2,10},{4,12},{6,14},{8,0},{10,2},{12,4},{14,6},{1,9},{3,11}... | collective-permute-start | bytes 208904 | tf_op jit(solution)/shard_map/ppermute | solution.py:268
  8.9 5.1 %collective-permute-start.2 = (bf16[2,272,128]{2,1,0:T(8,128)(2,1)S(1)}, bf16[2,272,128]{2,1,0:T(8,128)(2,1)S(1)}, u32[]{:S(2)}, u32[]{:S(2)}) collective-permute-start(bf16[2,272,128]{2,1,0:T(8,128)(2,1)S(1)} %pad_maximum_fusion.1), channel_id=1, source_target_pairs={{0,4},{2,6},{4,0},{6,2},{8,12},{10,14},{12,8},{14,10},{1,5},{3,7},... | collective-permute-start | bytes 417800 | tf_op jit(solution)/shard_map/ppermute | solution.py:268
  10.1 9.0 %collective-permute-start.1 = (bf16[2,272,128]{2,1,0:T(8,128)(2,1)S(1)}, bf16[2,272,128]{2,1,0:T(8,128)(2,1)S(1)}, u32[]{:S(2)}, u32[]{:S(2)}) collective-permute-start(bf16[2,272,128]{2,1,0:T(8,128)(2,1)S(1)} %pad_maximum_fusion.1), channel_id=1, source_target_pairs={{0,2},{2,0},{4,6},{6,4},{8,10},{10,8},{12,14},{14,12},{1,3},{3,1},... | collective-permute-start | bytes 417800 | tf_op jit(solution)/shard_map/ppermute | solution.py:268
  14.1 5.1 %collective-permute-start.3 = (bf16[2,272,128]{2,1,0:T(8,128)(2,1)S(1)}, bf16[2,272,128]{2,1,0:T(8,128)(2,1)S(1)}, u32[]{:S(2)}, u32[]{:S(2)}) collective-permute-start(bf16[2,272,128]{2,1,0:T(8,128)(2,1)S(1)} %collective-permute-done.2), channel_id=1, source_target_pairs={{0,2},{2,0},{4,6},{6,4},{8,10},{10,8},{12,14},{14,12},{1,3},{3,1},... | collective-permute-start | bytes 417800 | tf_op jit(solution)/shard_map/ppermute | solution.py:268
  19.1 1.6 %copy-start.7 = (s32[64]{0:T(128)S(1)}, s32[64]{0:T(128)}, u32[]{:S(2)}) copy-start(s32[64]{0:T(128)} %len_hbm.3) | copy-start | bytes 772
  19.2 1.6 %collective-permute-start.4 = (bf16[4,272,128]{2,1,0:T(8,128)(2,1)S(1)}, bf16[4,272,128]{2,1,0:T(8,128)(2,1)S(1)}, u32[]{:S(2)}, u32[]{:S(2)}) collective-permute-start(bf16[4,272,128]{2,1,0:T(8,128)(2,1)S(1)} %constant_dynamic-update-slice_fusion.rows_ref.mine_ref), channel_id=1, source_target_pairs={{0,1},{1,0},{2,3},{3,2},{4,5},{5,4},{6,7},{7,6},{8,9},{9,8},{10,11... | collective-permute-start | bytes 835592 | tf_op jit(solution)/shard_map/ppermute | solution.py:271
  19.3 5.5 %collective-permute-start.5 = (bf16[4,272,128]{2,1,0:T(8,128)(2,1)S(1)}, bf16[4,272,128]{2,1,0:T(8,128)(2,1)S(1)}, u32[]{:S(2)}, u32[]{:S(2)}) collective-permute-start(bf16[4,272,128]{2,1,0:T(8,128)(2,1)S(1)} %pad_maximum_fusion.refs_0_.mine_ref), channel_id=1, source_target_pairs={{0,1},{1,0},{2,3},{3,2},{4,5},{5,4},{6,7},{7,6},{8,9},{9,8},{10,11... | collective-permute-start | bytes 835592 | tf_op jit(solution)/shard_map/ppermute | solution.py:271
  23.0 3.7 %collective-permute-start.6 = (f32[16,64]{1,0:T(8,128)S(1)}, f32[16,64]{1,0:T(8,128)S(1)}, u32[]{:S(2)}, u32[]{:S(2)}) collective-permute-start(f32[16,64]{1,0:T(8,128)S(1)} %bitcast.10), channel_id=1, source_target_pairs={{0,2},{2,0},{4,6},{6,4},{8,10},{10,8},{12,14},{14,12},{1,3},{3,1},... | collective-permute-start | bytes 12296 | tf_op jit(solution)/shard_map/ppermute | solution.py:268
  26.8 3.7 %collective-permute-start.7 = (f32[16,32]{1,0:T(8,128)S(1)}, f32[16,32]{1,0:T(8,128)S(1)}, u32[]{:S(2)}, u32[]{:S(2)}) collective-permute-start(f32[16,32]{1,0:T(8,128)S(1)} %slice.26), channel_id=1, source_target_pairs={{0,4},{2,6},{4,0},{6,2},{8,12},{10,14},{12,8},{14,10},{1,5},{3,7},... | collective-permute-start | bytes 6152 | tf_op jit(solution)/shard_map/ppermute | solution.py:268
  30.5 4.6 %collective-permute-start.8 = (f32[16,16]{1,0:T(8,128)S(1)}, f32[16,16]{1,0:T(8,128)S(1)}, u32[]{:S(2)}, u32[]{:S(2)}) collective-permute-start(f32[16,16]{1,0:T(8,128)S(1)} %slice.28), channel_id=1, source_target_pairs={{0,8},{2,10},{4,12},{6,14},{8,0},{10,2},{12,4},{14,6},{1,9},{3,11}... | collective-permute-start | bytes 3080 | tf_op jit(solution)/shard_map/ppermute | solution.py:268
  35.1 1.2 %collective-permute-start.9 = (f32[16,16]{1,0:T(8,128)S(1)}, f32[16,16]{1,0:T(8,128)S(1)}, u32[]{:S(2)}, u32[]{:S(2)}) collective-permute-start(f32[16,16]{1,0:T(8,128)S(1)} %slice_add_fusion), channel_id=1, source_target_pairs={{0,1},{1,0},{2,3},{3,2},{4,5},{5,4},{6,7},{7,6},{8,9},{9,8},{10,11... | collective-permute-start | bytes 3080 | tf_op jit(solution)/shard_map/ppermute | solution.py:271

commit v8 on v7

--- a/solution.py
+++ b/solution.py
@@ -397,10 +397,23 @@
     far_scores, near_found = score(find(far), far, swap_sub(far), near)
     near_scores, _ = score(near_found, near, near_other)
     total = near_scores + swap_shard(far_scores, 1)
-    for d in reversed(steps[:-1]):
+    for d in reversed(steps[2:-1]):
         half = total.shape[1] // 2
         total = total[:, :half] + swap_shard(total[:, half:], d)
-    return total + swap_sub(total)
+    far_d, near_d = steps[:2]
+    core = lax.axis_index("sub")
+
+    def swap_apart(x, even, odd):
+        count = shards * halves
+        pairs = [(i, i ^ (halves * (odd if i % 2 else even))) for i in range(count)]
+        return lax.ppermute(x, ("shard", "sub"), pairs)
+
+    total = total + swap_sub(total)
+    mine, to_far, to_near, to_both = (total[:, i * picks : (i + 1) * picks] for i in range(4))
+    one = swap_apart(jnp.where(core == 1, to_far, to_near), near_d, far_d)
+    two = swap_apart(to_both, 1, far_d ^ near_d)
+    part = one + jnp.where(core == 1, two, mine)
+    return part + swap_sub(part)
 
 
 def solution(mesh):

time: 37 us -> 36.6 us (0.989)
  waiting for transfers between devices: 6.14 us -> 4.93 us
  starting transfers between devices: 14.9 us -> 15.8 us
    ppermute x7 -> x5, waiting for transfers between devices: 4.9 us -> 0.74 us  [swap_shard(): return lax.ppermute(x, 'shard', [(i, i ^ d) for i in range(shards)])]
    ppermute x7 -> x5, starting transfers between devices: 14.3 us -> 10.3 us  [swap_shard(): return lax.ppermute(x, 'shard', [(i, i ^ d) for i in range(shards)])]
    ppermute x0 -> x2, starting transfers between devices: none -> 2.59 us  [swap_apart(): return lax.ppermute(x, ('shard', 'sub'), pairs)]
    ppermute x3 -> x4, starting transfers between devices: 0.63 us -> 2.98 us  [swap_sub(): return lax.ppermute(x, 'sub', [(i, i ^ 1) for i in range(halves)])]
    ppermute x0 -> x2, waiting for transfers between devices: none -> 2.13 us  [swap_apart(): return lax.ppermute(x, ('shard', 'sub'), pairs)]
    ppermute x3 -> x4, waiting for transfers between devices: 1.24 us -> 2.05 us  [swap_sub(): return lax.ppermute(x, 'sub', [(i, i ^ 1) for i in range(halves)])]
  transfers between devices with their start and end apart: 10 -> 11, of which waited for: 7 -> 8; matrix products, arithmetic and copies ran while one was open for 0% -> 0% of each run, Pallas kernels for 37% -> 38%
where the time goes in v8:
time: 36.6 us; the launch traced here: 36.5 us
  starting transfers between devices  15.8 us (43%)
  Pallas kernels  13.9 us (38%)
  waiting for transfers between devices  4.93 us (13%)
  local copies, waits for them, and re-layouts  0.89 us (2%)
  other arithmetic  0.73 us (2%)
    ppermute x5, starting transfers between devices, swap_shard(): return lax.ppermute(x, 'shard', [(i, i ^ d) for i in range(shards)])  10.3 us
    pallas_call x3, Pallas kernels, decode(): pl.pallas_call(functools.partial(decode_kernel, first, start, stop), out_...  8.78 us
    pallas_call x2, Pallas kernels, score(): pl.pallas_call(functools.partial(pair_kernel, query_count, picks, capacit...  4.08 us
    ppermute x4, starting transfers between devices, swap_sub(): return lax.ppermute(x, 'sub', [(i, i ^ 1) for i in range(halves)])  2.98 us
    ppermute x2, starting transfers between devices, swap_apart(): return lax.ppermute(x, ('shard', 'sub'), pairs)  2.59 us
    ppermute x2, waiting for transfers between devices, swap_apart(): return lax.ppermute(x, ('shard', 'sub'), pairs)  2.13 us
    ppermute x4, waiting for transfers between devices, swap_sub(): return lax.ppermute(x, 'sub', [(i, i ^ 1) for i in range(halves)])  2.05 us
    pallas_call x1, Pallas kernels, find(): pl.pallas_call(functools.partial(slot_kernel, query_count, picks, capacit...  0.88 us
  transfers between devices with their start and end apart: 11, of which 8 were waited for; matrix products, arithmetic and copies ran while one was open for 0% of the time, Pallas kernels for 38%

profile of v8, /device:TPU:0, one launch (start us, length us, event | category | flops | bytes accessed | tf_op | source)
XLA Modules:
  0.0 36.5 jit_solution(3468421318984659023)
XLA Ops:
  0.0 0.0 copy-start.2
  0.0 0.0 copy-start.5
  0.0 0.8 %copy-done.2 = bf16[16,16,128]{2,1,0:T(8,128)(2,1)S(1)} copy-done((bf16[16,16,128]{2,1,0:T(8,128)(2,1)S(1)}, bf16[16,16,128]{2,1,0:T(8,128)(2,1)}, u32[]{:S(2)}) %copy-start.2) | copy-done | bytes 65560
  0.8 0.0 copy-done.5
  0.8 0.0 copy-start
  0.8 0.0 copy-start.1
  0.8 0.0 copy-start.3
  0.9 0.0 copy-start.4
  0.9 0.0 copy-start.6
  0.9 0.2 pack.1
  1.0 4.1 %collective-permute-start = (bf16[1,272,128]{2,1,0:T(8,128)(2,1)S(1)}, bf16[1,272,128]{2,1,0:T(8,128)(2,1)S(1)}, u32[]{:S(2)}, u32[]{:S(2)}) collective-permute-start(bf16[1,272,128]{2,1,0:T(8,128)(2,1)S(1)} %bitcast.4), channel_id=1, source_target_pairs={{0,8},{2,10},{4,12},{6,14},{8,0},{10,2},{12,4},{14,6},{1,9},{3,11}... | collective-permute-start | bytes 208904 | tf_op jit(solution)/shard_map/ppermute | solution.py:268
  5.1 0.0 copy-done
  5.1 0.0 copy-done.1
  5.1 0.0 copy-done.3
  5.1 0.0 copy-done.4
  5.1 0.0 copy-done.6
  5.2 3.2 %decode.3 = (bf16[64,128,128]{2,1,0:T(8,128)(2,1)S(1)}, f32[4096,128]{1,0:T(8,128)S(1)}) custom-call(s32[64,128]{1,0:T(8,128)S(1)} %copy-done.3, s32[64,16,128]{2,1,0:T(8,128)S(1)} %bitcast.7, bf16[64,128]{1,0:T(8,128)(2,1)S(1)} %copy-done.4, bf16[1,4]{1,0:T(2,128)(2,1)S(1)} %bitcast.11, bf16[4096,128]{1,0:T(8,128)(2,1)S(1)} %copy-done), custom_call_target="tpu_custom_call" | custom-call | flops 4800000000 | tf_op jit(solution)/shard_map/decode/pallas_call | solution.py:312
  8.4 0.5 %collective-permute-done = bf16[1,272,128]{2,1,0:T(8,128)(2,1)S(1)} collective-permute-done((bf16[1,272,128]{2,1,0:T(8,128)(2,1)S(1)}, bf16[1,272,128]{2,1,0:T(8,128)(2,1)S(1)}, u32[]{:S(2)}, u32[]{:S(2)}) %collective-permute-start) | collective-permute-done | bytes 69664 | tf_op jit(solution)/shard_map/ppermute | solution.py:268
  8.9 1.1 %collective-permute-start.2 = (bf16[2,272,128]{2,1,0:T(8,128)(2,1)S(1)}, bf16[2,272,128]{2,1,0:T(8,128)(2,1)S(1)}, u32[]{:S(2)}, u32[]{:S(2)}) collective-permute-start(bf16[2,272,128]{2,1,0:T(8,128)(2,1)S(1)} %pad_maximum_fusion.1), channel_id=1, source_target_pairs={{0,4},{2,6},{4,0},{6,2},{8,12},{10,14},{12,8},{14,10},{1,5},{3,7},... | collective-permute-start | bytes 417800 | tf_op jit(solution)/shard_map/ppermute | solution.py:268
  10.0 1.5 %collective-permute-start.1 = (bf16[2,272,128]{2,1,0:T(8,128)(2,1)S(1)}, bf16[2,272,128]{2,1,0:T(8,128)(2,1)S(1)}, u32[]{:S(2)}, u32[]{:S(2)}) collective-permute-start(bf16[2,272,128]{2,1,0:T(8,128)(2,1)S(1)} %pad_maximum_fusion.1), channel_id=1, source_target_pairs={{0,2},{2,0},{4,6},{6,4},{8,10},{10,8},{12,14},{14,12},{1,3},{3,1},... | collective-permute-start | bytes 417800 | tf_op jit(solution)/shard_map/ppermute | solution.py:268
  11.6 2.4 %decode.4.refs_5_ = bf16[64,128,128]{2,1,0:T(8,128)(2,1)S(1)} custom-call(s32[64,128]{1,0:T(8,128)S(1)} %copy-done.3, s32[64,16,128]{2,1,0:T(8,128)S(1)} %bitcast.8, bf16[64,128]{1,0:T(8,128)(2,1)S(1)} %copy-done.4, bf16[1,4]{1,0:T(2,128)(2,1)S(1)} %bitcast.12, f32[4096,128]{1,0:T(8,128)S(1)} %get-tuple-element.20.refs_4_, ...), custom_call_target="tpu_custom_call", output_to_operand_aliasing={{}: (5, {})} | custom-call | flops 3200000000 | tf_op jit(solution)/shard_map/decode/pallas_call | solution.py:312
  13.9 0.1 collective-permute-done.2
  14.1 1.7 %collective-permute-start.3 = (bf16[2,272,128]{2,1,0:T(8,128)(2,1)S(1)}, bf16[2,272,128]{2,1,0:T(8,128)(2,1)S(1)}, u32[]{:S(2)}, u32[]{:S(2)}) collective-permute-start(bf16[2,272,128]{2,1,0:T(8,128)(2,1)S(1)} %collective-permute-done.2), channel_id=1, source_target_pairs={{0,2},{2,0},{4,6},{6,4},{8,10},{10,8},{12,14},{14,12},{1,3},{3,1},... | collective-permute-start | bytes 417800 | tf_op jit(solution)/shard_map/ppermute | solution.py:268
  15.8 3.2 %decode.5.emb_ref = bf16[64,128,128]{2,1,0:T(8,128)(2,1)S(1)} custom-call(s32[64,128]{1,0:T(8,128)S(1)} %copy-done.3, s32[64,16,128]{2,1,0:T(8,128)S(1)} %bitcast.9, bf16[64,128]{1,0:T(8,128)(2,1)S(1)} %copy-done.4, bf16[1,4]{1,0:T(2,128)(2,1)S(1)} %bitcast.13, f32[4096,128]{1,0:T(8,128)S(1)} %get-tuple-element.20.refs_4_, ...), custom_call_target="tpu_custom_call", output_to_operand_aliasing={{}: (5, {})} | custom-call | flops 4800000000 | tf_op jit(solution)/shard_map/decode/pallas_call | solution.py:312
  19.0 0.0 collective-permute-done.1
  19.0 0.1 collective-permute-done.3
  19.1 0.0 copy-start.7
  19.1 0.1 collective-permute-start.4
  19.3 0.6 %collective-permute-start.5 = (bf16[4,272,128]{2,1,0:T(8,128)(2,1)S(1)}, bf16[4,272,128]{2,1,0:T(8,128)(2,1)S(1)}, u32[]{:S(2)}, u32[]{:S(2)}) collective-permute-start(bf16[4,272,128]{2,1,0:T(8,128)(2,1)S(1)} %pad_maximum_fusion.refs_0_.mine_ref), channel_id=1, source_target_pairs={{0,1},{1,0},{2,3},{3,2},{4,5},{5,4},{6,7},{7,6},{8,9},{9,8},{10,11... | collective-permute-start | bytes 835592 | tf_op jit(solution)/shard_map/ppermute | solution.py:271
  19.8 0.9 %slots.1 = (s32[16,128]{1,0:T(8,128)S(1)}, s32[64,128]{1,0:T(8,128)S(1)}) custom-call(bf16[4,272,128]{2,1,0:T(8,128)(2,1)S(1)} %constant_dynamic-update-slice_fusion.rows_ref.mine_ref), custom_call_target="tpu_custom_call" | custom-call | flops 1000000000 | tf_op jit(solution)/shard_map/slots/pallas_call | solution.py:333
  20.7 0.1 collective-permute-done.4.other_ref
  20.8 0.0 copy-done.7
  20.8 2.2 %pairs.2 = (f32[16,128]{1,0:T(8,128)S(1)}, s32[16,128]{1,0:T(8,128)S(1)}, s32[64,128]{1,0:T(8,128)S(1)}) custom-call(s32[64]{0:T(128)S(1)} %copy-done.7, s32[16,128]{1,0:T(8,128)S(1)} %get-tuple-element.25.slot_ref, s32[64,128]{1,0:T(8,128)S(1)} %get-tuple-element.26.rank_ref, bf16[4,272,128]{2,1,0:T(8,128)(2,1)S(1)} %constant_dynamic-update-slice_fusion.rows_ref.mine_ref, ...), custom_call_target="tpu_custom_call" | custom-call | flops 3000000000 | tf_op jit(solution)/shard_map/pairs/pallas_call | solution.py:352
  23.0 1.8 %collective-permute-start.6 = (f32[16,64]{1,0:T(8,128)S(1)}, f32[16,64]{1,0:T(8,128)S(1)}, u32[]{:S(2)}, u32[]{:S(2)}) collective-permute-start(f32[16,64]{1,0:T(8,128)S(1)} %bitcast.10), channel_id=1, source_target_pairs={{0,2},{2,0},{4,6},{6,4},{8,10},{10,8},{12,14},{14,12},{1,3},{3,1},... | collective-permute-start | bytes 12296 | tf_op jit(solution)/shard_map/ppermute | solution.py:268
  24.8 0.0 collective-permute-done.5.other_ref
  24.8 1.9 %pairs.3 = f32[16,128]{1,0:T(8,128)S(1)} custom-call(s32[64]{0:T(128)S(1)} %copy-done.7, s32[16,128]{1,0:T(8,128)S(1)} %get-tuple-element.28.slot_ref, s32[64,128]{1,0:T(8,128)S(1)} %get-tuple-element.29.rank_ref, bf16[4,272,128]{2,1,0:T(8,128)(2,1)S(1)} %pad_maximum_fusion.refs_0_.mine_ref, bf16[4,272,128]{2,1,0:T(8,128)(2,1)S(1)} %collective-permute-done.5.other_ref, ...), custom_call_target="tpu_custom_call" | custom-call | flops 3000000000 | tf_op jit(solution)/shard_map/pairs/pallas_call | solution.py:352
  26.7 0.0 collective-permute-done.6
  26.7 0.1 collective-permute-start.7
  26.8 1.2 %collective-permute-done.7 = f32[16,64]{1,0:T(8,128)S(1)} collective-permute-done((f32[16,64]{1,0:T(8,128)S(1)}, f32[16,64]{1,0:T(8,128)S(1)}, u32[]{:S(2)}, u32[]{:S(2)}) %collective-permute-start.7) | collective-permute-done | bytes 4128 | tf_op jit(solution)/shard_map/ppermute | solution.py:271
  27.9 0.1 fusion.1
  28.0 1.1 %collective-permute-start.8 = (f32[16,16]{1,0:T(8,128)S(1)}, f32[16,16]{1,0:T(8,128)S(1)}, u32[]{:S(2)}, u32[]{:S(2)}) collective-permute-start(f32[16,16]{1,0:T(8,128)S(1)} %get-tuple-element.32), channel_id=1, source_target_pairs={{0,4},{1,9},{2,6},{3,11},{4,0},{5,13},{6,2},{7,15},{8,12},{9,1},{1... | collective-permute-start | bytes 3080 | tf_op jit(solution)/shard_map/ppermute | solution.py:409
  29.1 1.5 %collective-permute-start.9 = (f32[16,16]{1,0:T(8,128)S(1)}, f32[16,16]{1,0:T(8,128)S(1)}, u32[]{:S(2)}, u32[]{:S(2)}) collective-permute-start(f32[16,16]{1,0:T(8,128)S(1)} %get-tuple-element.31), channel_id=1, source_target_pairs={{0,2},{1,13},{2,0},{3,15},{4,6},{5,9},{6,4},{7,11},{8,10},{9,5},{1... | collective-permute-start | bytes 3080 | tf_op jit(solution)/shard_map/ppermute | solution.py:409
  30.6 1.1 %collective-permute-done.8 = f32[16,16]{1,0:T(8,128)S(1)} collective-permute-done((f32[16,16]{1,0:T(8,128)S(1)}, f32[16,16]{1,0:T(8,128)S(1)}, u32[]{:S(2)}, u32[]{:S(2)}) %collective-permute-start.8) | collective-permute-done | bytes 1056 | tf_op jit(solution)/shard_map/ppermute | solution.py:409
  31.7 1.1 %collective-permute-done.9 = f32[16,16]{1,0:T(8,128)S(1)} collective-permute-done((f32[16,16]{1,0:T(8,128)S(1)}, f32[16,16]{1,0:T(8,128)S(1)}, u32[]{:S(2)}, u32[]{:S(2)}) %collective-permute-start.9) | collective-permute-done | bytes 1056 | tf_op jit(solution)/shard_map/ppermute | solution.py:409
  32.7 2.3 %collective-permute-start.10 = (f32[16,16]{1,0:T(8,128)S(1)}, f32[16,16]{1,0:T(8,128)S(1)}, u32[]{:S(2)}, u32[]{:S(2)}) collective-permute-start(f32[16,16]{1,0:T(8,128)S(1)} %fusion), channel_id=1, source_target_pairs={{0,1},{1,0},{2,3},{3,2},{4,5},{5,4},{6,7},{7,6},{8,9},{9,8},{10,11... | collective-permute-start | bytes 3080 | tf_op jit(solution)/shard_map/ppermute | solution.py:271
  35.0 0.8 %collective-permute-done.10 = f32[16,16]{1,0:T(8,128)S(1)} collective-permute-done((f32[16,16]{1,0:T(8,128)S(1)}, f32[16,16]{1,0:T(8,128)S(1)}, u32[]{:S(2)}, u32[]{:S(2)}) %collective-permute-start.10) | collective-permute-done | bytes 1056 | tf_op jit(solution)/shard_map/ppermute | solution.py:271
  35.9 0.6 %add.15 = f32[16,16]{1,0:T(8,128)} add(f32[16,16]{1,0:T(8,128)S(1)} %fusion, f32[16,16]{1,0:T(8,128)S(1)} %collective-permute-done.10) | non-fusion elementwise | flops 256 | bytes 3072 | tf_op jit(solution)/shard_map/add | solution.py:416
  (8 shorter events, 0.1 us)
Async XLA Ops:
  0.0 0.8 %copy-start.2 = (bf16[16,16,128]{2,1,0:T(8,128)(2,1)S(1)}, bf16[16,16,128]{2,1,0:T(8,128)(2,1)}, u32[]{:S(2)}) copy-start(bf16[16,16,128]{2,1,0:T(8,128)(2,1)} %query_ref.1) | copy-start | bytes 196612
  0.0 0.8 %copy-start.5 = (s32[16,16]{1,0:T(8,128)S(1)}, s32[16,16]{1,0:T(8,128)}, u32[]{:S(2)}) copy-start(s32[16,16]{1,0:T(8,128)} %cand_ref.1) | copy-start | bytes 3076
  0.8 4.3 %copy-start = (bf16[4096,128]{1,0:T(8,128)(2,1)S(1)}, bf16[4096,128]{1,0:T(8,128)(2,1)}, u32[]{:S(2)}) copy-start(bf16[4096,128]{1,0:T(8,128)(2,1)} %refs_4_.1) | copy-start | bytes 3145732
  0.8 4.3 %copy-start.1 = (s32[64,128,16]{1,2,0:T(8,128)S(1)}, s32[64,128,16]{1,2,0:T(8,128)}, u32[]{:S(2)}) copy-start(s32[64,128,16]{1,2,0:T(8,128)} %param.10) | copy-start | bytes 1572868
  0.8 4.3 %copy-start.3 = (s32[64,128]{1,0:T(8,128)S(1)}, s32[64,128]{1,0:T(8,128)}, u32[]{:S(2)}) copy-start(s32[64,128]{1,0:T(8,128)} %refs_0_.5) | copy-start | bytes 98308
  0.9 4.3 %copy-start.4 = (bf16[64,128]{1,0:T(8,128)(2,1)S(1)}, bf16[64,128]{1,0:T(8,128)(2,1)}, u32[]{:S(2)}) copy-start(bf16[64,128]{1,0:T(8,128)(2,1)} %refs_2_.5) | copy-start | bytes 49156
  0.9 4.3 %copy-start.6 = (bf16[4]{0:T(256)(128)(2,1)S(1)}, bf16[4]{0:T(256)(128)(2,1)}, u32[]{:S(2)}) copy-start(bf16[4]{0:T(256)(128)(2,1)} %param.15) | copy-start | bytes 28
  1.0 7.9 %collective-permute-start = (bf16[1,272,128]{2,1,0:T(8,128)(2,1)S(1)}, bf16[1,272,128]{2,1,0:T(8,128)(2,1)S(1)}, u32[]{:S(2)}, u32[]{:S(2)}) collective-permute-start(bf16[1,272,128]{2,1,0:T(8,128)(2,1)S(1)} %bitcast.4), channel_id=1, source_target_pairs={{0,8},{2,10},{4,12},{6,14},{8,0},{10,2},{12,4},{14,6},{1,9},{3,11}... | collective-permute-start | bytes 208904 | tf_op jit(solution)/shard_map/ppermute | solution.py:268
  8.9 5.1 %collective-permute-start.2 = (bf16[2,272,128]{2,1,0:T(8,128)(2,1)S(1)}, bf16[2,272,128]{2,1,0:T(8,128)(2,1)S(1)}, u32[]{:S(2)}, u32[]{:S(2)}) collective-permute-start(bf16[2,272,128]{2,1,0:T(8,128)(2,1)S(1)} %pad_maximum_fusion.1), channel_id=1, source_target_pairs={{0,4},{2,6},{4,0},{6,2},{8,12},{10,14},{12,8},{14,10},{1,5},{3,7},... | collective-permute-start | bytes 417800 | tf_op jit(solution)/shard_map/ppermute | solution.py:268
  10.0 9.0 %collective-permute-start.1 = (bf16[2,272,128]{2,1,0:T(8,128)(2,1)S(1)}, bf16[2,272,128]{2,1,0:T(8,128)(2,1)S(1)}, u32[]{:S(2)}, u32[]{:S(2)}) collective-permute-start(bf16[2,272,128]{2,1,0:T(8,128)(2,1)S(1)} %pad_maximum_fusion.1), channel_id=1, source_target_pairs={{0,2},{2,0},{4,6},{6,4},{8,10},{10,8},{12,14},{14,12},{1,3},{3,1},... | collective-permute-start | bytes 417800 | tf_op jit(solution)/shard_map/ppermute | solution.py:268
  14.1 5.1 %collective-permute-start.3 = (bf16[2,272,128]{2,1,0:T(8,128)(2,1)S(1)}, bf16[2,272,128]{2,1,0:T(8,128)(2,1)S(1)}, u32[]{:S(2)}, u32[]{:S(2)}) collective-permute-start(bf16[2,272,128]{2,1,0:T(8,128)(2,1)S(1)} %collective-permute-done.2), channel_id=1, source_target_pairs={{0,2},{2,0},{4,6},{6,4},{8,10},{10,8},{12,14},{14,12},{1,3},{3,1},... | collective-permute-start | bytes 417800 | tf_op jit(solution)/shard_map/ppermute | solution.py:268
  19.1 1.6 %copy-start.7 = (s32[64]{0:T(128)S(1)}, s32[64]{0:T(128)}, u32[]{:S(2)}) copy-start(s32[64]{0:T(128)} %len_hbm.3) | copy-start | bytes 772
  19.1 1.6 %collective-permute-start.4 = (bf16[4,272,128]{2,1,0:T(8,128)(2,1)S(1)}, bf16[4,272,128]{2,1,0:T(8,128)(2,1)S(1)}, u32[]{:S(2)}, u32[]{:S(2)}) collective-permute-start(bf16[4,272,128]{2,1,0:T(8,128)(2,1)S(1)} %constant_dynamic-update-slice_fusion.rows_ref.mine_ref), channel_id=1, source_target_pairs={{0,1},{1,0},{2,3},{3,2},{4,5},{5,4},{6,7},{7,6},{8,9},{9,8},{10,11... | collective-permute-start | bytes 835592 | tf_op jit(solution)/shard_map/ppermute | solution.py:271
  19.3 5.5 %collective-permute-start.5 = (bf16[4,272,128]{2,1,0:T(8,128)(2,1)S(1)}, bf16[4,272,128]{2,1,0:T(8,128)(2,1)S(1)}, u32[]{:S(2)}, u32[]{:S(2)}) collective-permute-start(bf16[4,272,128]{2,1,0:T(8,128)(2,1)S(1)} %pad_maximum_fusion.refs_0_.mine_ref), channel_id=1, source_target_pairs={{0,1},{1,0},{2,3},{3,2},{4,5},{5,4},{6,7},{7,6},{8,9},{9,8},{10,11... | collective-permute-start | bytes 835592 | tf_op jit(solution)/shard_map/ppermute | solution.py:271
  23.0 3.7 %collective-permute-start.6 = (f32[16,64]{1,0:T(8,128)S(1)}, f32[16,64]{1,0:T(8,128)S(1)}, u32[]{:S(2)}, u32[]{:S(2)}) collective-permute-start(f32[16,64]{1,0:T(8,128)S(1)} %bitcast.10), channel_id=1, source_target_pairs={{0,2},{2,0},{4,6},{6,4},{8,10},{10,8},{12,14},{14,12},{1,3},{3,1},... | collective-permute-start | bytes 12296 | tf_op jit(solution)/shard_map/ppermute | solution.py:268
  26.7 1.2 %collective-permute-start.7 = (f32[16,64]{1,0:T(8,128)S(1)}, f32[16,64]{1,0:T(8,128)S(1)}, u32[]{:S(2)}, u32[]{:S(2)}) collective-permute-start(f32[16,64]{1,0:T(8,128)S(1)} %slice_add_fusion), channel_id=1, source_target_pairs={{0,1},{1,0},{2,3},{3,2},{4,5},{5,4},{6,7},{7,6},{8,9},{9,8},{10,11... | collective-permute-start | bytes 12296 | tf_op jit(solution)/shard_map/ppermute | solution.py:271
  28.0 3.7 %collective-permute-start.8 = (f32[16,16]{1,0:T(8,128)S(1)}, f32[16,16]{1,0:T(8,128)S(1)}, u32[]{:S(2)}, u32[]{:S(2)}) collective-permute-start(f32[16,16]{1,0:T(8,128)S(1)} %get-tuple-element.32), channel_id=1, source_target_pairs={{0,4},{1,9},{2,6},{3,11},{4,0},{5,13},{6,2},{7,15},{8,12},{9,1},{1... | collective-permute-start | bytes 3080 | tf_op jit(solution)/shard_map/ppermute | solution.py:409
  29.1 3.7 %collective-permute-start.9 = (f32[16,16]{1,0:T(8,128)S(1)}, f32[16,16]{1,0:T(8,128)S(1)}, u32[]{:S(2)}, u32[]{:S(2)}) collective-permute-start(f32[16,16]{1,0:T(8,128)S(1)} %get-tuple-element.31), channel_id=1, source_target_pairs={{0,2},{1,13},{2,0},{3,15},{4,6},{5,9},{6,4},{7,11},{8,10},{9,5},{1... | collective-permute-start | bytes 3080 | tf_op jit(solution)/shard_map/ppermute | solution.py:409
  32.7 3.1 %collective-permute-start.10 = (f32[16,16]{1,0:T(8,128)S(1)}, f32[16,16]{1,0:T(8,128)S(1)}, u32[]{:S(2)}, u32[]{:S(2)}) collective-permute-start(f32[16,16]{1,0:T(8,128)S(1)} %fusion), channel_id=1, source_target_pairs={{0,1},{1,0},{2,3},{3,2},{4,5},{5,4},{6,7},{7,6},{8,9},{9,8},{10,11... | collective-permute-start | bytes 3080 | tf_op jit(solution)/shard_map/ppermute | solution.py:271

commit v9 on v8

--- a/solution.py
+++ b/solution.py
@@ -410,8 +410,8 @@
 
     total = total + swap_sub(total)
     mine, to_far, to_near, to_both = (total[:, i * picks : (i + 1) * picks] for i in range(4))
-    one = swap_apart(jnp.where(core == 1, to_far, to_near), near_d, far_d)
-    two = swap_apart(to_both, 1, far_d ^ near_d)
+    one = swap_apart(jnp.where(core == 1, to_both, to_near), near_d, far_d ^ near_d)
+    two = swap_apart(to_far, 1, far_d)
     part = one + jnp.where(core == 1, two, mine)
     return part + swap_sub(part)
 

time: 36.6 us -> 36.5 us (level)
  no operation moved by 1% of the time
where the time goes in v9:
time: 36.5 us; the launch traced here: 36.3 us
  starting transfers between devices  15.7 us (43%)
  Pallas kernels  13.9 us (38%)
  waiting for transfers between devices  4.93 us (14%)
  local copies, waits for them, and re-layouts  0.89 us (2%)
  other arithmetic  0.73 us (2%)
    ppermute x5, starting transfers between devices, swap_shard(): return lax.ppermute(x, 'shard', [(i, i ^ d) for i in range(shards)])  10.3 us
    pallas_call x3, Pallas kernels, decode(): pl.pallas_call(functools.partial(decode_kernel, first, start, stop), out_...  8.77 us
    pallas_call x2, Pallas kernels, score(): pl.pallas_call(functools.partial(pair_kernel, query_count, picks, capacit...  4.09 us
    ppermute x4, starting transfers between devices, swap_sub(): return lax.ppermute(x, 'sub', [(i, i ^ 1) for i in range(halves)])  2.86 us
    ppermute x2, starting transfers between devices, swap_apart(): return lax.ppermute(x, ('shard', 'sub'), pairs)  2.58 us
    ppermute x2, waiting for transfers between devices, swap_apart(): return lax.ppermute(x, ('shard', 'sub'), pairs)  2.13 us
    ppermute x4, waiting for transfers between devices, swap_sub(): return lax.ppermute(x, 'sub', [(i, i ^ 1) for i in range(halves)])  2.05 us
    pallas_call x1, Pallas kernels, find(): pl.pallas_call(functools.partial(slot_kernel, query_count, picks, capacit...  0.88 us
  transfers between devices with their start and end apart: 11, of which 8 were waited for; matrix products, arithmetic and copies ran while one was open for 0% of the time, Pallas kernels for 38%

profile of v9, /device:TPU:0, one launch (start us, length us, event | category | flops | bytes accessed | tf_op | source)
XLA Modules:
  0.0 36.3 jit_solution(10221831379955214661)
XLA Ops:
  0.0 0.0 copy-start.2
  0.0 0.0 copy-start.5
  0.0 0.8 %copy-done.2 = bf16[16,16,128]{2,1,0:T(8,128)(2,1)S(1)} copy-done((bf16[16,16,128]{2,1,0:T(8,128)(2,1)S(1)}, bf16[16,16,128]{2,1,0:T(8,128)(2,1)}, u32[]{:S(2)}) %copy-start.2) | copy-done | bytes 65560
  0.8 0.0 copy-done.5
  0.8 0.0 copy-start
  0.8 0.0 copy-start.1
  0.8 0.0 copy-start.3
  0.9 0.0 copy-start.4
  0.9 0.0 copy-start.6
  0.9 0.2 pack.1
  1.0 4.1 %collective-permute-start = (bf16[1,272,128]{2,1,0:T(8,128)(2,1)S(1)}, bf16[1,272,128]{2,1,0:T(8,128)(2,1)S(1)}, u32[]{:S(2)}, u32[]{:S(2)}) collective-permute-start(bf16[1,272,128]{2,1,0:T(8,128)(2,1)S(1)} %bitcast.4), channel_id=1, source_target_pairs={{0,8},{2,10},{4,12},{6,14},{8,0},{10,2},{12,4},{14,6},{1,9},{3,11}... | collective-permute-start | bytes 208904 | tf_op jit(solution)/shard_map/ppermute | solution.py:268
  5.1 0.0 copy-done
  5.1 0.0 copy-done.1
  5.1 0.0 copy-done.3
  5.1 0.0 copy-done.4
  5.1 0.0 copy-done.6
  5.2 3.2 %decode.3 = (bf16[64,128,128]{2,1,0:T(8,128)(2,1)S(1)}, f32[4096,128]{1,0:T(8,128)S(1)}) custom-call(s32[64,128]{1,0:T(8,128)S(1)} %copy-done.3, s32[64,16,128]{2,1,0:T(8,128)S(1)} %bitcast.7, bf16[64,128]{1,0:T(8,128)(2,1)S(1)} %copy-done.4, bf16[1,4]{1,0:T(2,128)(2,1)S(1)} %bitcast.11, bf16[4096,128]{1,0:T(8,128)(2,1)S(1)} %copy-done), custom_call_target="tpu_custom_call" | custom-call | flops 4800000000 | tf_op jit(solution)/shard_map/decode/pallas_call | solution.py:312
  8.4 0.5 %collective-permute-done = bf16[1,272,128]{2,1,0:T(8,128)(2,1)S(1)} collective-permute-done((bf16[1,272,128]{2,1,0:T(8,128)(2,1)S(1)}, bf16[1,272,128]{2,1,0:T(8,128)(2,1)S(1)}, u32[]{:S(2)}, u32[]{:S(2)}) %collective-permute-start) | collective-permute-done | bytes 69664 | tf_op jit(solution)/shard_map/ppermute | solution.py:268
  8.9 1.1 %collective-permute-start.2 = (bf16[2,272,128]{2,1,0:T(8,128)(2,1)S(1)}, bf16[2,272,128]{2,1,0:T(8,128)(2,1)S(1)}, u32[]{:S(2)}, u32[]{:S(2)}) collective-permute-start(bf16[2,272,128]{2,1,0:T(8,128)(2,1)S(1)} %pad_maximum_fusion.1), channel_id=1, source_target_pairs={{0,4},{2,6},{4,0},{6,2},{8,12},{10,14},{12,8},{14,10},{1,5},{3,7},... | collective-permute-start | bytes 417800 | tf_op jit(solution)/shard_map/ppermute | solution.py:268
  10.1 1.5 %collective-permute-start.1 = (bf16[2,272,128]{2,1,0:T(8,128)(2,1)S(1)}, bf16[2,272,128]{2,1,0:T(8,128)(2,1)S(1)}, u32[]{:S(2)}, u32[]{:S(2)}) collective-permute-start(bf16[2,272,128]{2,1,0:T(8,128)(2,1)S(1)} %pad_maximum_fusion.1), channel_id=1, source_target_pairs={{0,2},{2,0},{4,6},{6,4},{8,10},{10,8},{12,14},{14,12},{1,3},{3,1},... | collective-permute-start | bytes 417800 | tf_op jit(solution)/shard_map/ppermute | solution.py:268
  11.6 2.3 %decode.4.refs_5_ = bf16[64,128,128]{2,1,0:T(8,128)(2,1)S(1)} custom-call(s32[64,128]{1,0:T(8,128)S(1)} %copy-done.3, s32[64,16,128]{2,1,0:T(8,128)S(1)} %bitcast.8, bf16[64,128]{1,0:T(8,128)(2,1)S(1)} %copy-done.4, bf16[1,4]{1,0:T(2,128)(2,1)S(1)} %bitcast.12, f32[4096,128]{1,0:T(8,128)S(1)} %get-tuple-element.20.refs_4_, ...), custom_call_target="tpu_custom_call", output_to_operand_aliasing={{}: (5, {})} | custom-call | flops 3200000000 | tf_op jit(solution)/shard_map/decode/pallas_call | solution.py:312
  13.9 0.1 collective-permute-done.2
  14.1 1.7 %collective-permute-start.3 = (bf16[2,272,128]{2,1,0:T(8,128)(2,1)S(1)}, bf16[2,272,128]{2,1,0:T(8,128)(2,1)S(1)}, u32[]{:S(2)}, u32[]{:S(2)}) collective-permute-start(bf16[2,272,128]{2,1,0:T(8,128)(2,1)S(1)} %collective-permute-done.2), channel_id=1, source_target_pairs={{0,2},{2,0},{4,6},{6,4},{8,10},{10,8},{12,14},{14,12},{1,3},{3,1},... | collective-permute-start | bytes 417800 | tf_op jit(solution)/shard_map/ppermute | solution.py:268
  15.8 3.2 %decode.5.emb_ref = bf16[64,128,128]{2,1,0:T(8,128)(2,1)S(1)} custom-call(s32[64,128]{1,0:T(8,128)S(1)} %copy-done.3, s32[64,16,128]{2,1,0:T(8,128)S(1)} %bitcast.9, bf16[64,128]{1,0:T(8,128)(2,1)S(1)} %copy-done.4, bf16[1,4]{1,0:T(2,128)(2,1)S(1)} %bitcast.13, f32[4096,128]{1,0:T(8,128)S(1)} %get-tuple-element.20.refs_4_, ...), custom_call_target="tpu_custom_call", output_to_operand_aliasing={{}: (5, {})} | custom-call | flops 4800000000 | tf_op jit(solution)/shard_map/decode/pallas_call | solution.py:312
  19.0 0.0 collective-permute-done.1
  19.0 0.1 collective-permute-done.3
  19.1 0.0 copy-start.7
  19.1 0.1 collective-permute-start.4
  19.3 0.6 %collective-permute-start.5 = (bf16[4,272,128]{2,1,0:T(8,128)(2,1)S(1)}, bf16[4,272,128]{2,1,0:T(8,128)(2,1)S(1)}, u32[]{:S(2)}, u32[]{:S(2)}) collective-permute-start(bf16[4,272,128]{2,1,0:T(8,128)(2,1)S(1)} %pad_maximum_fusion.refs_0_.mine_ref), channel_id=1, source_target_pairs={{0,1},{1,0},{2,3},{3,2},{4,5},{5,4},{6,7},{7,6},{8,9},{9,8},{10,11... | collective-permute-start | bytes 835592 | tf_op jit(solution)/shard_map/ppermute | solution.py:271
  19.8 0.9 %slots.1 = (s32[16,128]{1,0:T(8,128)S(1)}, s32[64,128]{1,0:T(8,128)S(1)}) custom-call(bf16[4,272,128]{2,1,0:T(8,128)(2,1)S(1)} %constant_dynamic-update-slice_fusion.rows_ref.mine_ref), custom_call_target="tpu_custom_call" | custom-call | flops 1000000000 | tf_op jit(solution)/shard_map/slots/pallas_call | solution.py:333
  20.7 0.1 collective-permute-done.4.other_ref
  20.8 0.0 copy-done.7
  20.8 2.2 %pairs.2 = (f32[16,128]{1,0:T(8,128)S(1)}, s32[16,128]{1,0:T(8,128)S(1)}, s32[64,128]{1,0:T(8,128)S(1)}) custom-call(s32[64]{0:T(128)S(1)} %copy-done.7, s32[16,128]{1,0:T(8,128)S(1)} %get-tuple-element.25.slot_ref, s32[64,128]{1,0:T(8,128)S(1)} %get-tuple-element.26.rank_ref, bf16[4,272,128]{2,1,0:T(8,128)(2,1)S(1)} %constant_dynamic-update-slice_fusion.rows_ref.mine_ref, ...), custom_call_target="tpu_custom_call" | custom-call | flops 3000000000 | tf_op jit(solution)/shard_map/pairs/pallas_call | solution.py:352
  23.0 1.8 %collective-permute-start.6 = (f32[16,64]{1,0:T(8,128)S(1)}, f32[16,64]{1,0:T(8,128)S(1)}, u32[]{:S(2)}, u32[]{:S(2)}) collective-permute-start(f32[16,64]{1,0:T(8,128)S(1)} %bitcast.10), channel_id=1, source_target_pairs={{0,2},{2,0},{4,6},{6,4},{8,10},{10,8},{12,14},{14,12},{1,3},{3,1},... | collective-permute-start | bytes 12296 | tf_op jit(solution)/shard_map/ppermute | solution.py:268
  24.8 0.0 collective-permute-done.5.other_ref
  24.8 1.9 %pairs.3 = f32[16,128]{1,0:T(8,128)S(1)} custom-call(s32[64]{0:T(128)S(1)} %copy-done.7, s32[16,128]{1,0:T(8,128)S(1)} %get-tuple-element.28.slot_ref, s32[64,128]{1,0:T(8,128)S(1)} %get-tuple-element.29.rank_ref, bf16[4,272,128]{2,1,0:T(8,128)(2,1)S(1)} %pad_maximum_fusion.refs_0_.mine_ref, bf16[4,272,128]{2,1,0:T(8,128)(2,1)S(1)} %collective-permute-done.5.other_ref, ...), custom_call_target="tpu_custom_call" | custom-call | flops 3000000000 | tf_op jit(solution)/shard_map/pairs/pallas_call | solution.py:352
  26.7 0.0 collective-permute-done.6
  26.7 0.1 collective-permute-start.7
  26.8 1.2 %collective-permute-done.7 = f32[16,64]{1,0:T(8,128)S(1)} collective-permute-done((f32[16,64]{1,0:T(8,128)S(1)}, f32[16,64]{1,0:T(8,128)S(1)}, u32[]{:S(2)}, u32[]{:S(2)}) %collective-permute-start.7) | collective-permute-done | bytes 4128 | tf_op jit(solution)/shard_map/ppermute | solution.py:271
  27.9 0.1 fusion.1
  28.0 1.1 %collective-permute-start.8 = (f32[16,16]{1,0:T(8,128)S(1)}, f32[16,16]{1,0:T(8,128)S(1)}, u32[]{:S(2)}, u32[]{:S(2)}) collective-permute-start(f32[16,16]{1,0:T(8,128)S(1)} %get-tuple-element.32), channel_id=1, source_target_pairs={{0,4},{1,13},{2,6},{3,15},{4,0},{5,9},{6,2},{7,11},{8,12},{9,5},{1... | collective-permute-start | bytes 3080 | tf_op jit(solution)/shard_map/ppermute | solution.py:409
  29.1 1.5 %collective-permute-start.9 = (f32[16,16]{1,0:T(8,128)S(1)}, f32[16,16]{1,0:T(8,128)S(1)}, u32[]{:S(2)}, u32[]{:S(2)}) collective-permute-start(f32[16,16]{1,0:T(8,128)S(1)} %get-tuple-element.31), channel_id=1, source_target_pairs={{0,2},{1,9},{2,0},{3,11},{4,6},{5,13},{6,4},{7,15},{8,10},{9,1},{1... | collective-permute-start | bytes 3080 | tf_op jit(solution)/shard_map/ppermute | solution.py:409
  30.6 1.1 %collective-permute-done.8 = f32[16,16]{1,0:T(8,128)S(1)} collective-permute-done((f32[16,16]{1,0:T(8,128)S(1)}, f32[16,16]{1,0:T(8,128)S(1)}, u32[]{:S(2)}, u32[]{:S(2)}) %collective-permute-start.8) | collective-permute-done | bytes 1056 | tf_op jit(solution)/shard_map/ppermute | solution.py:409
  31.7 1.1 %collective-permute-done.9 = f32[16,16]{1,0:T(8,128)S(1)} collective-permute-done((f32[16,16]{1,0:T(8,128)S(1)}, f32[16,16]{1,0:T(8,128)S(1)}, u32[]{:S(2)}, u32[]{:S(2)}) %collective-permute-start.9) | collective-permute-done | bytes 1056 | tf_op jit(solution)/shard_map/ppermute | solution.py:409
  32.7 2.2 %collective-permute-start.10 = (f32[16,16]{1,0:T(8,128)S(1)}, f32[16,16]{1,0:T(8,128)S(1)}, u32[]{:S(2)}, u32[]{:S(2)}) collective-permute-start(f32[16,16]{1,0:T(8,128)S(1)} %fusion), channel_id=1, source_target_pairs={{0,1},{1,0},{2,3},{3,2},{4,5},{5,4},{6,7},{7,6},{8,9},{9,8},{10,11... | collective-permute-start | bytes 3080 | tf_op jit(solution)/shard_map/ppermute | solution.py:271
  34.9 0.8 %collective-permute-done.10 = f32[16,16]{1,0:T(8,128)S(1)} collective-permute-done((f32[16,16]{1,0:T(8,128)S(1)}, f32[16,16]{1,0:T(8,128)S(1)}, u32[]{:S(2)}, u32[]{:S(2)}) %collective-permute-start.10) | collective-permute-done | bytes 1056 | tf_op jit(solution)/shard_map/ppermute | solution.py:271
  35.7 0.6 %add.15 = f32[16,16]{1,0:T(8,128)} add(f32[16,16]{1,0:T(8,128)S(1)} %fusion, f32[16,16]{1,0:T(8,128)S(1)} %collective-permute-done.10) | non-fusion elementwise | flops 256 | bytes 3072 | tf_op jit(solution)/shard_map/add | solution.py:416
  (8 shorter events, 0.1 us)
Async XLA Ops:
  0.0 0.8 %copy-start.2 = (bf16[16,16,128]{2,1,0:T(8,128)(2,1)S(1)}, bf16[16,16,128]{2,1,0:T(8,128)(2,1)}, u32[]{:S(2)}) copy-start(bf16[16,16,128]{2,1,0:T(8,128)(2,1)} %query_ref.1) | copy-start | bytes 196612
  0.0 0.8 %copy-start.5 = (s32[16,16]{1,0:T(8,128)S(1)}, s32[16,16]{1,0:T(8,128)}, u32[]{:S(2)}) copy-start(s32[16,16]{1,0:T(8,128)} %cand_ref.1) | copy-start | bytes 3076
  0.8 4.3 %copy-start = (bf16[4096,128]{1,0:T(8,128)(2,1)S(1)}, bf16[4096,128]{1,0:T(8,128)(2,1)}, u32[]{:S(2)}) copy-start(bf16[4096,128]{1,0:T(8,128)(2,1)} %refs_4_.1) | copy-start | bytes 3145732
  0.8 4.3 %copy-start.1 = (s32[64,128,16]{1,2,0:T(8,128)S(1)}, s32[64,128,16]{1,2,0:T(8,128)}, u32[]{:S(2)}) copy-start(s32[64,128,16]{1,2,0:T(8,128)} %param.10) | copy-start | bytes 1572868
  0.8 4.3 %copy-start.3 = (s32[64,128]{1,0:T(8,128)S(1)}, s32[64,128]{1,0:T(8,128)}, u32[]{:S(2)}) copy-start(s32[64,128]{1,0:T(8,128)} %refs_0_.5) | copy-start | bytes 98308
  0.9 4.3 %copy-start.4 = (bf16[64,128]{1,0:T(8,128)(2,1)S(1)}, bf16[64,128]{1,0:T(8,128)(2,1)}, u32[]{:S(2)}) copy-start(bf16[64,128]{1,0:T(8,128)(2,1)} %refs_2_.5) | copy-start | bytes 49156
  0.9 4.3 %copy-start.6 = (bf16[4]{0:T(256)(128)(2,1)S(1)}, bf16[4]{0:T(256)(128)(2,1)}, u32[]{:S(2)}) copy-start(bf16[4]{0:T(256)(128)(2,1)} %param.15) | copy-start | bytes 28
  1.0 7.9 %collective-permute-start = (bf16[1,272,128]{2,1,0:T(8,128)(2,1)S(1)}, bf16[1,272,128]{2,1,0:T(8,128)(2,1)S(1)}, u32[]{:S(2)}, u32[]{:S(2)}) collective-permute-start(bf16[1,272,128]{2,1,0:T(8,128)(2,1)S(1)} %bitcast.4), channel_id=1, source_target_pairs={{0,8},{2,10},{4,12},{6,14},{8,0},{10,2},{12,4},{14,6},{1,9},{3,11}... | collective-permute-start | bytes 208904 | tf_op jit(solution)/shard_map/ppermute | solution.py:268
  8.9 5.1 %collective-permute-start.2 = (bf16[2,272,128]{2,1,0:T(8,128)(2,1)S(1)}, bf16[2,272,128]{2,1,0:T(8,128)(2,1)S(1)}, u32[]{:S(2)}, u32[]{:S(2)}) collective-permute-start(bf16[2,272,128]{2,1,0:T(8,128)(2,1)S(1)} %pad_maximum_fusion.1), channel_id=1, source_target_pairs={{0,4},{2,6},{4,0},{6,2},{8,12},{10,14},{12,8},{14,10},{1,5},{3,7},... | collective-permute-start | bytes 417800 | tf_op jit(solution)/shard_map/ppermute | solution.py:268
  10.1 8.9 %collective-permute-start.1 = (bf16[2,272,128]{2,1,0:T(8,128)(2,1)S(1)}, bf16[2,272,128]{2,1,0:T(8,128)(2,1)S(1)}, u32[]{:S(2)}, u32[]{:S(2)}) collective-permute-start(bf16[2,272,128]{2,1,0:T(8,128)(2,1)S(1)} %pad_maximum_fusion.1), channel_id=1, source_target_pairs={{0,2},{2,0},{4,6},{6,4},{8,10},{10,8},{12,14},{14,12},{1,3},{3,1},... | collective-permute-start | bytes 417800 | tf_op jit(solution)/shard_map/ppermute | solution.py:268
  14.1 5.1 %collective-permute-start.3 = (bf16[2,272,128]{2,1,0:T(8,128)(2,1)S(1)}, bf16[2,272,128]{2,1,0:T(8,128)(2,1)S(1)}, u32[]{:S(2)}, u32[]{:S(2)}) collective-permute-start(bf16[2,272,128]{2,1,0:T(8,128)(2,1)S(1)} %collective-permute-done.2), channel_id=1, source_target_pairs={{0,2},{2,0},{4,6},{6,4},{8,10},{10,8},{12,14},{14,12},{1,3},{3,1},... | collective-permute-start | bytes 417800 | tf_op jit(solution)/shard_map/ppermute | solution.py:268
  19.1 1.6 %copy-start.7 = (s32[64]{0:T(128)S(1)}, s32[64]{0:T(128)}, u32[]{:S(2)}) copy-start(s32[64]{0:T(128)} %len_hbm.3) | copy-start | bytes 772
  19.1 1.6 %collective-permute-start.4 = (bf16[4,272,128]{2,1,0:T(8,128)(2,1)S(1)}, bf16[4,272,128]{2,1,0:T(8,128)(2,1)S(1)}, u32[]{:S(2)}, u32[]{:S(2)}) collective-permute-start(bf16[4,272,128]{2,1,0:T(8,128)(2,1)S(1)} %constant_dynamic-update-slice_fusion.rows_ref.mine_ref), channel_id=1, source_target_pairs={{0,1},{1,0},{2,3},{3,2},{4,5},{5,4},{6,7},{7,6},{8,9},{9,8},{10,11... | collective-permute-start | bytes 835592 | tf_op jit(solution)/shard_map/ppermute | solution.py:271
  19.3 5.5 %collective-permute-start.5 = (bf16[4,272,128]{2,1,0:T(8,128)(2,1)S(1)}, bf16[4,272,128]{2,1,0:T(8,128)(2,1)S(1)}, u32[]{:S(2)}, u32[]{:S(2)}) collective-permute-start(bf16[4,272,128]{2,1,0:T(8,128)(2,1)S(1)} %pad_maximum_fusion.refs_0_.mine_ref), channel_id=1, source_target_pairs={{0,1},{1,0},{2,3},{3,2},{4,5},{5,4},{6,7},{7,6},{8,9},{9,8},{10,11... | collective-permute-start | bytes 835592 | tf_op jit(solution)/shard_map/ppermute | solution.py:271
  23.0 3.7 %collective-permute-start.6 = (f32[16,64]{1,0:T(8,128)S(1)}, f32[16,64]{1,0:T(8,128)S(1)}, u32[]{:S(2)}, u32[]{:S(2)}) collective-permute-start(f32[16,64]{1,0:T(8,128)S(1)} %bitcast.10), channel_id=1, source_target_pairs={{0,2},{2,0},{4,6},{6,4},{8,10},{10,8},{12,14},{14,12},{1,3},{3,1},... | collective-permute-start | bytes 12296 | tf_op jit(solution)/shard_map/ppermute | solution.py:268
  26.7 1.2 %collective-permute-start.7 = (f32[16,64]{1,0:T(8,128)S(1)}, f32[16,64]{1,0:T(8,128)S(1)}, u32[]{:S(2)}, u32[]{:S(2)}) collective-permute-start(f32[16,64]{1,0:T(8,128)S(1)} %slice_add_fusion), channel_id=1, source_target_pairs={{0,1},{1,0},{2,3},{3,2},{4,5},{5,4},{6,7},{7,6},{8,9},{9,8},{10,11... | collective-permute-start | bytes 12296 | tf_op jit(solution)/shard_map/ppermute | solution.py:271
  28.0 3.7 %collective-permute-start.8 = (f32[16,16]{1,0:T(8,128)S(1)}, f32[16,16]{1,0:T(8,128)S(1)}, u32[]{:S(2)}, u32[]{:S(2)}) collective-permute-start(f32[16,16]{1,0:T(8,128)S(1)} %get-tuple-element.32), channel_id=1, source_target_pairs={{0,4},{1,13},{2,6},{3,15},{4,0},{5,9},{6,2},{7,11},{8,12},{9,5},{1... | collective-permute-start | bytes 3080 | tf_op jit(solution)/shard_map/ppermute | solution.py:409
  29.1 3.7 %collective-permute-start.9 = (f32[16,16]{1,0:T(8,128)S(1)}, f32[16,16]{1,0:T(8,128)S(1)}, u32[]{:S(2)}, u32[]{:S(2)}) collective-permute-start(f32[16,16]{1,0:T(8,128)S(1)} %get-tuple-element.31), channel_id=1, source_target_pairs={{0,2},{1,9},{2,0},{3,11},{4,6},{5,13},{6,4},{7,15},{8,10},{9,1},{1... | collective-permute-start | bytes 3080 | tf_op jit(solution)/shard_map/ppermute | solution.py:409
  32.7 3.0 %collective-permute-start.10 = (f32[16,16]{1,0:T(8,128)S(1)}, f32[16,16]{1,0:T(8,128)S(1)}, u32[]{:S(2)}, u32[]{:S(2)}) collective-permute-start(f32[16,16]{1,0:T(8,128)S(1)} %fusion), channel_id=1, source_target_pairs={{0,1},{1,0},{2,3},{3,2},{4,5},{5,4},{6,7},{7,6},{8,9},{9,8},{10,11... | collective-permute-start | bytes 3080 | tf_op jit(solution)/shard_map/ppermute | solution.py:271
